TPU v7x, 128 devices: a whole 4x4x4 slice. The times are simulated.
128 devices in a mesh: slab: 16 (over y, z), img: 8 (over x, core).
Axes of the slice: x: 4, y: 4, z: 4, core: 2. Of those that a mesh axis runs over, the one named last changes fastest.
Arguments:
- images: bfloat16 [16384, 16384], P('img', 'slab'), may hold values from -6 to 6
- volume: bfloat16 [32, 512, 1024], P('slab'), may hold values from -2 to 2
- precision: float32 [16384], P('img'), may hold values from 0.03 to 1
- candidates: int32 [16384, 16], P('img'), may hold values from 0 to 511, all different within a row
- slot_key: int32 [16, 16, 64], replicated, may hold values from -1 to 511, as said below
- slot_voxel: int32 [16, 16, 64], replicated, may hold values from 0 to 1022, as said below
- slot_weight: int32 [16, 16, 64], replicated, may hold values from 0 to 16
Outputs:
- density: float32 [32, 512, 512], P('slab', None, 'img')
- posterior: float32 [16384, 16], P('img')
Inputs may be any that keep to these rules, and one draw needn't show every extreme that they name: slot_key[s, d, :] holds keys p + j (pose p, row j of block d) taken from slab s, live slots first and -1 after; every key of every block d stands exactly once over all s; each (s, d) has at most 64 live slots, and every block has a slab with exactly 64. `slot_voxel`: z * 512 + y with z below 2 and y below 511.
All inputs are finite; a program needn't handle non-finite values.
Results may differ from a plain program's by a relative error of at most 0.0096.
Values may be sent and summed in bfloat16 or wider, within the bound.
A program may use at most 64 MiB of HBM per device.

v0:
```python
import math

import jax
import jax.numpy as jnp
from jax import lax
from jax.sharding import PartitionSpec as P

NPOSE = 512
WSTEPS = 16


ridge = 0.25


def gridding(samples, first, total):
    offset = (
        jnp.asarray(first).astype(jnp.float32) + jnp.arange(samples, dtype=jnp.float32) - total / 2
    ) / total
    return 1.0 / jnp.sinc(offset) ** 2


def dft_tables(length):
    counter = jnp.arange(length, dtype=jnp.int32)
    phases = counter[:, None] * counter[None, :] % length
    angles = phases.astype(jnp.float32) * (2.0 * math.pi / length)
    return (jnp.cos(angles), jnp.sin(angles))


def interpolate(vol_rows, slot_keys, voxels, weights):
    fraction = (weights.astype(jnp.float32) / WSTEPS)[..., None]
    below_row = jnp.take(vol_rows, voxels, axis=0).astype(jnp.float32)
    above_row = jnp.take(vol_rows, voxels + 1, axis=0).astype(jnp.float32)
    values = fraction * below_row + (1.0 - fraction) * above_row
    return jnp.where((slot_keys >= 0)[..., None], values, 0.0).astype(jnp.bfloat16)


def posterior_of(score_rows, precision, candidates):
    picked = jnp.take_along_axis(score_rows, candidates, axis=1) * precision[:, None]
    largest = jnp.max(picked, axis=1, keepdims=True)
    exponent = jnp.exp(picked - largest)
    return exponent / jnp.sum(exponent, axis=1, keepdims=True)


def spread_weights(posterior, precision, candidates, poses):
    amounts = posterior * precision[:, None]
    columns = lax.broadcasted_iota(jnp.int32, (1, poses), 1)

    def add_one(position, spread_table):
        chosen = lax.dynamic_slice_in_dim(candidates, position, 1, 1)
        amount = lax.dynamic_slice_in_dim(amounts, position, 1, 1)
        return spread_table + jnp.where(chosen == columns, amount, 0.0)

    start_table = jnp.zeros((candidates.shape[0], poses), jnp.float32)
    spread_table = lax.fori_loop(0, candidates.shape[1], add_one, start_table)
    return spread_table.astype(jnp.bfloat16)


def per_device(images, volume, precision, candidates, slot_key, slot_voxel, slot_weight):
    img_count = lax.axis_size("img")
    own_slab = lax.axis_index("slab")
    img_rows, features = images.shape
    planes, edge_len, row_width = volume.shape
    rows_dev = features // row_width
    vol_rows = volume.reshape(planes * edge_len, row_width)
    out_keys = lax.dynamic_index_in_dim(slot_key, own_slab, 0, keepdims=False)
    out_voxels = lax.dynamic_index_in_dim(slot_voxel, own_slab, 0, keepdims=False)
    out_weights = lax.dynamic_index_in_dim(slot_weight, own_slab, 0, keepdims=False)
    in_keys = lax.dynamic_index_in_dim(slot_key, own_slab, 1, keepdims=False)
    outgoing_rows = interpolate(vol_rows, out_keys, out_voxels, out_weights)
    received = lax.all_to_all(outgoing_rows, "slab", split_axis=0, concat_axis=0, tiled=True)
    live_in = in_keys >= 0
    landing = jnp.where(live_in, in_keys, NPOSE * rows_dev)
    slices = jnp.zeros((NPOSE * rows_dev, row_width), jnp.bfloat16)
    slices = slices.at[landing.reshape(-1)].set(received.reshape(-1, row_width), mode="drop")
    cross = lax.dot_general(
        images, slices, (((1,), (1,)), ((), ())), preferred_element_type=jnp.float32
    )
    power = jnp.sum(jnp.square(slices.astype(jnp.float32)), axis=1)
    partial_score = cross - 0.5 * power[None, :]
    score_all = lax.psum(partial_score, "slab")
    posterior = posterior_of(score_all, precision, candidates)
    spread = spread_weights(posterior, precision, candidates, NPOSE)
    pose_weight = jnp.sum(spread.astype(jnp.float32), axis=0)
    back = lax.dot_general(
        spread, images, (((0,), (0,)), ((), ())), preferred_element_type=jnp.float32
    ).astype(jnp.bfloat16)
    safe_in = jnp.where(live_in, in_keys, 0)
    returning = jnp.where(
        live_in[..., None], jnp.take(back, safe_in, axis=0), jnp.zeros((), jnp.bfloat16)
    )
    returned = lax.all_to_all(returning, "slab", split_axis=0, concat_axis=0, tiled=True)
    use_fraction = (out_weights.astype(jnp.float32) / WSTEPS).reshape(-1)
    contrib = returned.astype(jnp.float32).reshape(-1, row_width)
    use_flat = out_voxels.reshape(-1)
    accumulated = jnp.zeros((planes * edge_len, row_width), jnp.float32)
    accumulated = accumulated.at[use_flat].add(use_fraction[:, None] * contrib)
    accumulated = accumulated.at[use_flat + 1].add((1.0 - use_fraction)[:, None] * contrib)
    live_out = out_keys >= 0
    fraction = (out_weights.astype(jnp.float32) / WSTEPS).reshape(-1)
    voxel_flat = out_voxels.reshape(-1)
    pose_ids = jnp.where(live_out, out_keys // rows_dev, 0)
    slot_mass = jnp.where(live_out, jnp.take(pose_weight, pose_ids), 0.0).reshape(-1)
    row_mass = jnp.zeros((planes * edge_len,), jnp.float32)
    row_mass = row_mass.at[voxel_flat].add(fraction * slot_mass)
    row_mass = row_mass.at[voxel_flat + 1].add((1.0 - fraction) * slot_mass)
    summed_volume, summed_mass = (
        lax.psum_scatter(
            accumulated.reshape(planes, edge_len, row_width), "img", scatter_dimension=1, tiled=True
        ),
        lax.psum_scatter(
            row_mass.reshape(planes, edge_len), "img", scatter_dimension=1, tiled=True
        ),
    )
    fourier = summed_volume / (summed_mass[:, :, None] + ridge)
    rows_part = fourier.shape[1]
    cosine, sine = dft_tables(edge_len)
    both_tables = jnp.concatenate([cosine, sine], axis=1)
    real_in = fourier[:, :, :edge_len].reshape(-1, edge_len)
    imag_in = fourier[:, :, edge_len:].reshape(-1, edge_len)
    real_turn = jnp.dot(real_in, both_tables, precision=lax.Precision.HIGHEST)
    imag_turn = jnp.dot(imag_in, both_tables, precision=lax.Precision.HIGHEST)
    real_part = real_turn[:, :edge_len] - imag_turn[:, edge_len:]
    imag_part = real_turn[:, edge_len:] + imag_turn[:, :edge_len]
    col_count = edge_len // img_count
    sectioned = jnp.concatenate(
        [
            real_part.reshape(planes, rows_part, img_count, col_count),
            imag_part.reshape(planes, rows_part, img_count, col_count),
        ],
        axis=3,
    )
    crossed = lax.all_to_all(sectioned, "img", split_axis=2, concat_axis=1, tiled=True)
    crossed = crossed.reshape(planes, edge_len, 2 * col_count)
    with_cos = jnp.einsum("ky,zkc->zyc", cosine, crossed, precision=lax.Precision.HIGHEST)
    with_sin = jnp.einsum("ky,zkc->zyc", sine, crossed, precision=lax.Precision.HIGHEST)
    density = (with_cos[:, :, :col_count] - with_sin[:, :, col_count:]) / edge_len
    row_correction = gridding(edge_len, 0, edge_len)
    col_correction = gridding(col_count, lax.axis_index("img") * col_count, edge_len)
    density = density * row_correction[None, :, None] * col_correction[None, None, :]
    return (density, posterior)


def solution(mesh):
    placed = (P("img", "slab"), P("slab", None, None), P("img"), P("img", None), P(), P(), P())
    return jax.shard_map(
        per_device,
        mesh=mesh,
        in_specs=placed,
        out_specs=(P("slab", None, "img"), P("img", None)),
        check_vma=False,
    )
```

profile of v0, /device:TPU:1, one launch (start us, length us, event | category | flops | bytes accessed | tf_op | source)
XLA Modules:
  0.0 813.2 jit_solution(3756778374884615266)
XLA Ops:
  8.8 5.3 gather_fusion.3
  14.1 5.3 gather_fusion.4
  22.7 4.1 select_convert_fusion
  26.8 8.6 %all-to-all-start = ((bf16[16,64,1024]{2,1,0:T(8,128)(2,1)}), bf16[16,64,1024]{2,1,0:T(8,128)(2,1)}, u32[]{:S(2)}, u32[]{:S(2)}) async-start(bf16[16,64,1024]{2,1,0:T(8,128)(2,1)} %select_convert_fusion), calls=%async_computation | async-start | bytes 4194304 | tf_op jit(solution)/shard_map/all_to_all | solution.py:70
  37.6 25.8 %all-to-all-done = bf16[16,64,1024]{2,1,0:T(8,128)(2,1)} async-done(((bf16[16,64,1024]{2,1,0:T(8,128)(2,1)}), bf16[16,64,1024]{2,1,0:T(8,128)(2,1)}, u32[]{:S(2)}, u32[]{:S(2)}) %all-to-all-start) | async-done | bytes 2097184 | tf_op jit(solution)/shard_map/all_to_all | solution.py:70
  63.4 6.3 scatter_custom_fusion
  70.0 6.5 subtract_bitcast_fusion
  79.4 101.4 %all-reduce.2.cloned.1.call-done = f32[2048,512]{0,1:T(8,128)} async-done(((f32[2048,512]{0,1:T(8,128)}), f32[2048,512]{0,1:T(8,128)}) %all-reduce.2.cloned.1.call-update) | async-done | bytes 4194320 | tf_op jit(solution)/shard_map/psum | solution.py:80
  180.8 412.7 %gather_fusion.2 = f32[32768]{0:T(1024)S(1)} fusion(f32[2048,512]{0,1:T(8,128)} %all-reduce.2.cloned.1.call-done, s32[32768]{0:T(1024)S(1)} %reshape.387), kind=kCustom, calls=%fused_computation.4 | custom fusion | bytes 524288 | tf_op jit(solution)/shard_map/jit(take_along_axis)/gather | solution.py:38
  594.9 61.7 %while.14 = (s32[]{:T(128)}, f32[2048,512]{1,0:T(8,128)}, s32[2048,16]{0,1:T(8,128)S(1)}, f32[2048,16]{0,1:T(8,128)S(1)}, s32[]{:T(128)}, /*index=5*/s32[]{:T(128)}) while((s32[]{:T(128)}, f32[2048,512]{1,0:T(8,128)}, s32[2048,16]{0,1:T(8,128)S(1)}, f32[2048,16]{0,1:T(8,128)S(1)}, s32[]{:T(128)}, /*index=5*/s32[]{:T(128)}) %tuple.66), condition=%wide.region_6.8_spmd.clone, body=%wide.region_5.7_spmd.clone.sunk | while | flops 4194307 | bytes 8437847 | solution.py:54
  656.6 5.8 convolution_convert_fusion
  662.5 5.4 gather_fusion
  670.7 5.4 all-to-all-start.1
  679.0 6.9 gather_fusion.1
  685.9 7.6 scatter_custom_fusion.3
  693.5 7.6 scatter_fusion
  702.3 12.1 %scatter_custom_fusion.1 = f32[1024,1024]{1,0:T(8,128)} fusion(s32[1024]{0:T(1024)S(1)} %bitcast.91, bf16[1024,1024]{1,0:T(8,128)(2,1)} %bitcast.16, f32[1024]{0:T(1024)S(1)} %div.80, f32[]{:T(128)} %constant.206.clone.1), kind=kCustom, calls=%fused_computation.17 | custom fusion | flops 3145728 | bytes 6295556 | tf_op jit(solution)/shard_map/scatter-add | solution.py:96
  714.4 14.0 %scatter_custom_fusion.2 = f32[1024,1024]{1,0:T(8,128)} fusion(f32[1024,1024]{1,0:T(8,128)} %scatter_custom_fusion.1, s32[1024]{0:T(1024)S(1)} %bitcast.89, bf16[1024,1024]{1,0:T(8,128)(2,1)} %bitcast.16, f32[1024]{0:T(1024)S(1)} %get-tuple-element.163), kind=kCustom, calls=%fused_computation.18 | custom fusion | flops 3145728 | bytes 6295552 | tf_op jit(solution)/shard_map/scatter-add | solution.py:97
  728.5 5.3 fusion.18
  734.6 36.2 %reduce-scatter.5.cloned.1.call-done = f32[2,64,1024]{2,1,0:T(8,128)} async-done(((f32[2,512,1024]{2,1,0:T(8,128)}), f32[2,64,1024]{2,1,0:T(8,128)}) %reduce-scatter.5.cloned.1.call-update) | async-done | bytes 524304 | tf_op jit(solution)/shard_map/reduce_scatter | solution.py:107
  777.6 7.0 all-to-all-start.2
  784.7 9.4 %all-to-all-done.2 = f32[2,64,8,128]{3,1,0,2:T(8,128)S(1)} async-done(((f32[2,64,8,128]{3,1,0,2:T(8,128)}), f32[2,64,8,128]{3,1,0,2:T(8,128)S(1)}, u32[]{:S(2)}, u32[]{:S(2)}) %all-to-all-start.2) | async-done | bytes 524320 | tf_op jit(solution)/shard_map/all_to_all | solution.py:132
  794.1 5.9 convolution_bitcast_fusion
  800.0 5.8 convolution_bitcast_fusion.1
  (142 shorter events, 88.2 us)
Async XLA Ops:
  7.2 1.6 copy-start
  8.0 0.6 copy-start.4
  20.8 0.6 copy-start.8
  22.1 0.6 copy-start.6
  26.8 36.6 %all-to-all-start = ((bf16[16,64,1024]{2,1,0:T(8,128)(2,1)}), bf16[16,64,1024]{2,1,0:T(8,128)(2,1)}, u32[]{:S(2)}, u32[]{:S(2)}) async-start(bf16[16,64,1024]{2,1,0:T(8,128)(2,1)} %select_convert_fusion), calls=%async_computation | async-start | bytes 4194304 | tf_op jit(solution)/shard_map/all_to_all | solution.py:70
  35.4 145.3 %all-reduce.2.cloned.1.call-start = ((), (), s32[]{:S(2)}) async-start(), calls=%async_computation.5 | async-start | bytes 8388608 | tf_op jit(solution)/shard_map/psum | solution.py:80
  76.5 0.9 copy-start.2
  180.8 413.3 %copy-start.3 = (s32[2048,16]{0,1:T(8,128)S(1)}, s32[2048,16]{0,1:T(8,128)}, u32[]{:S(2)}) copy-start(s32[2048,16]{0,1:T(8,128)} %param.14) | copy-start | bytes 393220
  180.8 413.3 %copy-start.11 = (f32[2048]{0:T(1024)S(1)}, f32[2048]{0:T(1024)}, u32[]{:S(2)}) copy-start(f32[2048]{0:T(1024)} %param.13) | copy-start | bytes 24580
  656.6 5.8 copy-start.10
  662.4 5.4 copy-start.13
  662.5 5.4 copy-start.14
  667.8 8.3 %copy-start.7 = (f32[1,16,64]{2,1,0:T(8,128)S(1)}, f32[1,16,64]{2,1,0:T(8,128)}, u32[]{:S(2)}) copy-start(f32[1,16,64]{2,1,0:T(8,128)} %copy-done.6) | copy-start | bytes 12292
  667.8 8.4 %copy-start.9 = (s32[1,16,64]{2,1,0:T(8,128)S(1)}, s32[1,16,64]{2,1,0:T(8,128)}, u32[]{:S(2)}) copy-start(s32[1,16,64]{2,1,0:T(8,128)} %copy-done.8) | copy-start | bytes 12292
  667.9 8.4 %copy-start.5 = (s32[1,16,64]{2,1,0:T(8,128)S(1)}, s32[1,16,64]{2,1,0:T(8,128)}, u32[]{:S(2)}) copy-start(s32[1,16,64]{2,1,0:T(8,128)} %copy-done.4) | copy-start | bytes 12292
  667.9 8.5 %copy-start.12 = (s32[16,64,1]{1,0,2:T(8,128)S(1)}, s32[16,64,1]{1,0,2:T(8,128)}, u32[]{:S(2)}) copy-start(s32[16,64,1]{1,0,2:T(8,128)} %get-tuple-element.141) | copy-start | bytes 12292
  670.7 31.6 %all-to-all-start.1 = ((bf16[16,64,1024]{2,1,0:T(8,128)(2,1)}), bf16[16,64,1024]{2,1,0:T(8,128)(2,1)}, u32[]{:S(2)}, u32[]{:S(2)}) async-start(bf16[16,64,1024]{2,1,0:T(8,128)(2,1)} %select_select_fusion), calls=%async_computation.1 | async-start | bytes 4194304 | tf_op jit(solution)/shard_map/all_to_all | solution.py:91
  676.1 57.7 %reduce-scatter.7.cloned.1.call-start = ((), (), s32[]{:S(2)}) async-start(), calls=%async_computation.7 | async-start | bytes 294912
  702.0 68.9 %reduce-scatter.5.cloned.1.call-start = ((), (), s32[]{:S(2)}) async-start(), calls=%async_computation.6 | async-start | bytes 4718592 | tf_op jit(solution)/shard_map/reduce_scatter | solution.py:107
  770.9 3.8 copy-start.1
  777.6 16.5 %all-to-all-start.2 = ((f32[2,64,8,128]{3,1,0,2:T(8,128)}), f32[2,64,8,128]{3,1,0,2:T(8,128)S(1)}, u32[]{:S(2)}, u32[]{:S(2)}) async-start(f32[2,64,8,128]{3,1,0,2:T(8,128)} %pad_maximum_fusion.3), calls=%async_computation.3 | async-start | bytes 1048576 | tf_op jit(solution)/shard_map/all_to_all | solution.py:132
Sparse Core Ops, SparseCore 0:
  76.7 104.0 all-reduce.1
  702.1 29.6 reduce-scatter.6
  734.4 36.4 reduce-scatter.4
where the time goes:
time: 827 us; the launch traced here: 813 us
  local copies, waits for them, and re-layouts  451 us (55%)
  waiting for transfers between devices  173 us (21%)
  other arithmetic  126 us (15%)
  matrix products  27.9 us (3%)
  starting transfers between devices  21.4 us (3%)
  between operations  14.1 us (2%)
    gather x5, local copies, waits for them, and re-layouts, posterior_of(): jnp.take_along_axis(score_rows, candidates, axis=1) * precision[:, None]  414 us
    psum x1, waiting for transfers between devices, per_device(): score_all = lax.psum(partial_score, 'slab')  101 us
    add x16, other arithmetic, add_one(): return spread_table + jnp.where(chosen == columns, amount, 0.0)  61.1 us
    reduce_scatter x1, waiting for transfers between devices, per_device(): lax.psum_scatter(accumulated.reshape(planes, edge_len, row_width), 'img',...  36.2 us
    all_to_all x1, waiting for transfers between devices, per_device(): lax.all_to_all(outgoing_rows, 'slab', split_axis=0, concat_axis=0, tiled=...  25.8 us
  transfers between devices with their start and end apart: 6, of which 4 were waited for; matrix products, arithmetic and copies ran while one was open for 8% of the time, Pallas kernels for 0%

commit v1 on v0

v1 whole, which is shorter than its diff:
```python
import math

import jax
import jax.numpy as jnp
import numpy as np
from jax import lax
from jax.sharding import PartitionSpec as P

NPOSE = 512
WSTEPS = 16
RIDGE = 0.25


def gridding(samples):
    offset = (np.arange(samples) - samples / 2) / samples
    return 1.0 / np.sinc(offset) ** 2


def angles(length):
    counter = np.arange(length)
    return (counter[:, None] * counter[None, :] % length) * (2.0 * math.pi / length)


def column_table(length, members):
    turn = angles(length)
    cosine, sine = np.cos(turn), np.sin(turn)
    scale = gridding(length)[None, :]
    to_re = np.concatenate([cosine, -sine], axis=0) * scale
    to_im = np.concatenate([sine, cosine], axis=0) * scale
    width = length // members
    both = np.stack([to_re.reshape(-1, members, width), to_im.reshape(-1, members, width)], axis=2)
    return jnp.asarray(both.reshape(2 * length, 2 * length), jnp.bfloat16)


def row_table(length):
    turn = angles(length)
    scale = gridding(length)[:, None] / length
    return jnp.asarray(np.concatenate([np.cos(turn), -np.sin(turn)], axis=1) * scale, jnp.bfloat16)


def per_device(images, volume, precision, candidates, slot_key, slot_voxel, slot_weight):
    members = lax.axis_size("img")
    slabs = lax.axis_size("slab")
    own = lax.axis_index("slab")
    member = lax.axis_index("img")
    planes, edge, width = volume.shape
    cap = slot_key.shape[2]
    deep = cap // members
    share = NPOSE // members
    voxels = planes * edge
    counts = jnp.sum((slot_key >= 0).astype(jnp.int32), axis=2)
    starts = jnp.cumsum(counts, axis=0) - counts

    out_start = lax.dynamic_index_in_dim(starts, own, 0, keepdims=False)
    residue = (jnp.arange(members)[:, None] - out_start[None, :]) % members
    chosen = residue[:, :, None, None] == jnp.arange(members)[None, None, None, :]

    def by_member(table):
        mine = lax.dynamic_index_in_dim(table, own, 0, keepdims=False).reshape(1, slabs, deep, members)
        return jnp.sum(jnp.where(chosen, mine, 0), axis=3).reshape(-1)

    all_key = by_member(slot_key)
    all_voxel = by_member(slot_voxel)
    all_weight = by_member(slot_weight)
    lower = jnp.where(all_key >= 0, all_weight, 0).astype(jnp.float32) / WSTEPS
    upper = jnp.where(all_key >= 0, WSTEPS - all_weight, 0).astype(jnp.float32) / WSTEPS
    places = jnp.arange(voxels)
    spot = all_voxel[None, :]
    weave = jnp.where(spot == places[:, None], lower[None, :], 0.0) + jnp.where(
        spot + 1 == places[:, None], upper[None, :], 0.0
    )
    weave = weave.astype(jnp.bfloat16)

    in_start = lax.dynamic_index_in_dim(starts, own, 1, keepdims=False)
    in_count = lax.dynamic_index_in_dim(counts, own, 1, keepdims=False)
    in_key = lax.dynamic_index_in_dim(slot_key, own, 1, keepdims=False)
    slot = jnp.arange(deep)[None, :] * members + ((member - in_start) % members)[:, None]
    row = jnp.where(slot < in_count[:, None], (in_start[:, None] + slot) // members, -1).reshape(-1)
    pack = (jnp.arange(share)[:, None] == row[None, :]).astype(jnp.bfloat16)
    order = in_start[:, None] + jnp.arange(cap)[None, :]
    order = (order % members) * share + order // members
    pose_row = jnp.sum(
        jnp.where(in_key.reshape(-1, 1) == jnp.arange(NPOSE)[None, :], order.reshape(-1, 1), 0), axis=0
    )

    mine = slabs * deep
    take = lax.dynamic_slice_in_dim(weave, member * mine, mine, 1)
    outgoing = lax.dot_general(
        take, volume.reshape(voxels, width), (((0,), (0,)), ((), ())), preferred_element_type=jnp.float32
    ).astype(jnp.bfloat16)
    received = lax.all_to_all(outgoing.reshape(slabs, deep, width), "slab", 0, 0, tiled=True)
    block = jnp.dot(pack, received.reshape(mine, width), preferred_element_type=jnp.float32).astype(jnp.bfloat16)
    slices = lax.all_gather(block, "img", axis=0, tiled=True)

    score = lax.dot_general(slices, images, (((1,), (1,)), ((), ())), preferred_element_type=jnp.float32)
    power = jnp.sum(jnp.square(slices.astype(jnp.float32)), axis=1)
    score = score - 0.5 * power[:, None]
    poses = candidates.T
    one_hot = poses[:, None, :] == jnp.arange(NPOSE)[None, :, None]
    rows = jnp.sum(jnp.where(one_hot, pose_row[None, :, None], 0), axis=1)
    row_ids = jnp.arange(NPOSE)[:, None]
    picked = jnp.stack(
        [jnp.sum(jnp.where(rows[k][None, :] == row_ids, score, 0.0), axis=0) for k in range(rows.shape[0])]
    )
    picked = lax.psum(picked, "slab") * precision[None, :]
    exponent = jnp.exp(picked - jnp.max(picked, axis=0, keepdims=True))
    posterior = exponent / jnp.sum(exponent, axis=0, keepdims=True)

    amount = posterior * precision[None, :]
    spread = jnp.zeros((NPOSE, images.shape[0]), jnp.float32)
    for k in range(rows.shape[0]):
        spread = jnp.where(rows[k][None, :] == row_ids, amount[k][None, :], spread)
    spread = spread.astype(jnp.bfloat16)
    row_weight = jnp.sum(spread.astype(jnp.float32), axis=1)
    pose_weight = jnp.sum(jnp.where(row_ids == pose_row[None, :], row_weight[:, None], 0.0), axis=0)
    pose_weight = lax.psum(pose_weight, "img")
    back = jnp.dot(spread, images, preferred_element_type=jnp.float32).astype(jnp.bfloat16)
    parts = lax.all_to_all(back.reshape(members, share, width), "img", 0, 0, tiled=True)
    summed = jnp.sum(parts.astype(jnp.float32), axis=0).astype(jnp.bfloat16)
    unpacked = lax.dot_general(
        pack, summed, (((0,), (0,)), ((), ())), preferred_element_type=jnp.float32
    ).astype(jnp.bfloat16)
    returned = lax.all_to_all(unpacked.reshape(slabs, deep, width), "slab", 0, 0, tiled=True)

    turned = jnp.dot(
        returned.reshape(mine, width), column_table(edge, members), preferred_element_type=jnp.float32
    ).astype(jnp.bfloat16)
    turned = turned.reshape(mine, members, width // members).transpose(1, 0, 2)
    crossed = lax.all_to_all(turned, "img", 0, 0, tiled=True).reshape(members * mine, width // members)
    accumulated = jnp.dot(weave, crossed, preferred_element_type=jnp.float32)
    slot_mass = jnp.sum(
        jnp.where(all_key[:, None] == jnp.arange(NPOSE)[None, :], pose_weight[None, :], 0.0), axis=1
    )
    mass = jnp.sum(weave.astype(jnp.float32) * slot_mass[None, :], axis=1)
    fourier = (accumulated / (mass[:, None] + RIDGE)).astype(jnp.bfloat16)
    half = width // members // 2
    fourier = fourier.reshape(planes, edge, 2, half).transpose(0, 2, 1, 3).reshape(planes, 2 * edge, half)
    density = jnp.einsum("yk,zkx->zyx", row_table(edge), fourier, preferred_element_type=jnp.float32)
    return (density, posterior.T)


def solution(mesh):
    placed = (P("img", "slab"), P("slab", None, None), P("img"), P("img", None), P(), P(), P())
    return jax.shard_map(
        per_device,
        mesh=mesh,
        in_specs=placed,
        out_specs=(P("slab", None, "img"), P("img", None)),
        check_vma=False,
    )
```

time: 827 us -> 240 us (0.29); the launches traced: 813 us -> 240 us
  local copies, waits for them, and re-layouts: 451 us -> 6.05 us
  other arithmetic: 126 us -> 38.9 us
  waiting for transfers between devices: 173 us -> 101 us
  blocking collectives: 0 us -> 34.4 us
    gather x9 -> x0, local copies, waits for them, and re-layouts: 437 us -> none  [the longest x5 414 us: posterior_of(): jnp.take_along_axis(score_rows, candidates, axis=1) * precision[:, None]]
    add x17 -> x5, other arithmetic: 61.1 us -> 0.17 us  [the longest x1 0.07 us: per_device(): in_start[:, None] + slot]
    scatter-add x4 -> x0, other arithmetic: 41.4 us -> none  [the longest x1 14 us: per_device(): accumulated.at[use_flat + 1].add((1.0 - use_fraction)[:, None] * contrib)]
    reduce_scatter x1 -> x0, waiting for transfers between devices: 36.2 us -> none  [per_device(): lax.psum_scatter(accumulated.reshape(planes, edge_len, row_width), 'img',...]
    reduce_sum x2 -> x10, other arithmetic: 2.56 us -> 33.1 us  [the longest x1 14.8 us: per_device(): row_weight = jnp.sum(spread.astype(jnp.float32), axis=1)]
    all_to_all x3, waiting for transfers between devices: 35.2 us -> 10.6 us  [the longest x1 5.47 us: per_device(): lax.all_to_all(turned, 'img', 0, 0, tiled=True)]
    all_to_all x0 -> x1, blocking collectives: none -> 21.3 us  [per_device(): lax.all_to_all(back.reshape(members, share, width), 'img', 0, 0, tiled=True)]
    psum x1, waiting for transfers between devices: 101 us -> 80.5 us  [per_device(): picked = lax.psum(picked, 'slab') * precision[None, :]]
  transfers between devices with their start and end apart: 6 -> 5, of which waited for: 4 -> 4; matrix products, arithmetic and copies ran while one was open for 8% -> 7% of each run, Pallas kernels for 0% -> 0%
where the time goes in v1:
time: 240 us
  waiting for transfers between devices  101 us (42%)
  other arithmetic  38.9 us (16%)
  blocking collectives  34.4 us (14%)
  matrix products  27.4 us (11%)
  starting transfers between devices  17.6 us (7%)
  between operations  14.3 us (6%)
  local copies, waits for them, and re-layouts  6.05 us (3%)
    psum x1, waiting for transfers between devices, per_device(): picked = lax.psum(picked, 'slab') * precision[None, :]  80.5 us
    all_to_all x1, blocking collectives, per_device(): lax.all_to_all(back.reshape(members, share, width), 'img', 0, 0, tiled=True)  21.3 us
    reduce_sum x1, other arithmetic, per_device(): row_weight = jnp.sum(spread.astype(jnp.float32), axis=1)  14.8 us
    dot_general x1, matrix products, per_device(): lax.dot_general(slices, images, (((1,), (1,)), ((), ())), preferred_eleme...  14.3 us
    reduce_sum x1, other arithmetic, per_device(): rows = jnp.sum(jnp.where(one_hot, pose_row[None, :, None], 0), axis=1)  13.2 us
    psum x1, blocking collectives, per_device(): pose_weight = lax.psum(pose_weight, 'img')  13.1 us
    all_gather x1, waiting for transfers between devices, per_device(): slices = lax.all_gather(block, 'img', axis=0, tiled=True)  9.88 us
    all_to_all x1, starting transfers between devices, per_device(): lax.all_to_all(outgoing.reshape(slabs, deep, width), 'slab', 0, 0, tiled=...  8.6 us
  transfers between devices with their start and end apart: 5, of which 4 were waited for; matrix products, arithmetic and copies ran while one was open for 7% of the time, Pallas kernels for 0%

profile of v1, /device:TPU:1, one launch (start us, length us, event | category | flops | bytes accessed | tf_op | source)
XLA Modules:
  0.0 239.6 jit_solution(12554999962809058420)
XLA Ops:
  7.2 1.4 convert_reduce_fusion.1
  11.2 1.2 add_convert_fusion
  12.4 1.2 fusion.1
  13.6 8.6 %all-to-all-start = ((bf16[16,8,1024]{2,1,0:T(8,128)(2,1)}), bf16[16,8,1024]{2,1,0:T(8,128)(2,1)S(1)}, u32[]{:S(2)}, u32[]{:S(2)}) async-start(bf16[16,8,1024]{2,1,0:T(8,128)(2,1)} %fusion.1), calls=%async_computation | async-start | bytes 524288 | tf_op jit(solution)/shard_map/all_to_all | solution.py:91
  24.6 5.1 %all-to-all-done = bf16[16,8,1024]{2,1,0:T(8,128)(2,1)S(1)} async-done(((bf16[16,8,1024]{2,1,0:T(8,128)(2,1)}), bf16[16,8,1024]{2,1,0:T(8,128)(2,1)S(1)}, u32[]{:S(2)}, u32[]{:S(2)}) %all-to-all-start) | async-done | bytes 262176 | tf_op jit(solution)/shard_map/all_to_all | solution.py:91
  30.6 13.2 %select_reduce_fusion = s32[16,2048]{1,0:T(8,128)S(1)} fusion(s32[512]{0:T(512)S(1)} %select_reduce_fusion.18, s32[16,2048]{1,0:T(8,128)S(1)} %bitcast.96), kind=kLoop, calls=%fused_computation | loop fusion | flops 50298880 | bytes 264192 | tf_op jit(solution)/shard_map/reduce_sum | solution.py:100
  43.9 9.9 %all-gather.2.cloned.1.call-done = bf16[512,1024]{1,0:T(8,128)(2,1)} async-done(((bf16[64,1024]{1,0:T(8,128)(2,1)}), bf16[512,1024]{1,0:T(8,128)(2,1)}) %all-gather.2.cloned.1.call-update) | async-done | bytes 1048592 | tf_op jit(solution)/shard_map/all_gather | solution.py:93
  53.7 1.5 multiply_reduce_fusion.1
  55.3 14.3 %select_reduce_fusion.1 = (f32[2048]{0:T(1024)S(1)}, f32[2048]{0:T(1024)S(1)}, f32[2048]{0:T(1024)S(1)}, f32[2048]{0:T(1024)S(1)}, f32[2048]{0:T(1024)S(1)}, /*i...) fusion(s32[2048]{0:T(1024)S(1)} %bitcast.127, ...), kind=kOutput, calls=%fused_computation.5 | convolution fusion | flops 2198831104 | bytes 5507072 | tf_op jit(solution)/shard_map/dot_general | solution.py:95
  69.6 1.5 stack.67
  71.1 80.5 %all-reduce.2.cloned.1.call-done = f32[16,2048]{1,0:T(8,128)} async-done(((f32[16,2048]{1,0:T(8,128)}), f32[16,2048]{1,0:T(8,128)}) %all-reduce.2.cloned.1.call-update) | async-done | bytes 131088 | tf_op jit(solution)/shard_map/psum | solution.py:105
  153.4 1.6 fusion.9
  155.1 14.8 %convert_reduce_fusion = (f32[512]{0:T(512)S(1)}, bf16[512,2048]{1,0:T(8,128)(2,1)S(1)}) fusion(f32[2048]{0:T(1024)S(1)} %bitcast.130, s32[2048]{0:T(1024)S(1)} %bitcast.98, f32[2048]{0:T(1024)S(1)} %bitcast.131, s32[2048]{0:T(1024)S(1)} %bitcast.126, f32[2048]{0:T(1024)S(1)} %bitcast.132, s32[2048]{0:T(1024)S(1)} %bitcast.124, f32[2048]{0:T(1024)S(1)} %bitcast.133, ...), kind=kLoop, calls=%fused_computation.3 | loop fusion | flops 35651072 | bytes 2361344 | tf_op jit(solution)/shard_map/reduce_sum | solution.py:114
  169.9 4.5 %convolution_convert_fusion = bf16[512,1024]{1,0:T(8,128)(2,1)S(1)} fusion(bf16[512,2048]{1,0:T(8,128)(2,1)S(1)} %get-tuple-element.24, bf16[2048,1024]{1,0:T(8,128)(2,1)} %param.9), kind=kOutput, calls=%fused_computation.46 | convolution fusion | flops 2148007936 | bytes 7340032 | tf_op jit(solution)/shard_map/dot_general | solution.py:117
  174.4 21.3 %all_to_all.20 = bf16[8,64,1024]{2,1,0:T(8,128)(2,1)S(1)} all-to-all(bf16[8,64,1024]{2,1,0:T(8,128)(2,1)S(1)} %bitcast.91), channel_id=1, replica_groups=mesh['slab'=16,'img'=8] {'img'}, dimensions={0} | all-to-all | bytes 2097152 | tf_op jit(solution)/shard_map/all_to_all | solution.py:118
  196.0 1.0 fusion.3
  196.9 4.7 %all-to-all-start.2 = ((bf16[16,8,1024]{2,1,0:T(8,128)(2,1)}), bf16[16,8,1024]{2,1,0:T(8,128)(2,1)S(1)}, u32[]{:S(2)}, u32[]{:S(2)}) async-start(bf16[16,8,1024]{2,1,0:T(8,128)(2,1)} %fusion.3), calls=%async_computation.2 | async-start | bytes 524288 | tf_op jit(solution)/shard_map/all_to_all | solution.py:123
  201.9 13.1 %psum.15 = f32[512]{0:T(512)S(1)} all-reduce(f32[512]{0:T(512)S(1)} %select_reduce_fusion.19), channel_id=1, replica_groups=mesh['slab'=16,'img'=8] {'img'}, use_global_device_ids=true, to_apply=%region_30.31 | all-reduce | flops 512 | bytes 4096 | tf_op jit(solution)/shard_map/psum | solution.py:116
  215.4 2.0 fusion.2
  218.2 4.3 %all-to-all-start.3 = ((bf16[8,128,128]{2,1,0:T(8,128)(2,1)}), bf16[8,128,128]{2,1,0:T(8,128)(2,1)S(1)}, u32[]{:S(2)}, u32[]{:S(2)}) async-start(bf16[8,128,128]{2,1,0:T(8,128)(2,1)} %bitcast.89), calls=%async_computation.3 | async-start | bytes 524288 | tf_op jit(solution)/shard_map/all_to_all | solution.py:129
  222.5 1.0 multiply_reduce_fusion
  223.5 5.5 %all-to-all-done.3 = bf16[8,128,128]{2,1,0:T(8,128)(2,1)S(1)} async-done(((bf16[8,128,128]{2,1,0:T(8,128)(2,1)}), bf16[8,128,128]{2,1,0:T(8,128)(2,1)S(1)}, u32[]{:S(2)}, u32[]{:S(2)}) %all-to-all-start.3) | async-done | bytes 262176 | tf_op jit(solution)/shard_map/all_to_all | solution.py:129
  229.0 1.1 fusion
  230.3 2.4 %convolution_bitcast_fusion = f32[2,512,64]{1,2,0:T(8,128)} fusion(bf16[2,1024,64]{2,1,0:T(8,128)(2,1)S(1)} %reshape.245, bf16[512,1024,1]{1,0,2:T(8,128)(2,1)} %constant.126), kind=kOutput, calls=%fused_computation.55 | convolution fusion | flops 134217728 | bytes 1572864 | tf_op jit(solution)/shard_map/yk,zkx->zyx/dot_general | solution.py:138
  (56 shorter events, 9.7 us)
Async XLA Ops:
  7.2 5.2 %copy-start = (bf16[2,512,1024]{2,1,0:T(8,128)(2,1)S(1)}, bf16[2,512,1024]{2,1,0:T(8,128)(2,1)}, u32[]{:S(2)}) copy-start(bf16[2,512,1024]{2,1,0:T(8,128)(2,1)} %param.10) | copy-start | bytes 6291460
  7.2 23.4 %copy-start.1 = (s32[2048,16]{0,1:T(8,128)S(1)}, s32[2048,16]{0,1:T(8,128)}, u32[]{:S(2)}) copy-start(s32[2048,16]{0,1:T(8,128)} %param.12) | copy-start | bytes 393220
  13.6 16.1 %all-to-all-start = ((bf16[16,8,1024]{2,1,0:T(8,128)(2,1)}), bf16[16,8,1024]{2,1,0:T(8,128)(2,1)S(1)}, u32[]{:S(2)}, u32[]{:S(2)}) async-start(bf16[16,8,1024]{2,1,0:T(8,128)(2,1)} %fusion.1), calls=%async_computation | async-start | bytes 524288 | tf_op jit(solution)/shard_map/all_to_all | solution.py:91
  22.2 31.5 %all-gather.2.cloned.1.call-start = ((), (), s32[]{:S(2)}) async-start(), calls=%async_computation.4 | async-start | bytes 1179648 | tf_op jit(solution)/shard_map/all_gather | solution.py:93
  30.5 121.0 %all-reduce.2.cloned.1.call-start = ((), (), s32[]{:S(2)}) async-start(), calls=%async_computation.5 | async-start | bytes 262144 | tf_op jit(solution)/shard_map/psum | solution.py:105
  55.3 96.3 %copy-start.2 = (f32[2048]{0:T(1024)S(1)}, f32[2048]{0:T(1024)}, u32[]{:S(2)}) copy-start(f32[2048]{0:T(1024)} %param.11) | copy-start | bytes 24580
  196.9 18.5 %all-to-all-start.2 = ((bf16[16,8,1024]{2,1,0:T(8,128)(2,1)}), bf16[16,8,1024]{2,1,0:T(8,128)(2,1)S(1)}, u32[]{:S(2)}, u32[]{:S(2)}) async-start(bf16[16,8,1024]{2,1,0:T(8,128)(2,1)} %fusion.3), calls=%async_computation.2 | async-start | bytes 524288 | tf_op jit(solution)/shard_map/all_to_all | solution.py:123
  218.2 10.8 %all-to-all-start.3 = ((bf16[8,128,128]{2,1,0:T(8,128)(2,1)}), bf16[8,128,128]{2,1,0:T(8,128)(2,1)S(1)}, u32[]{:S(2)}, u32[]{:S(2)}) async-start(bf16[8,128,128]{2,1,0:T(8,128)(2,1)} %bitcast.89), calls=%async_computation.3 | async-start | bytes 524288 | tf_op jit(solution)/shard_map/all_to_all | solution.py:129
Sparse Core Ops, SparseCore 0:
  30.7 23.0 all-gather.1
  71.2 80.2 all-reduce.1

commit v2 on v1

v2 whole, which is shorter than its diff:
```python
import functools
import math

import jax
import jax.numpy as jnp
import numpy as np
from jax import lax
from jax.experimental import pallas as pl
from jax.experimental.pallas import tpu as pltpu
from jax.sharding import PartitionSpec as P

NPOSE = 512
WSTEPS = 16
RIDGE = 0.25
LANES = 128
F32 = jnp.float32
BF16 = jnp.bfloat16


def gridding(samples):
    offset = (np.arange(samples) - samples / 2) / samples
    return 1.0 / np.sinc(offset) ** 2


def angles(length):
    counter = np.arange(length)
    return (counter[:, None] * counter[None, :] % length) * (2.0 * math.pi / length)


def column_table(length, members):
    turn = angles(length)
    cosine, sine = np.cos(turn), np.sin(turn)
    scale = gridding(length)[None, :]
    to_re = np.concatenate([cosine, -sine], axis=0) * scale
    to_im = np.concatenate([sine, cosine], axis=0) * scale
    width = length // members
    both = np.stack([to_re.reshape(-1, members, width), to_im.reshape(-1, members, width)], axis=2)
    return jnp.asarray(both.reshape(2 * length, 2 * length), BF16)


def row_table(length):
    turn = angles(length)
    scale = gridding(length)[:, None] / length
    return jnp.asarray(np.concatenate([np.cos(turn), -np.sin(turn)], axis=1) * scale, BF16)


def remote(src, dst, sends, recvs, device):
    return pltpu.make_async_remote_copy(
        src_ref=src,
        dst_ref=dst,
        send_sem=sends,
        recv_sem=recvs,
        device_id=device,
        device_id_type=pl.DeviceIdType.MESH,
    )


def dot(left, right):
    return jnp.dot(left, right, preferred_element_type=F32)


def each(count, step, first=0):
    def body(index, carry):
        step(index)
        return carry

    lax.fori_loop(first, count, body, 0)


def rows_at(start, size):
    return pl.ds(pl.multiple_of(start, size), size)


def iota(shape, axis):
    return lax.broadcasted_iota(jnp.int32, shape, axis)


def pick_row(mask, values):
    return jnp.sum(jnp.where(mask, values, 0.0), axis=0, keepdims=True)


def kernel(
    slabs, members,
    images, volume, columns, rows, precision_in, poses_in, keys_in, voxels_in, weights_in,
    density, posterior,
    images_v, volume_v, columns_v, rows_v, precision, poses, keys, voxel_of, weight_of,
    slot_table, pack_table, pose_row,
    outgoing, incoming, slices, half_power, weave,
    picks, picks_in, shares, spread, row_weight,
    away, away_in, kept, opposite, opposite_in, ring, ring_in,
    masses, inverse, returning, returned, crossing, crossed,
    loads, slab_send, slab_recv, img_send, img_recv,
):
    own = lax.axis_index("slab")
    member = lax.axis_index("img")
    ring_len = members // 2
    chip, core = member // 2, lax.rem(member, 2)
    share = NPOSE // members
    half = share // 2
    side = ring_len * share
    deep = outgoing.shape[1]
    mine = slabs * deep
    cap = keys.shape[2]
    width = volume_v.shape[1]
    voxels = volume_v.shape[0]
    cands = poses.shape[0]
    right = 2 * lax.rem(chip + 1, ring_len) + core
    left = 2 * lax.rem(chip + ring_len - 1, ring_len) + core
    partner = 2 * chip + 1 - core

    def slab_peer(step):
        return lax.rem(own + step, slabs)

    def img_peer(step):
        return lax.rem(member + step, members)

    barrier = pltpu.get_barrier_semaphore()

    def greet(axis, peer):
        pl.semaphore_signal(barrier, inc=1, device_id={axis: peer}, device_id_type=pl.DeviceIdType.MESH)

    sources = [keys_in, voxels_in, weights_in, volume, poses_in, images, precision_in, columns, rows]
    targets = [keys, voxel_of, weight_of, volume_v, poses, images_v, precision, columns_v, rows_v]
    load = [pltpu.make_async_copy(src, dst, loads.at[i]) for i, (src, dst) in enumerate(zip(sources, targets))]
    for index in range(5):
        load[index].start()
    for step in range(1, slabs):
        greet("slab", slab_peer(step))
    for step in range(1, members):
        greet("img", img_peer(step))

    for index in range(3):
        load[index].wait()
    before = jnp.zeros((slabs, cap), F32)
    for slab in range(slabs):
        before += jnp.where(keys[slab] >= 0, 1.0, 0.0) * jnp.where(own > slab, 1.0, 0.0)
    out_start = jnp.sum(before, axis=1, keepdims=True)
    total_slots = slabs * cap
    position = iota((1, total_slots), 1)
    block_sel = iota((slabs, total_slots), 0) == ((position >> 3) & (slabs - 1))
    start_row = pick_row(block_sel, out_start).astype(jnp.int32)
    slot_row = members * (position & 7) + (((position >> 7) - start_row) & 7)
    slot_sel = iota((cap, total_slots), 0) == slot_row
    own_key = keys[own]
    own_code = voxel_of[own] * 32 + jnp.where(own_key >= 0, weight_of[own], 31)
    chooser = jnp.where(block_sel, 1.0, 0.0)

    def ordered(table):
        wide = lax.dot_general(
            table.astype(F32), chooser, (((0,), (0,)), ((), ())),
            precision=lax.Precision.HIGHEST, preferred_element_type=F32,
        )
        return pick_row(slot_sel, wide)

    code_row = ordered(own_code).astype(jnp.int32)
    level = code_row & 31
    alive = level <= WSTEPS
    slot_table[0:1, :] = (code_row >> 5).astype(F32)
    slot_table[1:2, :] = jnp.where(alive, level, 0).astype(F32) * (1.0 / WSTEPS)
    slot_table[2:3, :] = jnp.where(alive, WSTEPS - level, 0).astype(F32) * (1.0 / WSTEPS)
    slot_table[3:4, :] = ordered(own_key)
    slot_table[4:8, :] = jnp.zeros((4, total_slots), F32)

    own_cols = slot_table[:, rows_at(member * mine, mine)].T
    place = iota((mine, voxels), 1)
    spot = own_cols[:, 0:1].astype(jnp.int32)
    take = jnp.where(place == spot, own_cols[:, 1:2], 0.0) + jnp.where(place == spot + 1, own_cols[:, 2:3], 0.0)
    load[3].wait()
    for index in range(5, len(load)):
        load[index].start()
    woven = dot(take.astype(BF16), volume_v[...])
    for block in range(slabs):
        outgoing[block] = woven[block * deep : (block + 1) * deep].astype(BF16)
    pl.semaphore_wait(barrier, slabs - 1 + members - 1)

    def slab_copy(stage, src, dst, step):
        peer = slab_peer(step)
        return remote(
            src.at[peer], dst.at[own], slab_send.at[stage, step], slab_recv.at[stage, step], {"slab": peer}
        )

    def slab_arrival(stage, dst, step):
        peer = slab_peer(slabs - step)
        return remote(
            dst.at[peer], dst.at[peer], slab_send.at[stage, step], slab_recv.at[stage, step], {"slab": peer}
        )

    def slab_exchange(stage, src, dst):
        for step in range(1, slabs):
            slab_copy(stage, src, dst, step).start()

    def slab_arrivals(stage, dst):
        for step in range(1, slabs):
            slab_arrival(stage, dst, step).wait_recv()

    def img_copy(slot, src, dst, device):
        return remote(src, dst, img_send.at[slot], img_recv.at[slot], {"img": device})

    slab_exchange(0, outgoing, incoming)
    incoming[own] = outgoing[own]

    in_key = jnp.concatenate(
        [jnp.sum(jnp.where(iota((slabs, cap), 0) == own, keys[slab], 0), axis=0, keepdims=True) for slab in range(slabs)],
        axis=0,
    )
    live = jnp.where(in_key >= 0, 1.0, 0.0).astype(BF16)
    count = dot(live, jnp.ones((cap, LANES), BF16))
    earlier = jnp.where(iota((slabs, slabs), 1) < iota((slabs, slabs), 0), 1.0, 0.0).astype(BF16)
    start = dot(earlier, count.astype(BF16))
    lane = iota((1, mine), 1)
    slab_sel = iota((slabs, mine), 0) == (lane >> 3)
    in_start = pick_row(slab_sel, start).astype(jnp.int32)
    in_count = pick_row(slab_sel, count).astype(jnp.int32)
    slot = members * (lane & 7) + ((member - in_start) & 7)
    pack_row = jnp.where(slot < in_count, (in_start + slot) >> 3, -1)
    pack_table[...] = jnp.broadcast_to(pack_row, (8, mine)).astype(F32)

    number = start[:, :cap].astype(jnp.int32) + iota((slabs, cap), 1)
    holder = number & (members - 1)
    ahead = ((holder >> 1) - chip) & (ring_len - 1)
    near = jnp.where(ahead == 0, 3, jnp.where(ahead == 1, 1, jnp.where(ahead == 2, 0, 2)))
    row = jnp.where((holder & 1) == core, near, members - 1 - near) * share + (number >> 3)
    key_cols, row_cols = in_key.astype(F32).T, row.astype(F32).T
    pose_ids = iota((cap, NPOSE), 1).astype(F32)
    found_rows = jnp.zeros((cap, NPOSE), F32)
    for slab in range(slabs):
        found_rows += jnp.where(key_cols[:, slab : slab + 1] == pose_ids, row_cols[:, slab : slab + 1], 0.0)
    pose_row[...] = jnp.broadcast_to(jnp.sum(found_rows, axis=0, keepdims=True), (8, NPOSE)).astype(jnp.int32)

    load[4].wait()
    for part in range(poses.shape[1] // LANES):
        for k in range(0, cands, 8):
            at = (slice(k, k + 8), slice(part * LANES, (part + 1) * LANES))
            pose = poses[at]
            low, high = pose & (LANES - 1), pose >> 7
            renamed = jnp.zeros_like(pose)
            for piece in range(NPOSE // LANES):
                table = pose_row[:, piece * LANES : (piece + 1) * LANES]
                found = jnp.take_along_axis(table, low, axis=1, mode="promise_in_bounds")
                renamed = jnp.where(high == piece, found, renamed)
            poses[at] = renamed

    slab_arrivals(0, incoming)
    arrived = jnp.concatenate([incoming[block].astype(F32) for block in range(slabs)], axis=0).astype(BF16)
    pack = jnp.where(iota((share, mine), 0).astype(F32) == pack_table[0:1, :], 1.0, 0.0).astype(BF16)

    def block_of(index, first=0, size=share):
        return slices.at[index * share + first : index * share + first + size]

    FAR, RIGHT, LEFT, HOME = 0, 1, 2, 3
    slices[HOME * share : (HOME + 1) * share, :] = dot(pack, arrived).astype(BF16)

    def other(index):
        return members - 1 - index

    def top(index):
        return block_of(index, 0, half)

    def bottom(index):
        return block_of(index, half, half)

    gathers = [
        img_copy(0, top(HOME), top(LEFT), right),
        img_copy(1, bottom(HOME), bottom(RIGHT), left),
        img_copy(2, block_of(HOME), block_of(other(HOME)), partner),
        img_copy(3, bottom(HOME), bottom(LEFT), right),
        img_copy(4, top(HOME), top(RIGHT), left),
        img_copy(5, top(LEFT), top(FAR), right),
        img_copy(6, bottom(RIGHT), bottom(FAR), left),
        img_copy(7, block_of(LEFT), block_of(other(LEFT)), partner),
        img_copy(8, block_of(RIGHT), block_of(other(RIGHT)), partner),
        img_copy(9, top(FAR), top(other(FAR)), partner),
        img_copy(10, bottom(FAR), bottom(other(FAR)), partner),
    ]
    for index in range(5):
        gathers[index].start()

    def weave_step(index):
        at = iota((LANES, total_slots), 0) + index * LANES
        spots = slot_table[0:1, :].astype(jnp.int32)
        value = jnp.where(spots == at, slot_table[1:2, :], 0.0) + jnp.where(spots + 1 == at, slot_table[2:3, :], 0.0)
        weave[rows_at(index * LANES, LANES), :] = value.astype(BF16)

    each(voxels // LANES, weave_step)
    gathers[0].wait_recv()
    gathers[5].start()
    gathers[1].wait_recv()
    gathers[6].start()
    gathers[3].wait_recv()
    gathers[7].start()
    gathers[4].wait_recv()
    gathers[8].start()
    load[5].wait()

    def power_step(index):
        at = rows_at(index * share, share)
        values = slices[at, :].astype(F32)
        total = 0.5 * jnp.sum(values * values, axis=1, keepdims=True)
        half_power[at, :] = jnp.broadcast_to(total, (share, LANES))

    chunk = 2 * LANES
    chunks = images_v.shape[0] // chunk

    def picks_of(score, pieces, numbers, value):
        for first, offset, size in pieces:
            block = score[offset : offset + size] - half_power[first : first + size, :]
            for group in range(size // 8):
                picked = jnp.take_along_axis(
                    block[group * 8 : (group + 1) * 8], numbers[0], axis=0, mode="promise_in_bounds"
                )
                value[0] = jnp.where(numbers[2] == first // 8 + group, picked, value[0])
                picked = jnp.take_along_axis(
                    block[group * 8 : (group + 1) * 8], numbers[1], axis=0, mode="promise_in_bounds"
                )
                value[1] = jnp.where(numbers[3] == first // 8 + group, picked, value[1])
        return value

    def score_chunk(index, table, pieces, resume):
        score = lax.dot_general(
            table, images_v[rows_at(index * chunk, chunk), :],
            (((1,), (1,)), ((), ())), preferred_element_type=F32,
        )
        for part in range(chunk // LANES):
            number = poses[:, rows_at(index * chunk + part * LANES, LANES)]
            numbers = [number[0:8] & 7, number[8:16] & 7, number[0:8] >> 3, number[8:16] >> 3]
            block = index * (chunk // LANES) + part
            if resume:
                value = [picks[block, 0:8], picks[block, 8:16]]
            else:
                value = [jnp.zeros((8, LANES), F32), jnp.zeros((8, LANES), F32)]
            value = picks_of(score[:, part * LANES : (part + 1) * LANES], pieces, numbers, value)
            picks[block] = jnp.concatenate(value, axis=0)

    def near_step(index):
        score_chunk(index, slices[share : NPOSE - share, :], [(share, 0, NPOSE - 2 * share)], False)

    gathers[2].wait_recv()
    gathers[7].wait_recv()
    gathers[8].wait_recv()
    each(members - 1, power_step, 1)
    each(chunks // 2, near_step)
    gathers[5].wait_recv()
    gathers[9].start()
    gathers[6].wait_recv()
    gathers[10].start()
    each(chunks, near_step, chunks // 2)
    gathers[9].wait_recv()
    gathers[10].wait_recv()
    power_step(0)
    power_step(members - 1)

    def far_chunk(index):
        table = jnp.concatenate([slices[0:share, :], slices[NPOSE - share : NPOSE, :]], axis=0)
        score_chunk(index, table, [(0, 0, share), (NPOSE - share, share, share)], True)

    def pick_copy(peer):
        step = lax.rem(peer - own + slabs, slabs)
        return slab_copy(1, picks, picks_in, step)

    def far_step(turn):
        index = lax.rem(own // 2 + turn, chunks)
        far_chunk(index)
        pick_copy(2 * index).start()
        pick_copy(2 * index + 1).start()

    each(chunks, far_step, 1)
    far_chunk(own // 2)
    sibling = own + 1 - 2 * lax.rem(own, 2)
    pick_copy(sibling).start()
    picks_in[own] = picks[own]
    load[6].wait()
    row_weight[...] = jnp.zeros_like(row_weight)
    slab_arrivals(1, picks_in)
    total = picks_in[0]
    for block in range(1, slabs):
        total = total + picks_in[block]
    total = total * precision[:, rows_at(own * LANES, LANES)]
    exponent = jnp.exp(total - jnp.max(total, axis=0, keepdims=True))
    shares[own] = exponent / jnp.sum(exponent, axis=0, keepdims=True)

    def share_copy(step):
        return remote(
            shares.at[own], shares.at[own], slab_send.at[2, step], slab_recv.at[2, step], {"slab": slab_peer(step)}
        )

    for step in range(1, slabs):
        share_copy(step).start()
    tile = LANES

    def spread_chunk(block):
        at = rows_at(block * LANES, LANES)
        amount = shares[block] * precision[:, at]
        number = poses[:, at]
        for first in range(0, NPOSE, tile):
            row = iota((tile, LANES), 0) + first
            value = jnp.zeros((tile, LANES), F32)
            for k in range(cands):
                value = jnp.where(number[k : k + 1] == row, amount[k : k + 1], value)
            rounded = value.astype(BF16)
            spread[first : first + tile, at] = rounded
            row_weight[first : first + tile, :] += rounded.astype(F32)

    def spread_step(step):
        slab_arrival(2, shares, step).wait_recv()
        spread_chunk(slab_peer(slabs - step))

    spread_chunk(own)
    each(slabs, spread_step, 1)

    stripe = 2 * LANES
    stripes = width // stripe

    def away_copy(index):
        at = rows_at(index * stripe, stripe)
        return img_copy(24 + index, away.at[:, at], away_in.at[:, at], partner)

    def away_step(index):
        at = rows_at(index * stripe, stripe)
        away[:, at] = dot(spread[side : 2 * side, :], images_v[:, at]).astype(BF16)
        away_copy(index).start()

    def kept_step(index):
        at = rows_at(index * stripe, stripe)
        kept[:, at] = dot(spread[0:side, :], images_v[:, at])

    each(stripes, away_step)
    each(stripes, kept_step)
    each(stripes, lambda index: away_copy(index).wait_recv())

    def kept_part(index, first=0, size=share):
        here = index * share + first
        there = (ring_len - 1 - index) * share + first
        return kept[here : here + size, :] + away_in[there : there + size, :].astype(F32)

    opposite[...] = kept_part(FAR).astype(BF16)
    ring_copies = [
        img_copy(11, opposite.at[0:half], opposite_in.at[0:half], right),
        img_copy(12, opposite.at[half:share], opposite_in.at[half:share], left),
        img_copy(13, ring.at[0, half:share], ring_in.at[0, half:share], right),
        img_copy(14, ring.at[1, 0:half], ring_in.at[1, 0:half], left),
        img_copy(15, ring.at[0, 0:half], ring_in.at[0, 0:half], right),
        img_copy(28, ring.at[1, half:share], ring_in.at[1, half:share], left),
    ]
    ring_copies[0].start()
    ring_copies[1].start()
    ring[0, half:share] = kept_part(RIGHT, half, half).astype(BF16)
    ring_copies[2].start()
    ring[1, 0:half] = kept_part(LEFT, 0, half).astype(BF16)
    ring_copies[3].start()
    ring_copies[0].wait_recv()
    ring[0, 0:half] = (kept_part(RIGHT, 0, half) + opposite_in[0:half, :].astype(F32)).astype(BF16)
    ring_copies[4].start()
    ring_copies[1].wait_recv()
    ring[1, half:share] = (kept_part(LEFT, half, half) + opposite_in[half:share, :].astype(F32)).astype(BF16)
    ring_copies[5].start()

    weight = jnp.sum(row_weight[...], axis=1, keepdims=True)
    mass_row = pick_row(iota((NPOSE, NPOSE), 0) == pose_row[0:1, :], weight)
    masses[member] = jnp.broadcast_to(mass_row, (8, NPOSE))

    def mass_copy(step):
        return img_copy(16 + step, masses.at[member], masses.at[member], img_peer(step))

    def mass_arrival(step):
        peer = img_peer(members - step)
        return img_copy(16 + step, masses.at[peer], masses.at[peer], peer)

    for step in range(1, members):
        mass_copy(step).start()
    for block in range(slabs):
        posterior[:, block * LANES : (block + 1) * LANES] = shares[block]
    held = kept_part(HOME)
    for index in range(2, 6):
        ring_copies[index].wait_recv()
    summed = (held + ring_in[0].astype(F32) + ring_in[1].astype(F32)).astype(BF16)

    unpack = jnp.where(pack_table[...].T[:, 0:1] == iota((mine, share), 1).astype(F32), 1.0, 0.0).astype(BF16)
    unpacked = dot(unpack, summed)
    for block in range(slabs):
        returning[block] = unpacked[block * deep : (block + 1) * deep].astype(BF16)
    slab_exchange(3, returning, returned)
    returned[own] = returning[own]

    for step in range(1, members):
        mass_arrival(step).wait_recv()
    mass_total = masses[0]
    for index in range(1, members):
        mass_total = mass_total + masses[index]
    lanes = iota((LANES, LANES), 1)
    mass_cols = []
    for block in range(members):
        key_col = slot_table[:, block * LANES : (block + 1) * LANES].T[:, 3:4]
        matched = key_col == iota((LANES, NPOSE), 1).astype(F32)
        amount = jnp.sum(jnp.where(matched, mass_total[0:1, :], 0.0), axis=1, keepdims=True)
        first = amount.astype(BF16).astype(F32)
        second = (amount - first).astype(BF16).astype(F32)
        third = amount - first - second
        mass_cols.append(
            jnp.where(lanes == 0, first, jnp.where(lanes == 1, second, jnp.where(lanes == 2, third, 0.0))).astype(BF16)
        )
    mass_table = jnp.concatenate(mass_cols, axis=0)

    def mass_step(index):
        at = rows_at(index * LANES, LANES)
        mass = jnp.sum(dot(weave[at, :], mass_table), axis=1, keepdims=True)
        inverse[at, :] = jnp.broadcast_to(1.0 / (mass + RIDGE), (LANES, LANES))

    each(voxels // LANES, mass_step)
    load[7].wait()
    load[8].wait()
    slab_arrivals(3, returned)

    gathered = jnp.concatenate([returned[block].astype(F32) for block in range(slabs)], axis=0).astype(BF16)
    turned = dot(gathered, columns_v[...])
    for block in range(members):
        crossing[block] = turned[:, block * LANES : (block + 1) * LANES].astype(BF16)

    def cross_copy(step):
        peer = img_peer(step)
        return img_copy(32 + step, crossing.at[peer], crossed.at[member], peer)

    def cross_arrival(step):
        peer = img_peer(members - step)
        return img_copy(32 + step, crossed.at[peer], crossed.at[peer], peer)

    for step in range(1, members):
        cross_copy(step).start()
    crossed[member] = crossing[member]

    for step in range(1, slabs):
        slab_copy(0, outgoing, incoming, step).wait_send()
        slab_copy(1, picks, picks_in, step).wait_send()
        share_copy(step).wait_send()
        slab_copy(3, returning, returned, step).wait_send()
    for copy in gathers + ring_copies:
        copy.wait_send()
    each(stripes, lambda index: away_copy(index).wait_send())
    for step in range(1, members):
        mass_copy(step).wait_send()
    for step in range(1, members):
        cross_arrival(step).wait_recv()

    voxel_rows = dot(weave[...], crossed[...].reshape(members * LANES, LANES)) * inverse[...]
    fourier = voxel_rows.astype(BF16)
    edge = density.shape[2]
    columns_out = density.shape[1]
    for plane in range(density.shape[0]):
        field = fourier[plane * edge : (plane + 1) * edge]
        real = dot(rows_v[:, :edge], field)
        imag = dot(rows_v[:, edge:], field)
        density[plane] = (real[:, :columns_out] + imag[:, columns_out:]).T
    for step in range(1, members):
        cross_copy(step).wait_send()


def per_device(images, volume, precision, candidates, slot_key, slot_voxel, slot_weight):
    members = lax.axis_size("img")
    slabs = lax.axis_size("slab")
    planes, edge, width = volume.shape
    particles, cands = candidates.shape
    cap = slot_key.shape[2]
    deep = cap // members
    share = NPOSE // members
    voxels = planes * edge
    mine = slabs * deep
    side = NPOSE // 2
    big = pl.BlockSpec(memory_space=pl.ANY)
    near = pl.BlockSpec(memory_space=pltpu.VMEM)
    scratch = [
        pltpu.VMEM((particles, width), BF16),
        pltpu.VMEM((voxels, width), BF16),
        pltpu.VMEM((width, width), BF16),
        pltpu.VMEM((edge, 2 * edge), BF16),
        pltpu.VMEM((1, particles), F32),
        pltpu.VMEM((cands, particles), jnp.int32),
        pltpu.VMEM(slot_key.shape, jnp.int32),
        pltpu.VMEM(slot_key.shape, jnp.int32),
        pltpu.VMEM(slot_key.shape, jnp.int32),
        pltpu.VMEM((8, slabs * cap), F32),
        pltpu.VMEM((8, mine), F32),
        pltpu.VMEM((8, NPOSE), jnp.int32),
        pltpu.VMEM((slabs, deep, width), BF16),
        pltpu.VMEM((slabs, deep, width), BF16),
        pltpu.VMEM((NPOSE, width), BF16),
        pltpu.VMEM((NPOSE, LANES), F32),
        pltpu.VMEM((voxels, slabs * cap), BF16),
        pltpu.VMEM((slabs, cands, LANES), F32),
        pltpu.VMEM((slabs, cands, LANES), F32),
        pltpu.VMEM((slabs, cands, LANES), F32),
        pltpu.VMEM((NPOSE, particles), BF16),
        pltpu.VMEM((NPOSE, LANES), F32),
        pltpu.VMEM((side, width), BF16),
        pltpu.VMEM((side, width), BF16),
        pltpu.VMEM((side, width), F32),
        pltpu.VMEM((share, width), BF16),
        pltpu.VMEM((share, width), BF16),
        pltpu.VMEM((2, share, width), BF16),
        pltpu.VMEM((2, share, width), BF16),
        pltpu.VMEM((members, 8, NPOSE), F32),
        pltpu.VMEM((voxels, LANES), F32),
        pltpu.VMEM((slabs, deep, width), BF16),
        pltpu.VMEM((slabs, deep, width), BF16),
        pltpu.VMEM((members, mine, LANES), BF16),
        pltpu.VMEM((members, mine, LANES), BF16),
        pltpu.SemaphoreType.DMA((9,)),
        pltpu.SemaphoreType.DMA((4, slabs)),
        pltpu.SemaphoreType.DMA((4, slabs)),
        pltpu.SemaphoreType.DMA((40,)),
        pltpu.SemaphoreType.DMA((40,)),
    ]
    density, posterior = pl.pallas_call(
        functools.partial(kernel, slabs, members),
        out_shape=(
            jax.ShapeDtypeStruct((planes, edge // members, edge), F32),
            jax.ShapeDtypeStruct((cands, particles), F32),
        ),
        in_specs=[big] * 9,
        out_specs=(near, near),
        scratch_shapes=scratch,
        compiler_params=pltpu.CompilerParams(
            collective_id=0, has_side_effects=True, vmem_limit_bytes=56 * 1024 * 1024
        ),
    )(
        images, volume.reshape(voxels, width), column_table(edge, members), row_table(edge),
        precision[None, :], candidates.T, slot_key, slot_voxel, slot_weight,
    )
    return density.transpose(0, 2, 1), posterior.T


def solution(mesh):
    placed = (P("img", "slab"), P("slab", None, None), P("img"), P("img", None), P(), P(), P())
    return jax.shard_map(
        per_device,
        mesh=mesh,
        in_specs=placed,
        out_specs=(P("slab", None, "img"), P("img", None)),
        check_vma=False,
    )
```

time: 240 us -> 73.1 us (0.30)
  waiting for transfers between devices: 101 us -> 0 us
  Pallas kernels: 0 us -> 69 us
  other arithmetic: 38.9 us -> 0 us
  blocking collectives: 34.4 us -> 0 us
  matrix products: 27.4 us -> 0 us
  starting transfers between devices: 17.6 us -> 0 us
  between operations: 14.3 us -> 0.64 us
  local copies, waits for them, and re-layouts: 6.05 us -> 3.24 us
    psum x1 -> x0, waiting for transfers between devices: 80.5 us -> none  [per_device(): picked = lax.psum(picked, 'slab') * precision[None, :]]
    pallas_call x0 -> x1, Pallas kernels: none -> 69 us  [per_device(): pl.pallas_call(functools.partial(kernel, slabs, members), out_shape=(jax....]
    reduce_sum x11 -> x0, other arithmetic: 34.6 us -> none  [the longest x1 14.8 us: per_device(): row_weight = jnp.sum(spread.astype(jnp.float32), axis=1)]
    dot_general x8 -> x0, matrix products: 27.4 us -> none  [the longest x1 14.3 us: per_device(): lax.dot_general(slices, images, (((1,), (1,)), ((), ())), preferred_eleme...]
    all_to_all x1 -> x0, blocking collectives: 21.3 us -> none  [per_device(): lax.all_to_all(back.reshape(members, share, width), 'img', 0, 0, tiled=True)]
    all_to_all x3 -> x0, starting transfers between devices: 17.5 us -> none  [the longest x1 8.6 us: per_device(): lax.all_to_all(outgoing.reshape(slabs, deep, width), 'slab', 0, 0, tiled=...]
    psum x1 -> x0, blocking collectives: 13.1 us -> none  [per_device(): pose_weight = lax.psum(pose_weight, 'img')]
    all_to_all x3 -> x0, waiting for transfers between devices: 10.6 us -> none  [the longest x1 5.47 us: per_device(): lax.all_to_all(turned, 'img', 0, 0, tiled=True)]
  transfers between devices with their start and end apart: 5 -> 0, of which waited for: 4 -> 0; matrix products, arithmetic and copies ran while one was open for 7% -> 0% of each run, Pallas kernels for 0% -> 0%
where the time goes in v2:
time: 73.1 us; the launch traced here: 72.9 us
  Pallas kernels  69 us (94%)
  local copies, waits for them, and re-layouts  3.24 us (4%)
    pallas_call x1, Pallas kernels, per_device(): pl.pallas_call(functools.partial(kernel, slabs, members), out_shape=(jax....  69 us
    unnamed x2, local copies, waits for them, and re-layouts  3.24 us

profile of v2, /device:TPU:1, one launch (start us, length us, event | category | flops | bytes accessed | tf_op | source)
XLA Modules:
  0.0 72.9 jit_solution(14724567367491153922)
XLA Ops:
  0.6 69.0 %shard_map.104 = (f32[2,64,512]{2,1,0:T(8,128)}, f32[16,2048]{1,0:T(8,128)}) custom-call(bf16[2048,1024]{1,0:T(8,128)(2,1)} %images.1, bf16[1024,1024]{1,0:T(8,128)(2,1)} %bitcast.5, bf16[1024,1024]{1,0:T(8,128)(2,1)} %constant.4.clone.columns, bf16[512,1024]{1,0:T(8,128)(2,1)} %constant.5.clone.rows, f32[1,2048]{1,0:T(1,128)} %bitcast.9, ...), custom_call_target="tpu_custom_call" | custom-call | tf_op jit(solution)/shard_map/pallas_call | solution.py:611
  69.7 1.7 %copy.13 = f32[2,512,64]{1,2,0:T(8,128)} copy(f32[2,512,64]{1,2,0:T(8,128)} %bitcast.6) | data formatting | bytes 524288
  71.3 1.6 %copy.14 = f32[2048,16]{0,1:T(8,128)} copy(f32[2048,16]{0,1:T(8,128)} %bitcast.8) | data formatting | bytes 262144

commit v3 on v2

--- a/solution.py
+++ b/solution.py
@@ -136,32 +136,36 @@
         before += jnp.where(keys[slab] >= 0, 1.0, 0.0) * jnp.where(own > slab, 1.0, 0.0)
     out_start = jnp.sum(before, axis=1, keepdims=True)
     total_slots = slabs * cap
-    position = iota((1, total_slots), 1)
-    block_sel = iota((slabs, total_slots), 0) == ((position >> 3) & (slabs - 1))
-    start_row = pick_row(block_sel, out_start).astype(jnp.int32)
-    slot_row = members * (position & 7) + (((position >> 7) - start_row) & 7)
-    slot_sel = iota((cap, total_slots), 0) == slot_row
     own_key = keys[own]
     own_code = voxel_of[own] * 32 + jnp.where(own_key >= 0, weight_of[own], 31)
-    chooser = jnp.where(block_sel, 1.0, 0.0)
-
-    def ordered(table):
-        wide = lax.dot_general(
-            table.astype(F32), chooser, (((0,), (0,)), ((), ())),
-            precision=lax.Precision.HIGHEST, preferred_element_type=F32,
-        )
-        return pick_row(slot_sel, wide)
-
-    code_row = ordered(own_code).astype(jnp.int32)
-    level = code_row & 31
-    alive = level <= WSTEPS
-    slot_table[0:1, :] = (code_row >> 5).astype(F32)
-    slot_table[1:2, :] = jnp.where(alive, level, 0).astype(F32) * (1.0 / WSTEPS)
-    slot_table[2:3, :] = jnp.where(alive, WSTEPS - level, 0).astype(F32) * (1.0 / WSTEPS)
-    slot_table[3:4, :] = ordered(own_key)
-    slot_table[4:8, :] = jnp.zeros((4, total_slots), F32)
-
-    own_cols = slot_table[:, rows_at(member * mine, mine)].T
+
+    def ordered(first, count, tables):
+        position = iota((1, count), 1) + first
+        block_sel = iota((slabs, count), 0) == ((position >> 3) & (slabs - 1))
+        start_row = pick_row(block_sel, out_start).astype(jnp.int32)
+        slot_row = members * (position & 7) + (((position >> 7) - start_row) & 7)
+        slot_sel = iota((cap, count), 0) == slot_row
+        chooser = jnp.where(block_sel, 1.0, 0.0)
+        found = []
+        for table in tables:
+            wide = lax.dot_general(
+                table.astype(F32), chooser, (((0,), (0,)), ((), ())),
+                precision=lax.Precision.HIGHEST, preferred_element_type=F32,
+            )
+            found.append(pick_row(slot_sel, wide))
+        return found
+
+    def decoded(code):
+        code_row = code.astype(jnp.int32)
+        level = code_row & 31
+        alive = level <= WSTEPS
+        spot = (code_row >> 5).astype(F32)
+        lower = jnp.where(alive, level, 0).astype(F32) * (1.0 / WSTEPS)
+        upper = jnp.where(alive, WSTEPS - level, 0).astype(F32) * (1.0 / WSTEPS)
+        return spot, lower, upper
+
+    parts = decoded(ordered(member * mine, mine, [own_code])[0])
+    own_cols = jnp.concatenate(list(parts) + [jnp.zeros((5, mine), F32)], axis=0).T
     place = iota((mine, voxels), 1)
     spot = own_cols[:, 0:1].astype(jnp.int32)
     take = jnp.where(place == spot, own_cols[:, 1:2], 0.0) + jnp.where(place == spot + 1, own_cols[:, 2:3], 0.0)
@@ -198,6 +202,11 @@
 
     slab_exchange(0, outgoing, incoming)
     incoming[own] = outgoing[own]
+
+    code, key_row = ordered(0, total_slots, [own_code, own_key])
+    for index, value in enumerate(decoded(code) + (key_row,)):
+        slot_table[index : index + 1, :] = value
+    slot_table[4:8, :] = jnp.zeros((4, total_slots), F32)
 
     in_key = jnp.concatenate(
         [jnp.sum(jnp.where(iota((slabs, cap), 0) == own, keys[slab], 0), axis=0, keepdims=True) for slab in range(slabs)],
@@ -389,16 +398,15 @@
 
     def spread_chunk(block):
         at = rows_at(block * LANES, LANES)
-        amount = shares[block] * precision[:, at]
-        number = poses[:, at]
+        amount = (shares[block] * precision[:, at]).astype(BF16)
+        number = poses[:, at].astype(jnp.int16)
         for first in range(0, NPOSE, tile):
-            row = iota((tile, LANES), 0) + first
-            value = jnp.zeros((tile, LANES), F32)
+            row = (iota((tile, LANES), 0) + first).astype(jnp.int16)
+            value = jnp.zeros((tile, LANES), BF16)
             for k in range(cands):
                 value = jnp.where(number[k : k + 1] == row, amount[k : k + 1], value)
-            rounded = value.astype(BF16)
-            spread[first : first + tile, at] = rounded
-            row_weight[first : first + tile, :] += rounded.astype(F32)
+            spread[first : first + tile, at] = value
+            row_weight[first : first + tile, :] += value.astype(F32)
 
     def spread_step(step):
         slab_arrival(2, shares, step).wait_recv()
@@ -408,51 +416,87 @@
     each(slabs, spread_step, 1)
 
     stripe = 2 * LANES
-    stripes = width // stripe
+    halves = 2
+    wide = width // halves
+    per_half = wide // stripe
 
     def away_copy(index):
-        at = rows_at(index * stripe, stripe)
-        return img_copy(24 + index, away.at[:, at], away_in.at[:, at], partner)
-
-    def away_step(index):
-        at = rows_at(index * stripe, stripe)
-        away[:, at] = dot(spread[side : 2 * side, :], images_v[:, at]).astype(BF16)
+        at = slice(index * stripe, (index + 1) * stripe)
+        return img_copy(40 + index, away.at[:, at], away_in.at[:, at], partner)
+
+    def back_stripe(index):
+        at = slice(index * stripe, (index + 1) * stripe)
+        part = dot(spread[...], images_v[:, at])
+        away[:, at] = part[side:].astype(BF16)
         away_copy(index).start()
-
-    def kept_step(index):
-        at = rows_at(index * stripe, stripe)
-        kept[:, at] = dot(spread[0:side, :], images_v[:, at])
-
-    each(stripes, away_step)
-    each(stripes, kept_step)
-    each(stripes, lambda index: away_copy(index).wait_recv())
-
-    def kept_part(index, first=0, size=share):
+        kept[:, at] = part[:side]
+
+    def columns_of(part):
+        return slice(part * wide, (part + 1) * wide)
+
+    def kept_part(index, part, first=0, size=share):
         here = index * share + first
         there = (ring_len - 1 - index) * share + first
-        return kept[here : here + size, :] + away_in[there : there + size, :].astype(F32)
-
-    opposite[...] = kept_part(FAR).astype(BF16)
-    ring_copies = [
-        img_copy(11, opposite.at[0:half], opposite_in.at[0:half], right),
-        img_copy(12, opposite.at[half:share], opposite_in.at[half:share], left),
-        img_copy(13, ring.at[0, half:share], ring_in.at[0, half:share], right),
-        img_copy(14, ring.at[1, 0:half], ring_in.at[1, 0:half], left),
-        img_copy(15, ring.at[0, 0:half], ring_in.at[0, 0:half], right),
-        img_copy(28, ring.at[1, half:share], ring_in.at[1, half:share], left),
-    ]
-    ring_copies[0].start()
-    ring_copies[1].start()
-    ring[0, half:share] = kept_part(RIGHT, half, half).astype(BF16)
-    ring_copies[2].start()
-    ring[1, 0:half] = kept_part(LEFT, 0, half).astype(BF16)
-    ring_copies[3].start()
-    ring_copies[0].wait_recv()
-    ring[0, 0:half] = (kept_part(RIGHT, 0, half) + opposite_in[0:half, :].astype(F32)).astype(BF16)
-    ring_copies[4].start()
-    ring_copies[1].wait_recv()
-    ring[1, half:share] = (kept_part(LEFT, half, half) + opposite_in[half:share, :].astype(F32)).astype(BF16)
-    ring_copies[5].start()
+        at = columns_of(part)
+        return kept[here : here + size, at] + away_in[there : there + size, at].astype(F32)
+
+    def ring_copy(part, index):
+        at = columns_of(part)
+        low, high = slice(0, half), slice(half, share)
+        refs = [
+            (opposite.at[low, at], opposite_in.at[low, at], right),
+            (opposite.at[high, at], opposite_in.at[high, at], left),
+            (ring.at[0, high, at], ring_in.at[0, high, at], right),
+            (ring.at[1, low, at], ring_in.at[1, low, at], left),
+            (ring.at[0, low, at], ring_in.at[0, low, at], right),
+            (ring.at[1, high, at], ring_in.at[1, high, at], left),
+        ]
+        return img_copy(48 + 6 * part + index, *refs[index])
+
+    def ring_start(part):
+        at = columns_of(part)
+        for index in range(part * per_half, (part + 1) * per_half):
+            away_copy(index).wait_recv()
+        opposite[:, at] = kept_part(FAR, part).astype(BF16)
+        ring_copy(part, 0).start()
+        ring_copy(part, 1).start()
+        ring[0, half:share, at] = kept_part(RIGHT, part, half, half).astype(BF16)
+        ring_copy(part, 2).start()
+        ring[1, 0:half, at] = kept_part(LEFT, part, 0, half).astype(BF16)
+        ring_copy(part, 3).start()
+
+    def ring_relay(part):
+        at = columns_of(part)
+        ring_copy(part, 0).wait_recv()
+        ring[0, 0:half, at] = (kept_part(RIGHT, part, 0, half) + opposite_in[0:half, at].astype(F32)).astype(BF16)
+        ring_copy(part, 4).start()
+        ring_copy(part, 1).wait_recv()
+        ring[1, half:share, at] = (
+            kept_part(LEFT, part, half, half) + opposite_in[half:share, at].astype(F32)
+        ).astype(BF16)
+        ring_copy(part, 5).start()
+
+    unpack = jnp.where(pack_table[...].T[:, 0:1] == iota((mine, share), 1).astype(F32), 1.0, 0.0).astype(BF16)
+
+    def ring_finish(part):
+        at = columns_of(part)
+        held = kept_part(HOME, part)
+        for index in range(2, 6):
+            ring_copy(part, index).wait_recv()
+        summed = (held + ring_in[0, :, at].astype(F32) + ring_in[1, :, at].astype(F32)).astype(BF16)
+        unpacked = dot(unpack, summed)
+        for block in range(slabs):
+            returning[part, block] = unpacked[block * deep : (block + 1) * deep].astype(BF16)
+        slab_exchange(3 + part, returning.at[part], returned.at[part])
+        returned[part, own] = returning[part, own]
+
+    back_stripe(0)
+    back_stripe(1)
+    back_stripe(2)
+    ring_start(0)
+    back_stripe(3)
+    ring_relay(0)
+    ring_start(1)
 
     weight = jnp.sum(row_weight[...], axis=1, keepdims=True)
     mass_row = pick_row(iota((NPOSE, NPOSE), 0) == pose_row[0:1, :], weight)
@@ -467,19 +511,11 @@
 
     for step in range(1, members):
         mass_copy(step).start()
+    ring_relay(1)
+    ring_finish(0)
+    ring_finish(1)
     for block in range(slabs):
         posterior[:, block * LANES : (block + 1) * LANES] = shares[block]
-    held = kept_part(HOME)
-    for index in range(2, 6):
-        ring_copies[index].wait_recv()
-    summed = (held + ring_in[0].astype(F32) + ring_in[1].astype(F32)).astype(BF16)
-
-    unpack = jnp.where(pack_table[...].T[:, 0:1] == iota((mine, share), 1).astype(F32), 1.0, 0.0).astype(BF16)
-    unpacked = dot(unpack, summed)
-    for block in range(slabs):
-        returning[block] = unpacked[block * deep : (block + 1) * deep].astype(BF16)
-    slab_exchange(3, returning, returned)
-    returned[own] = returning[own]
 
     for step in range(1, members):
         mass_arrival(step).wait_recv()
@@ -508,10 +544,12 @@
     each(voxels // LANES, mass_step)
     load[7].wait()
     load[8].wait()
-    slab_arrivals(3, returned)
-
-    gathered = jnp.concatenate([returned[block].astype(F32) for block in range(slabs)], axis=0).astype(BF16)
-    turned = dot(gathered, columns_v[...])
+
+    turned = jnp.zeros((mine, width), F32)
+    for part in range(halves):
+        slab_arrivals(3 + part, returned.at[part])
+        gathered = jnp.concatenate([returned[part, block].astype(F32) for block in range(slabs)], axis=0)
+        turned += dot(gathered.astype(BF16), columns_v[columns_of(part), :])
     for block in range(members):
         crossing[block] = turned[:, block * LANES : (block + 1) * LANES].astype(BF16)
 
@@ -531,10 +569,15 @@
         slab_copy(0, outgoing, incoming, step).wait_send()
         slab_copy(1, picks, picks_in, step).wait_send()
         share_copy(step).wait_send()
-        slab_copy(3, returning, returned, step).wait_send()
-    for copy in gathers + ring_copies:
+        for part in range(halves):
+            slab_copy(3 + part, returning.at[part], returned.at[part], step).wait_send()
+    for copy in gathers:
         copy.wait_send()
-    each(stripes, lambda index: away_copy(index).wait_send())
+    for index in range(halves * per_half):
+        away_copy(index).wait_send()
+    for part in range(halves):
+        for index in range(6):
+            ring_copy(part, index).wait_send()
     for step in range(1, members):
         mass_copy(step).wait_send()
     for step in range(1, members):
@@ -598,15 +641,15 @@
         pltpu.VMEM((2, share, width), BF16),
         pltpu.VMEM((members, 8, NPOSE), F32),
         pltpu.VMEM((voxels, LANES), F32),
-        pltpu.VMEM((slabs, deep, width), BF16),
-        pltpu.VMEM((slabs, deep, width), BF16),
+        pltpu.VMEM((2, slabs, deep, width // 2), BF16),
+        pltpu.VMEM((2, slabs, deep, width // 2), BF16),
         pltpu.VMEM((members, mine, LANES), BF16),
         pltpu.VMEM((members, mine, LANES), BF16),
         pltpu.SemaphoreType.DMA((9,)),
-        pltpu.SemaphoreType.DMA((4, slabs)),
-        pltpu.SemaphoreType.DMA((4, slabs)),
-        pltpu.SemaphoreType.DMA((40,)),
-        pltpu.SemaphoreType.DMA((40,)),
+        pltpu.SemaphoreType.DMA((5, slabs)),
+        pltpu.SemaphoreType.DMA((5, slabs)),
+        pltpu.SemaphoreType.DMA((60,)),
+        pltpu.SemaphoreType.DMA((60,)),
     ]
     density, posterior = pl.pallas_call(
         functools.partial(kernel, slabs, members),

time: 73.1 us -> 72.6 us (level)
  no operation moved by 1% of the time
where the time goes in v3:
time: 72.6 us; the launch traced here: 72.4 us
  Pallas kernels  68.6 us (94%)
  local copies, waits for them, and re-layouts  3.24 us (4%)
    pallas_call x1, Pallas kernels, per_device(): pl.pallas_call(functools.partial(kernel, slabs, members), out_shape=(jax....  68.6 us
    unnamed x2, local copies, waits for them, and re-layouts  3.24 us

profile of v3, /device:TPU:1, one launch (start us, length us, event | category | flops | bytes accessed | tf_op | source)
XLA Modules:
  0.0 72.4 jit_solution(16071559283913169941)
XLA Ops:
  0.6 68.6 %shard_map.104 = (f32[2,64,512]{2,1,0:T(8,128)}, f32[16,2048]{1,0:T(8,128)}) custom-call(bf16[2048,1024]{1,0:T(8,128)(2,1)} %images.1, bf16[1024,1024]{1,0:T(8,128)(2,1)} %bitcast.5, bf16[1024,1024]{1,0:T(8,128)(2,1)} %constant.4.clone.columns, bf16[512,1024]{1,0:T(8,128)(2,1)} %constant.5.clone.rows, f32[1,2048]{1,0:T(1,128)} %bitcast.9, ...), custom_call_target="tpu_custom_call" | custom-call | tf_op jit(solution)/shard_map/pallas_call | solution.py:654
  69.2 1.7 %copy.13 = f32[2,512,64]{1,2,0:T(8,128)} copy(f32[2,512,64]{1,2,0:T(8,128)} %bitcast.6) | data formatting | bytes 524288
  70.9 1.6 %copy.14 = f32[2048,16]{0,1:T(8,128)} copy(f32[2048,16]{0,1:T(8,128)} %bitcast.8) | data formatting | bytes 262144

commit v4 on v3

--- a/solution.py
+++ b/solution.py
@@ -86,7 +86,7 @@
     images_v, volume_v, columns_v, rows_v, precision, poses, keys, voxel_of, weight_of,
     slot_table, pack_table, pose_row,
     outgoing, incoming, slices, half_power, weave,
-    picks, picks_in, shares, spread, row_weight,
+    picks, picks_in, shares, spread, row_weight, partial,
     away, away_in, kept, opposite, opposite_in, ring, ring_in,
     masses, inverse, returning, returned, crossing, crossed,
     loads, slab_send, slab_recv, img_send, img_recv,
@@ -177,25 +177,19 @@
         outgoing[block] = woven[block * deep : (block + 1) * deep].astype(BF16)
     pl.semaphore_wait(barrier, slabs - 1 + members - 1)
 
-    def slab_copy(stage, src, dst, step):
-        peer = slab_peer(step)
-        return remote(
-            src.at[peer], dst.at[own], slab_send.at[stage, step], slab_recv.at[stage, step], {"slab": peer}
-        )
-
-    def slab_arrival(stage, dst, step):
-        peer = slab_peer(slabs - step)
-        return remote(
-            dst.at[peer], dst.at[peer], slab_send.at[stage, step], slab_recv.at[stage, step], {"slab": peer}
-        )
+    def slab_copy(stage, src, dst, peer):
+        return remote(src.at[peer], dst.at[own], slab_send.at[stage], slab_recv.at[stage], {"slab": peer})
+
+    def slab_whole(stage, ref, count):
+        blocks = ref.at[0:count]
+        return remote(blocks, blocks, slab_send.at[stage], slab_recv.at[stage], {"slab": slab_peer(1)})
 
     def slab_exchange(stage, src, dst):
         for step in range(1, slabs):
-            slab_copy(stage, src, dst, step).start()
+            slab_copy(stage, src, dst, slab_peer(step)).start()
 
     def slab_arrivals(stage, dst):
-        for step in range(1, slabs):
-            slab_arrival(stage, dst, step).wait_recv()
+        slab_whole(stage, dst, slabs - 1).wait_recv()
 
     def img_copy(slot, src, dst, device):
         return remote(src, dst, img_send.at[slot], img_recv.at[slot], {"img": device})
@@ -362,20 +356,17 @@
         table = jnp.concatenate([slices[0:share, :], slices[NPOSE - share : NPOSE, :]], axis=0)
         score_chunk(index, table, [(0, 0, share), (NPOSE - share, share, share)], True)
 
-    def pick_copy(peer):
-        step = lax.rem(peer - own + slabs, slabs)
-        return slab_copy(1, picks, picks_in, step)
-
-    def far_step(turn):
-        index = lax.rem(own // 2 + turn, chunks)
+    def pick_send(peer):
+        @pl.when(peer != own)
+        def _():
+            slab_copy(1, picks, picks_in, peer).start()
+
+    def far_step(index):
         far_chunk(index)
-        pick_copy(2 * index).start()
-        pick_copy(2 * index + 1).start()
-
-    each(chunks, far_step, 1)
-    far_chunk(own // 2)
-    sibling = own + 1 - 2 * lax.rem(own, 2)
-    pick_copy(sibling).start()
+        pick_send(2 * index)
+        pick_send(2 * index + 1)
+
+    each(chunks, far_step)
     picks_in[own] = picks[own]
     load[6].wait()
     row_weight[...] = jnp.zeros_like(row_weight)
@@ -386,14 +377,22 @@
     total = total * precision[:, rows_at(own * LANES, LANES)]
     exponent = jnp.exp(total - jnp.max(total, axis=0, keepdims=True))
     shares[own] = exponent / jnp.sum(exponent, axis=0, keepdims=True)
-
-    def share_copy(step):
-        return remote(
-            shares.at[own], shares.at[own], slab_send.at[2, step], slab_recv.at[2, step], {"slab": slab_peer(step)}
-        )
-
+    ahead_of = slabs // 2
+    turn = own // ahead_of
     for step in range(1, slabs):
-        share_copy(step).start()
+        remote(
+            shares.at[own], shares.at[own], slab_send.at[2], slab_recv.at[5 + turn], {"slab": slab_peer(step)}
+        ).start()
+
+    def shares_arrive(which):
+        @pl.when(turn == which)
+        def _():
+            slab_whole(5 + which, shares, ahead_of - 1).wait_recv()
+
+        @pl.when(turn != which)
+        def _():
+            slab_whole(5 + which, shares, ahead_of).wait_recv()
+
     tile = LANES
 
     def spread_chunk(block):
@@ -408,13 +407,6 @@
             spread[first : first + tile, at] = value
             row_weight[first : first + tile, :] += value.astype(F32)
 
-    def spread_step(step):
-        slab_arrival(2, shares, step).wait_recv()
-        spread_chunk(slab_peer(slabs - step))
-
-    spread_chunk(own)
-    each(slabs, spread_step, 1)
-
     stripe = 2 * LANES
     halves = 2
     wide = width // halves
@@ -426,7 +418,7 @@
 
     def back_stripe(index):
         at = slice(index * stripe, (index + 1) * stripe)
-        part = dot(spread[...], images_v[:, at])
+        part = partial[:, at] + dot(spread[:, early:], images_v[early:, at])
         away[:, at] = part[side:].astype(BF16)
         away_copy(index).start()
         kept[:, at] = part[:side]
@@ -490,6 +482,17 @@
         slab_exchange(3 + part, returning.at[part], returned.at[part])
         returned[part, own] = returning[part, own]
 
+    early = images_v.shape[0] // 2
+
+    def early_stripe(index):
+        at = rows_at(index * stripe, stripe)
+        partial[:, at] = dot(spread[:, :early], images_v[:early, at])
+
+    shares_arrive(0)
+    each(ahead_of, spread_chunk)
+    each(width // stripe, early_stripe)
+    shares_arrive(1)
+    each(slabs, spread_chunk, ahead_of)
     back_stripe(0)
     back_stripe(1)
     back_stripe(2)
@@ -503,11 +506,11 @@
     masses[member] = jnp.broadcast_to(mass_row, (8, NPOSE))
 
     def mass_copy(step):
-        return img_copy(16 + step, masses.at[member], masses.at[member], img_peer(step))
-
-    def mass_arrival(step):
-        peer = img_peer(members - step)
-        return img_copy(16 + step, masses.at[peer], masses.at[peer], peer)
+        return img_copy(16, masses.at[member], masses.at[member], img_peer(step))
+
+    def img_whole(slot, ref):
+        blocks = ref.at[0 : members - 1]
+        return img_copy(slot, blocks, blocks, img_peer(1))
 
     for step in range(1, members):
         mass_copy(step).start()
@@ -517,8 +520,7 @@
     for block in range(slabs):
         posterior[:, block * LANES : (block + 1) * LANES] = shares[block]
 
-    for step in range(1, members):
-        mass_arrival(step).wait_recv()
+    img_whole(16, masses).wait_recv()
     mass_total = masses[0]
     for index in range(1, members):
         mass_total = mass_total + masses[index]
@@ -555,22 +557,14 @@
 
     def cross_copy(step):
         peer = img_peer(step)
-        return img_copy(32 + step, crossing.at[peer], crossed.at[member], peer)
-
-    def cross_arrival(step):
-        peer = img_peer(members - step)
-        return img_copy(32 + step, crossed.at[peer], crossed.at[peer], peer)
+        return img_copy(17, crossing.at[peer], crossed.at[member], peer)
 
     for step in range(1, members):
         cross_copy(step).start()
     crossed[member] = crossing[member]
 
-    for step in range(1, slabs):
-        slab_copy(0, outgoing, incoming, step).wait_send()
-        slab_copy(1, picks, picks_in, step).wait_send()
-        share_copy(step).wait_send()
-        for part in range(halves):
-            slab_copy(3 + part, returning.at[part], returned.at[part], step).wait_send()
+    for stage, ref in ((0, outgoing), (1, picks), (2, shares), (3, returning.at[0]), (4, returning.at[1])):
+        slab_whole(stage, ref, slabs - 1).wait_send()
     for copy in gathers:
         copy.wait_send()
     for index in range(halves * per_half):
@@ -578,10 +572,8 @@
     for part in range(halves):
         for index in range(6):
             ring_copy(part, index).wait_send()
-    for step in range(1, members):
-        mass_copy(step).wait_send()
-    for step in range(1, members):
-        cross_arrival(step).wait_recv()
+    img_whole(16, masses).wait_send()
+    img_whole(17, crossed).wait_recv()
 
     voxel_rows = dot(weave[...], crossed[...].reshape(members * LANES, LANES)) * inverse[...]
     fourier = voxel_rows.astype(BF16)
@@ -592,8 +584,7 @@
         real = dot(rows_v[:, :edge], field)
         imag = dot(rows_v[:, edge:], field)
         density[plane] = (real[:, :columns_out] + imag[:, columns_out:]).T
-    for step in range(1, members):
-        cross_copy(step).wait_send()
+    img_whole(17, crossing).wait_send()
 
 
 def per_device(images, volume, precision, candidates, slot_key, slot_voxel, slot_weight):
@@ -632,6 +623,7 @@
         pltpu.VMEM((slabs, cands, LANES), F32),
         pltpu.VMEM((NPOSE, particles), BF16),
         pltpu.VMEM((NPOSE, LANES), F32),
+        pltpu.VMEM((NPOSE, width), F32),
         pltpu.VMEM((side, width), BF16),
         pltpu.VMEM((side, width), BF16),
         pltpu.VMEM((side, width), F32),
@@ -646,8 +638,8 @@
         pltpu.VMEM((members, mine, LANES), BF16),
         pltpu.VMEM((members, mine, LANES), BF16),
         pltpu.SemaphoreType.DMA((9,)),
-        pltpu.SemaphoreType.DMA((5, slabs)),
-        pltpu.SemaphoreType.DMA((5, slabs)),
+        pltpu.SemaphoreType.DMA((7,)),
+        pltpu.SemaphoreType.DMA((7,)),
         pltpu.SemaphoreType.DMA((60,)),
         pltpu.SemaphoreType.DMA((60,)),
     ]

time: 72.6 us -> 73.3 us (level)
  no operation moved by 1% of the time
where the time goes in v4:
time: 73.3 us; the launch traced here: 73.1 us
  Pallas kernels  69.2 us (94%)
  local copies, waits for them, and re-layouts  3.24 us (4%)
    pallas_call x1, Pallas kernels, per_device(): pl.pallas_call(functools.partial(kernel, slabs, members), out_shape=(jax....  69.2 us
    unnamed x2, local copies, waits for them, and re-layouts  3.24 us

profile of v4, /device:TPU:1, one launch (start us, length us, event | category | flops | bytes accessed | tf_op | source)
XLA Modules:
  0.0 73.1 jit_solution(12479767483871963358)
XLA Ops:
  0.6 69.2 %shard_map.104 = (f32[2,64,512]{2,1,0:T(8,128)}, f32[16,2048]{1,0:T(8,128)}) custom-call(bf16[2048,1024]{1,0:T(8,128)(2,1)} %images.1, bf16[1024,1024]{1,0:T(8,128)(2,1)} %bitcast.5, bf16[1024,1024]{1,0:T(8,128)(2,1)} %constant.4.clone.columns, bf16[512,1024]{1,0:T(8,128)(2,1)} %constant.5.clone.rows, f32[1,2048]{1,0:T(1,128)} %bitcast.9, ...), custom_call_target="tpu_custom_call" | custom-call | tf_op jit(solution)/shard_map/pallas_call | solution.py:646
  69.9 1.7 %copy.13 = f32[2,512,64]{1,2,0:T(8,128)} copy(f32[2,512,64]{1,2,0:T(8,128)} %bitcast.6) | data formatting | bytes 524288
  71.6 1.6 %copy.14 = f32[2048,16]{0,1:T(8,128)} copy(f32[2048,16]{0,1:T(8,128)} %bitcast.8) | data formatting | bytes 262144

commit v5 on v4

--- a/solution.py
+++ b/solution.py
@@ -85,7 +85,7 @@
     density, posterior,
     images_v, volume_v, columns_v, rows_v, precision, poses, keys, voxel_of, weight_of,
     slot_table, pack_table, pose_row,
-    outgoing, incoming, slices, half_power, weave,
+    outgoing, incoming, slices, half_power, scores, weave,
     picks, picks_in, shares, spread, row_weight, partial,
     away, away_in, kept, opposite, opposite_in, ring, ring_in,
     masses, inverse, returning, returned, crossing, crossed,
@@ -98,12 +98,14 @@
     share = NPOSE // members
     half = share // 2
     side = ring_len * share
-    deep = outgoing.shape[1]
+    deep = outgoing.shape[2]
     mine = slabs * deep
     cap = keys.shape[2]
     width = volume_v.shape[1]
     voxels = volume_v.shape[0]
     cands = poses.shape[0]
+    halves = 2
+    wide = width // halves
     right = 2 * lax.rem(chip + 1, ring_len) + core
     left = 2 * lax.rem(chip + ring_len - 1, ring_len) + core
     partner = 2 * chip + 1 - core
@@ -172,11 +174,6 @@
     load[3].wait()
     for index in range(5, len(load)):
         load[index].start()
-    woven = dot(take.astype(BF16), volume_v[...])
-    for block in range(slabs):
-        outgoing[block] = woven[block * deep : (block + 1) * deep].astype(BF16)
-    pl.semaphore_wait(barrier, slabs - 1 + members - 1)
-
     def slab_copy(stage, src, dst, peer):
         return remote(src.at[peer], dst.at[own], slab_send.at[stage], slab_recv.at[stage], {"slab": peer})
 
@@ -191,11 +188,22 @@
     def slab_arrivals(stage, dst):
         slab_whole(stage, dst, slabs - 1).wait_recv()
 
+    def columns_of(part):
+        return slice(part * wide, (part + 1) * wide)
+
     def img_copy(slot, src, dst, device):
         return remote(src, dst, img_send.at[slot], img_recv.at[slot], {"img": device})
 
-    slab_exchange(0, outgoing, incoming)
-    incoming[own] = outgoing[own]
+    woven_by = take.astype(BF16)
+    first_stage = [0, 7]
+    for part in range(halves):
+        woven = dot(woven_by, volume_v[:, columns_of(part)])
+        for block in range(slabs):
+            outgoing[part, block] = woven[block * deep : (block + 1) * deep].astype(BF16)
+        if part == 0:
+            pl.semaphore_wait(barrier, slabs - 1 + members - 1)
+        slab_exchange(first_stage[part], outgoing.at[part], incoming.at[part])
+        incoming[part, own] = outgoing[part, own]
 
     code, key_row = ordered(0, total_slots, [own_code, own_key])
     for index, value in enumerate(decoded(code) + (key_row,)):
@@ -243,40 +251,60 @@
                 renamed = jnp.where(high == piece, found, renamed)
             poses[at] = renamed
 
-    slab_arrivals(0, incoming)
-    arrived = jnp.concatenate([incoming[block].astype(F32) for block in range(slabs)], axis=0).astype(BF16)
     pack = jnp.where(iota((share, mine), 0).astype(F32) == pack_table[0:1, :], 1.0, 0.0).astype(BF16)
 
-    def block_of(index, first=0, size=share):
-        return slices.at[index * share + first : index * share + first + size]
-
     FAR, RIGHT, LEFT, HOME = 0, 1, 2, 3
-    slices[HOME * share : (HOME + 1) * share, :] = dot(pack, arrived).astype(BF16)
 
     def other(index):
         return members - 1 - index
 
-    def top(index):
-        return block_of(index, 0, half)
-
-    def bottom(index):
-        return block_of(index, half, half)
-
-    gathers = [
-        img_copy(0, top(HOME), top(LEFT), right),
-        img_copy(1, bottom(HOME), bottom(RIGHT), left),
-        img_copy(2, block_of(HOME), block_of(other(HOME)), partner),
-        img_copy(3, bottom(HOME), bottom(LEFT), right),
-        img_copy(4, top(HOME), top(RIGHT), left),
-        img_copy(5, top(LEFT), top(FAR), right),
-        img_copy(6, bottom(RIGHT), bottom(FAR), left),
-        img_copy(7, block_of(LEFT), block_of(other(LEFT)), partner),
-        img_copy(8, block_of(RIGHT), block_of(other(RIGHT)), partner),
-        img_copy(9, top(FAR), top(other(FAR)), partner),
-        img_copy(10, bottom(FAR), bottom(other(FAR)), partner),
-    ]
-    for index in range(5):
-        gathers[index].start()
+    def gather_copy(part, index):
+        at = columns_of(part)
+
+        def block_of(block, first=0, size=share):
+            return slices.at[block * share + first : block * share + first + size, at]
+
+        def top(block):
+            return block_of(block, 0, half)
+
+        def bottom(block):
+            return block_of(block, half, half)
+
+        refs = [
+            (top(HOME), top(LEFT), right),
+            (bottom(HOME), bottom(RIGHT), left),
+            (block_of(HOME), block_of(other(HOME)), partner),
+            (bottom(HOME), bottom(LEFT), right),
+            (top(HOME), top(RIGHT), left),
+            (top(LEFT), top(FAR), right),
+            (bottom(RIGHT), bottom(FAR), left),
+            (block_of(LEFT), block_of(other(LEFT)), partner),
+            (block_of(RIGHT), block_of(other(RIGHT)), partner),
+            (top(FAR), top(other(FAR)), partner),
+            (bottom(FAR), bottom(other(FAR)), partner),
+        ]
+        return img_copy(64 + 11 * part + index, *refs[index])
+
+    def gather_start(part):
+        slab_arrivals(first_stage[part], incoming.at[part])
+        arrived = jnp.concatenate([incoming[part, block].astype(F32) for block in range(slabs)], axis=0)
+        slices[HOME * share : (HOME + 1) * share, columns_of(part)] = dot(pack, arrived.astype(BF16)).astype(BF16)
+        for index in range(5):
+            gather_copy(part, index).start()
+
+    def gather_near(part):
+        for come, go in ((0, 5), (1, 6), (3, 7), (4, 8)):
+            gather_copy(part, come).wait_recv()
+            gather_copy(part, go).start()
+
+    def gather_far(part):
+        for come, go in ((5, 9), (6, 10)):
+            gather_copy(part, come).wait_recv()
+            gather_copy(part, go).start()
+
+    def gather_end(part):
+        for index in (2, 7, 8, 9, 10):
+            gather_copy(part, index).wait_recv()
 
     def weave_step(index):
         at = iota((LANES, total_slots), 0) + index * LANES
@@ -285,15 +313,32 @@
         weave[rows_at(index * LANES, LANES), :] = value.astype(BF16)
 
     each(voxels // LANES, weave_step)
-    gathers[0].wait_recv()
-    gathers[5].start()
-    gathers[1].wait_recv()
-    gathers[6].start()
-    gathers[3].wait_recv()
-    gathers[7].start()
-    gathers[4].wait_recv()
-    gathers[8].start()
+    gather_start(0)
+    gather_start(1)
+
+    gather_near(0)
+    gather_far(0)
+    gather_near(1)
     load[5].wait()
+    gather_end(0)
+
+    chunk = 2 * LANES
+    chunks = images_v.shape[0] // chunk
+
+    def score_of(index, part):
+        at = columns_of(part)
+        return lax.dot_general(
+            slices[:, at], images_v[rows_at(index * chunk, chunk), at],
+            (((1,), (1,)), ((), ())), preferred_element_type=F32,
+        )
+
+    def first_step(index):
+        scores[:, rows_at(index * chunk, chunk)] = score_of(index, 0)
+
+    each(chunks // 2, first_step)
+    gather_far(1)
+    each(chunks, first_step, chunks // 2)
+    gather_end(1)
 
     def power_step(index):
         at = rows_at(index * share, share)
@@ -301,75 +346,39 @@
         total = 0.5 * jnp.sum(values * values, axis=1, keepdims=True)
         half_power[at, :] = jnp.broadcast_to(total, (share, LANES))
 
-    chunk = 2 * LANES
-    chunks = images_v.shape[0] // chunk
-
-    def picks_of(score, pieces, numbers, value):
-        for first, offset, size in pieces:
-            block = score[offset : offset + size] - half_power[first : first + size, :]
-            for group in range(size // 8):
-                picked = jnp.take_along_axis(
-                    block[group * 8 : (group + 1) * 8], numbers[0], axis=0, mode="promise_in_bounds"
-                )
-                value[0] = jnp.where(numbers[2] == first // 8 + group, picked, value[0])
-                picked = jnp.take_along_axis(
-                    block[group * 8 : (group + 1) * 8], numbers[1], axis=0, mode="promise_in_bounds"
-                )
-                value[1] = jnp.where(numbers[3] == first // 8 + group, picked, value[1])
-        return value
-
-    def score_chunk(index, table, pieces, resume):
-        score = lax.dot_general(
-            table, images_v[rows_at(index * chunk, chunk), :],
-            (((1,), (1,)), ((), ())), preferred_element_type=F32,
-        )
-        for part in range(chunk // LANES):
-            number = poses[:, rows_at(index * chunk + part * LANES, LANES)]
-            numbers = [number[0:8] & 7, number[8:16] & 7, number[0:8] >> 3, number[8:16] >> 3]
-            block = index * (chunk // LANES) + part
-            if resume:
-                value = [picks[block, 0:8], picks[block, 8:16]]
-            else:
-                value = [jnp.zeros((8, LANES), F32), jnp.zeros((8, LANES), F32)]
-            value = picks_of(score[:, part * LANES : (part + 1) * LANES], pieces, numbers, value)
-            picks[block] = jnp.concatenate(value, axis=0)
-
-    def near_step(index):
-        score_chunk(index, slices[share : NPOSE - share, :], [(share, 0, NPOSE - 2 * share)], False)
-
-    gathers[2].wait_recv()
-    gathers[7].wait_recv()
-    gathers[8].wait_recv()
-    each(members - 1, power_step, 1)
-    each(chunks // 2, near_step)
-    gathers[5].wait_recv()
-    gathers[9].start()
-    gathers[6].wait_recv()
-    gathers[10].start()
-    each(chunks, near_step, chunks // 2)
-    gathers[9].wait_recv()
-    gathers[10].wait_recv()
-    power_step(0)
-    power_step(members - 1)
-
-    def far_chunk(index):
-        table = jnp.concatenate([slices[0:share, :], slices[NPOSE - share : NPOSE, :]], axis=0)
-        score_chunk(index, table, [(0, 0, share), (NPOSE - share, share, share)], True)
+    each(members, power_step)
+
+    def pick_chunk(index):
+        score = score_of(index, 1)
+        for piece in range(chunk // LANES):
+            at = rows_at(index * chunk + piece * LANES, LANES)
+            block = score[:, piece * LANES : (piece + 1) * LANES] + (scores[:, at] - half_power[...])
+            number = poses[:, at]
+            lows = [number[k : k + 8] & 7 for k in range(0, cands, 8)]
+            highs = [number[k : k + 8] >> 3 for k in range(0, cands, 8)]
+            value = [jnp.zeros((8, LANES), F32) for _ in lows]
+            for group in range(NPOSE // 8):
+                rows8 = block[group * 8 : (group + 1) * 8]
+                for k, (low, high) in enumerate(zip(lows, highs)):
+                    picked = jnp.take_along_axis(rows8, low, axis=0, mode="promise_in_bounds")
+                    value[k] = jnp.where(high == group, picked, value[k])
+            picks[index * (chunk // LANES) + piece] = jnp.concatenate(value, axis=0)
 
     def pick_send(peer):
         @pl.when(peer != own)
         def _():
             slab_copy(1, picks, picks_in, peer).start()
 
-    def far_step(index):
-        far_chunk(index)
+    def pick_step(index):
+        pick_chunk(index)
         pick_send(2 * index)
         pick_send(2 * index + 1)
 
-    each(chunks, far_step)
+    each(chunks, pick_step)
     picks_in[own] = picks[own]
     load[6].wait()
     row_weight[...] = jnp.zeros_like(row_weight)
+    masses[member] = jnp.zeros((8, LANES), F32)
     slab_arrivals(1, picks_in)
     total = picks_in[0]
     for block in range(1, slabs):
@@ -408,8 +417,6 @@
             row_weight[first : first + tile, :] += value.astype(F32)
 
     stripe = 2 * LANES
-    halves = 2
-    wide = width // halves
     per_half = wide // stripe
 
     def away_copy(index):
@@ -422,9 +429,6 @@
         away[:, at] = part[side:].astype(BF16)
         away_copy(index).start()
         kept[:, at] = part[:side]
-
-    def columns_of(part):
-        return slice(part * wide, (part + 1) * wide)
 
     def kept_part(index, part, first=0, size=share):
         here = index * share + first
@@ -493,6 +497,21 @@
     each(width // stripe, early_stripe)
     shares_arrive(1)
     each(slabs, spread_chunk, ahead_of)
+
+    weight = jnp.sum(row_weight[...], axis=1, keepdims=True)
+    mass_row = pick_row(iota((NPOSE, NPOSE), 0) == pose_row[0:1, :], weight)
+    for piece in range(NPOSE // LANES):
+        masses[member, piece : piece + 1, :] = mass_row[:, piece * LANES : (piece + 1) * LANES]
+
+    def mass_copy(step):
+        return img_copy(16, masses.at[member], masses.at[member], img_peer(step))
+
+    def img_whole(slot, ref):
+        blocks = ref.at[0 : members - 1]
+        return img_copy(slot, blocks, blocks, img_peer(1))
+
+    for step in range(1, members):
+        mass_copy(step).start()
     back_stripe(0)
     back_stripe(1)
     back_stripe(2)
@@ -500,20 +519,6 @@
     back_stripe(3)
     ring_relay(0)
     ring_start(1)
-
-    weight = jnp.sum(row_weight[...], axis=1, keepdims=True)
-    mass_row = pick_row(iota((NPOSE, NPOSE), 0) == pose_row[0:1, :], weight)
-    masses[member] = jnp.broadcast_to(mass_row, (8, NPOSE))
-
-    def mass_copy(step):
-        return img_copy(16, masses.at[member], masses.at[member], img_peer(step))
-
-    def img_whole(slot, ref):
-        blocks = ref.at[0 : members - 1]
-        return img_copy(slot, blocks, blocks, img_peer(1))
-
-    for step in range(1, members):
-        mass_copy(step).start()
     ring_relay(1)
     ring_finish(0)
     ring_finish(1)
@@ -521,15 +526,16 @@
         posterior[:, block * LANES : (block + 1) * LANES] = shares[block]
 
     img_whole(16, masses).wait_recv()
-    mass_total = masses[0]
+    mass_sum = masses[0]
     for index in range(1, members):
-        mass_total = mass_total + masses[index]
+        mass_sum = mass_sum + masses[index]
+    mass_total = jnp.concatenate([mass_sum[piece : piece + 1] for piece in range(NPOSE // LANES)], axis=1)
     lanes = iota((LANES, LANES), 1)
     mass_cols = []
     for block in range(members):
         key_col = slot_table[:, block * LANES : (block + 1) * LANES].T[:, 3:4]
         matched = key_col == iota((LANES, NPOSE), 1).astype(F32)
-        amount = jnp.sum(jnp.where(matched, mass_total[0:1, :], 0.0), axis=1, keepdims=True)
+        amount = jnp.sum(jnp.where(matched, mass_total, 0.0), axis=1, keepdims=True)
         first = amount.astype(BF16).astype(F32)
         second = (amount - first).astype(BF16).astype(F32)
         third = amount - first - second
@@ -563,10 +569,11 @@
         cross_copy(step).start()
     crossed[member] = crossing[member]
 
-    for stage, ref in ((0, outgoing), (1, picks), (2, shares), (3, returning.at[0]), (4, returning.at[1])):
+    for stage, ref in ((0, outgoing.at[0]), (7, outgoing.at[1]), (1, picks), (2, shares), (3, returning.at[0]), (4, returning.at[1])):
         slab_whole(stage, ref, slabs - 1).wait_send()
-    for copy in gathers:
-        copy.wait_send()
+    for part in range(halves):
+        for index in range(11):
+            gather_copy(part, index).wait_send()
     for index in range(halves * per_half):
         away_copy(index).wait_send()
     for part in range(halves):
@@ -613,10 +620,11 @@
         pltpu.VMEM((8, slabs * cap), F32),
         pltpu.VMEM((8, mine), F32),
         pltpu.VMEM((8, NPOSE), jnp.int32),
-        pltpu.VMEM((slabs, deep, width), BF16),
-        pltpu.VMEM((slabs, deep, width), BF16),
+        pltpu.VMEM((2, slabs, deep, width // 2), BF16),
+        pltpu.VMEM((2, slabs, deep, width // 2), BF16),
         pltpu.VMEM((NPOSE, width), BF16),
         pltpu.VMEM((NPOSE, LANES), F32),
+        pltpu.VMEM((NPOSE, particles), F32),
         pltpu.VMEM((voxels, slabs * cap), BF16),
         pltpu.VMEM((slabs, cands, LANES), F32),
         pltpu.VMEM((slabs, cands, LANES), F32),
@@ -631,17 +639,17 @@
         pltpu.VMEM((share, width), BF16),
         pltpu.VMEM((2, share, width), BF16),
         pltpu.VMEM((2, share, width), BF16),
-        pltpu.VMEM((members, 8, NPOSE), F32),
+        pltpu.VMEM((members, 8, LANES), F32),
         pltpu.VMEM((voxels, LANES), F32),
         pltpu.VMEM((2, slabs, deep, width // 2), BF16),
         pltpu.VMEM((2, slabs, deep, width // 2), BF16),
         pltpu.VMEM((members, mine, LANES), BF16),
         pltpu.VMEM((members, mine, LANES), BF16),
         pltpu.SemaphoreType.DMA((9,)),
-        pltpu.SemaphoreType.DMA((7,)),
-        pltpu.SemaphoreType.DMA((7,)),
-        pltpu.SemaphoreType.DMA((60,)),
-        pltpu.SemaphoreType.DMA((60,)),
+        pltpu.SemaphoreType.DMA((8,)),
+        pltpu.SemaphoreType.DMA((8,)),
+        pltpu.SemaphoreType.DMA((86,)),
+        pltpu.SemaphoreType.DMA((86,)),
     ]
     density, posterior = pl.pallas_call(
         functools.partial(kernel, slabs, members),

time: 73.3 us -> 75 us (1.023)
  Pallas kernels: 69.2 us -> 70.9 us
    pallas_call x1, Pallas kernels: 69.2 us -> 70.9 us  [per_device(): pl.pallas_call(functools.partial(kernel, slabs, members), out_shape=(jax....]
where the time goes in v5:
time: 75 us; the launch traced here: 74.8 us
  Pallas kernels  70.9 us (95%)
  local copies, waits for them, and re-layouts  3.24 us (4%)
    pallas_call x1, Pallas kernels, per_device(): pl.pallas_call(functools.partial(kernel, slabs, members), out_shape=(jax....  70.9 us
    unnamed x2, local copies, waits for them, and re-layouts  3.24 us

profile of v5, /device:TPU:1, one launch (start us, length us, event | category | flops | bytes accessed | tf_op | source)
XLA Modules:
  0.0 74.8 jit_solution(14464922549437764379)
XLA Ops:
  0.6 70.9 %shard_map.104 = (f32[2,64,512]{2,1,0:T(8,128)}, f32[16,2048]{1,0:T(8,128)}) custom-call(bf16[2048,1024]{1,0:T(8,128)(2,1)} %images.1, bf16[1024,1024]{1,0:T(8,128)(2,1)} %bitcast.5, bf16[1024,1024]{1,0:T(8,128)(2,1)} %constant.4.clone.columns, bf16[512,1024]{1,0:T(8,128)(2,1)} %constant.5.clone.rows, f32[1,2048]{1,0:T(1,128)} %bitcast.9, ...), custom_call_target="tpu_custom_call" | custom-call | tf_op jit(solution)/shard_map/pallas_call | solution.py:654
  71.6 1.7 %copy.13 = f32[2,512,64]{1,2,0:T(8,128)} copy(f32[2,512,64]{1,2,0:T(8,128)} %bitcast.6) | data formatting | bytes 524288
  73.2 1.6 %copy.14 = f32[2048,16]{0,1:T(8,128)} copy(f32[2048,16]{0,1:T(8,128)} %bitcast.8) | data formatting | bytes 262144

commit v6 on v4

--- a/solution.py
+++ b/solution.py
@@ -85,7 +85,7 @@
     density, posterior,
     images_v, volume_v, columns_v, rows_v, precision, poses, keys, voxel_of, weight_of,
     slot_table, pack_table, pose_row,
-    outgoing, incoming, slices, half_power, weave,
+    outgoing, incoming, slices, half_power, ranks, weave,
     picks, picks_in, shares, spread, row_weight, partial,
     away, away_in, kept, opposite, opposite_in, ring, ring_in,
     masses, inverse, returning, returned, crossing, crossed,
@@ -243,6 +243,21 @@
                 renamed = jnp.where(high == piece, found, renamed)
             poses[at] = renamed
 
+    ahead_of = slabs // 2
+    turn = own // ahead_of
+
+    def rank_chunk(block):
+        at = rows_at(block * LANES, LANES)
+        number = poses[:, at].astype(jnp.int16)
+        for first in range(0, NPOSE, LANES):
+            row = (iota((LANES, LANES), 0) + first).astype(jnp.int16)
+            value = jnp.full((LANES, LANES), cands, jnp.int16)
+            for k in range(cands):
+                value = jnp.where(number[k : k + 1] == row, jnp.int16(k), value)
+            ranks[first : first + LANES, at] = value.astype(jnp.int32)
+
+    each(slabs, rank_chunk, ahead_of)
+
     slab_arrivals(0, incoming)
     arrived = jnp.concatenate([incoming[block].astype(F32) for block in range(slabs)], axis=0).astype(BF16)
     pack = jnp.where(iota((share, mine), 0).astype(F32) == pack_table[0:1, :], 1.0, 0.0).astype(BF16)
@@ -370,19 +385,30 @@
     picks_in[own] = picks[own]
     load[6].wait()
     row_weight[...] = jnp.zeros_like(row_weight)
-    slab_arrivals(1, picks_in)
-    total = picks_in[0]
-    for block in range(1, slabs):
-        total = total + picks_in[block]
-    total = total * precision[:, rows_at(own * LANES, LANES)]
-    exponent = jnp.exp(total - jnp.max(total, axis=0, keepdims=True))
-    shares[own] = exponent / jnp.sum(exponent, axis=0, keepdims=True)
-    ahead_of = slabs // 2
-    turn = own // ahead_of
-    for step in range(1, slabs):
-        remote(
-            shares.at[own], shares.at[own], slab_send.at[2], slab_recv.at[5 + turn], {"slab": slab_peer(step)}
-        ).start()
+    masses[member] = jnp.zeros((8, LANES), F32)
+
+    def share_out():
+        slab_arrivals(1, picks_in)
+        total = picks_in[0]
+        for block in range(1, slabs):
+            total = total + picks_in[block]
+        total = total * precision[:, rows_at(own * LANES, LANES)]
+        exponent = jnp.exp(total - jnp.max(total, axis=0, keepdims=True))
+        shares[own] = exponent / jnp.sum(exponent, axis=0, keepdims=True)
+        for step in range(1, slabs):
+            remote(
+                shares.at[own], shares.at[own], slab_send.at[2], slab_recv.at[5 + turn], {"slab": slab_peer(step)}
+            ).start()
+
+    @pl.when(turn == 0)
+    def _():
+        share_out()
+
+    each(ahead_of, rank_chunk)
+
+    @pl.when(turn != 0)
+    def _():
+        share_out()
 
     def shares_arrive(which):
         @pl.when(turn == which)
@@ -393,22 +419,25 @@
         def _():
             slab_whole(5 + which, shares, ahead_of).wait_recv()
 
-    tile = LANES
-
     def spread_chunk(block):
         at = rows_at(block * LANES, LANES)
-        amount = (shares[block] * precision[:, at]).astype(BF16)
-        number = poses[:, at].astype(jnp.int16)
-        for first in range(0, NPOSE, tile):
-            row = (iota((tile, LANES), 0) + first).astype(jnp.int16)
-            value = jnp.zeros((tile, LANES), BF16)
-            for k in range(cands):
-                value = jnp.where(number[k : k + 1] == row, amount[k : k + 1], value)
-            spread[first : first + tile, at] = value
-            row_weight[first : first + tile, :] += value.astype(F32)
+        amount = shares[block] * precision[:, at]
+        rounded = amount.astype(BF16).astype(F32)
+        low, high = rounded[0:8], rounded[8:16]
+        for first in range(0, NPOSE, 16):
+            values = []
+            for group in (first, first + 8):
+                rank = ranks[group : group + 8, at]
+                place = rank & 7
+                from_low = jnp.take_along_axis(low, place, axis=0, mode="promise_in_bounds")
+                from_high = jnp.take_along_axis(high, place, axis=0, mode="promise_in_bounds")
+                value = jnp.where(rank < 8, from_low, jnp.where(rank < cands, from_high, 0.0))
+                row_weight[group : group + 8, :] += value
+                values.append(value)
+            spread[first : first + 16, at] = jnp.concatenate(values, axis=0).astype(BF16)
 
     stripe = 2 * LANES
-    halves = 2
+    halves = 1
     wide = width // halves
     per_half = wide // stripe
 
@@ -493,17 +522,11 @@
     each(width // stripe, early_stripe)
     shares_arrive(1)
     each(slabs, spread_chunk, ahead_of)
-    back_stripe(0)
-    back_stripe(1)
-    back_stripe(2)
-    ring_start(0)
-    back_stripe(3)
-    ring_relay(0)
-    ring_start(1)
 
     weight = jnp.sum(row_weight[...], axis=1, keepdims=True)
     mass_row = pick_row(iota((NPOSE, NPOSE), 0) == pose_row[0:1, :], weight)
-    masses[member] = jnp.broadcast_to(mass_row, (8, NPOSE))
+    for piece in range(NPOSE // LANES):
+        masses[member, piece : piece + 1, :] = mass_row[:, piece * LANES : (piece + 1) * LANES]
 
     def mass_copy(step):
         return img_copy(16, masses.at[member], masses.at[member], img_peer(step))
@@ -514,22 +537,25 @@
 
     for step in range(1, members):
         mass_copy(step).start()
-    ring_relay(1)
+    for index in range(width // stripe):
+        back_stripe(index)
+    ring_start(0)
+    ring_relay(0)
     ring_finish(0)
-    ring_finish(1)
     for block in range(slabs):
         posterior[:, block * LANES : (block + 1) * LANES] = shares[block]
 
     img_whole(16, masses).wait_recv()
-    mass_total = masses[0]
+    mass_sum = masses[0]
     for index in range(1, members):
-        mass_total = mass_total + masses[index]
+        mass_sum = mass_sum + masses[index]
+    mass_total = jnp.concatenate([mass_sum[piece : piece + 1] for piece in range(NPOSE // LANES)], axis=1)
     lanes = iota((LANES, LANES), 1)
     mass_cols = []
     for block in range(members):
         key_col = slot_table[:, block * LANES : (block + 1) * LANES].T[:, 3:4]
         matched = key_col == iota((LANES, NPOSE), 1).astype(F32)
-        amount = jnp.sum(jnp.where(matched, mass_total[0:1, :], 0.0), axis=1, keepdims=True)
+        amount = jnp.sum(jnp.where(matched, mass_total, 0.0), axis=1, keepdims=True)
         first = amount.astype(BF16).astype(F32)
         second = (amount - first).astype(BF16).astype(F32)
         third = amount - first - second
@@ -563,7 +589,7 @@
         cross_copy(step).start()
     crossed[member] = crossing[member]
 
-    for stage, ref in ((0, outgoing), (1, picks), (2, shares), (3, returning.at[0]), (4, returning.at[1])):
+    for stage, ref in ((0, outgoing), (1, picks), (2, shares), (3, returning.at[0])):
         slab_whole(stage, ref, slabs - 1).wait_send()
     for copy in gathers:
         copy.wait_send()
@@ -617,6 +643,7 @@
         pltpu.VMEM((slabs, deep, width), BF16),
         pltpu.VMEM((NPOSE, width), BF16),
         pltpu.VMEM((NPOSE, LANES), F32),
+        pltpu.VMEM((NPOSE, particles), jnp.int32),
         pltpu.VMEM((voxels, slabs * cap), BF16),
         pltpu.VMEM((slabs, cands, LANES), F32),
         pltpu.VMEM((slabs, cands, LANES), F32),
@@ -631,10 +658,10 @@
         pltpu.VMEM((share, width), BF16),
         pltpu.VMEM((2, share, width), BF16),
         pltpu.VMEM((2, share, width), BF16),
-        pltpu.VMEM((members, 8, NPOSE), F32),
+        pltpu.VMEM((members, 8, LANES), F32),
         pltpu.VMEM((voxels, LANES), F32),
-        pltpu.VMEM((2, slabs, deep, width // 2), BF16),
-        pltpu.VMEM((2, slabs, deep, width // 2), BF16),
+        pltpu.VMEM((1, slabs, deep, width), BF16),
+        pltpu.VMEM((1, slabs, deep, width), BF16),
         pltpu.VMEM((members, mine, LANES), BF16),
         pltpu.VMEM((members, mine, LANES), BF16),
         pltpu.SemaphoreType.DMA((9,)),

time: 73.3 us -> 71.7 us (0.978)
  Pallas kernels: 69.2 us -> 67.6 us
    pallas_call x1, Pallas kernels: 69.2 us -> 67.6 us  [per_device(): pl.pallas_call(functools.partial(kernel, slabs, members), out_shape=(jax....]
where the time goes in v6:
time: 71.7 us; the launch traced here: 71.5 us
  Pallas kernels  67.6 us (94%)
  local copies, waits for them, and re-layouts  3.24 us (5%)
    pallas_call x1, Pallas kernels, per_device(): pl.pallas_call(functools.partial(kernel, slabs, members), out_shape=(jax....  67.6 us
    unnamed x2, local copies, waits for them, and re-layouts  3.24 us

profile of v6, /device:TPU:1, one launch (start us, length us, event | category | flops | bytes accessed | tf_op | source)
XLA Modules:
  0.0 71.5 jit_solution(15255252523020467769)
XLA Ops:
  0.6 67.6 %shard_map.104 = (f32[2,64,512]{2,1,0:T(8,128)}, f32[16,2048]{1,0:T(8,128)}) custom-call(bf16[2048,1024]{1,0:T(8,128)(2,1)} %images.1, bf16[1024,1024]{1,0:T(8,128)(2,1)} %bitcast.5, bf16[1024,1024]{1,0:T(8,128)(2,1)} %constant.4.clone.columns, bf16[512,1024]{1,0:T(8,128)(2,1)} %constant.5.clone.rows, f32[1,2048]{1,0:T(1,128)} %bitcast.9, ...), custom_call_target="tpu_custom_call" | custom-call | tf_op jit(solution)/shard_map/pallas_call | solution.py:673
  68.3 1.7 %copy.13 = f32[2,512,64]{1,2,0:T(8,128)} copy(f32[2,512,64]{1,2,0:T(8,128)} %bitcast.6) | data formatting | bytes 524288
  69.9 1.6 %copy.14 = f32[2048,16]{0,1:T(8,128)} copy(f32[2048,16]{0,1:T(8,128)} %bitcast.8) | data formatting | bytes 262144

commit v7 on v1

v7 whole, which is shorter than its diff:
```python
import functools
import math

import jax
import jax.numpy as jnp
import numpy as np
from jax import lax
from jax.experimental import pallas as pl
from jax.experimental.pallas import tpu as pltpu
from jax.sharding import PartitionSpec as P

NPOSE = 512
WSTEPS = 16
RIDGE = 0.25
LANES = 128
F32 = jnp.float32
BF16 = jnp.bfloat16


def gridding(samples):
    offset = (np.arange(samples) - samples / 2) / samples
    return 1.0 / np.sinc(offset) ** 2


def angles(length):
    counter = np.arange(length)
    return (counter[:, None] * counter[None, :] % length) * (2.0 * math.pi / length)


def column_table(length, members):
    turn = angles(length)
    cosine, sine = np.cos(turn), np.sin(turn)
    scale = gridding(length)[None, :]
    to_re = np.concatenate([cosine, -sine], axis=0) * scale
    to_im = np.concatenate([sine, cosine], axis=0) * scale
    width = length // members
    both = np.stack([to_re.reshape(-1, members, width), to_im.reshape(-1, members, width)], axis=2)
    return jnp.asarray(both.reshape(2 * length, 2 * length), BF16)


def row_table(length):
    turn = angles(length)
    scale = gridding(length)[:, None] / length
    return jnp.asarray(np.concatenate([np.cos(turn), -np.sin(turn)], axis=1) * scale, BF16)


def remote(src, dst, sends, recvs, device):
    return pltpu.make_async_remote_copy(
        src_ref=src,
        dst_ref=dst,
        send_sem=sends,
        recv_sem=recvs,
        device_id=device,
        device_id_type=pl.DeviceIdType.MESH,
    )


def dot(left, right):
    return jnp.dot(left, right, preferred_element_type=F32)


def each(count, step, first=0):
    def body(index, carry):
        step(index)
        return carry

    lax.fori_loop(first, count, body, 0)


def rows_at(start, size):
    return pl.ds(pl.multiple_of(start, size), size)


def iota(shape, axis):
    return lax.broadcasted_iota(jnp.int32, shape, axis)


def pick_row(mask, values):
    return jnp.sum(jnp.where(mask, values, 0.0), axis=0, keepdims=True)


def kernel(
    slabs, members,
    images, volume, columns, rows, precision_in, poses_in, keys_in, voxels_in, weights_in,
    density, posterior,
    images_v, volume_v, columns_v, rows_v, precision, poses, keys, voxel_of, weight_of,
    slot_table, pack_table, pose_row,
    outgoing, incoming, slices, half_power, ranks, weave,
    picks, picks_in, shares, spread, row_weight, partial,
    away, away_in, kept, opposite, opposite_in, ring, ring_in,
    masses, inverse, returning, returned, crossing, crossed,
    loads, slab_send, slab_recv, img_send, img_recv,
):
    own = lax.axis_index("slab")
    member = lax.axis_index("img")
    ring_len = members // 2
    chip, core = member // 2, lax.rem(member, 2)
    share = NPOSE // members
    half = share // 2
    side = ring_len * share
    deep = outgoing.shape[1]
    mine = slabs * deep
    cap = keys.shape[2]
    width = volume_v.shape[1]
    voxels = volume_v.shape[0]
    cands = poses.shape[0]
    right = 2 * lax.rem(chip + 1, ring_len) + core
    left = 2 * lax.rem(chip + ring_len - 1, ring_len) + core
    partner = 2 * chip + 1 - core

    def slab_peer(step):
        return lax.rem(own + step, slabs)

    def img_peer(step):
        return lax.rem(member + step, members)

    barrier = pltpu.get_barrier_semaphore()

    def greet(axis, peer):
        pl.semaphore_signal(barrier, inc=1, device_id={axis: peer}, device_id_type=pl.DeviceIdType.MESH)

    sources = [keys_in, voxels_in, weights_in, volume, poses_in, images, precision_in, columns, rows]
    targets = [keys, voxel_of, weight_of, volume_v, poses, images_v, precision, columns_v, rows_v]
    load = [pltpu.make_async_copy(src, dst, loads.at[i]) for i, (src, dst) in enumerate(zip(sources, targets))]

    def start_load(index):
        src, dst = sources[index], targets[index]
        pieces = 8 if src.shape[0] >= 512 else 1
        size = src.shape[0] // pieces
        for piece in range(pieces):
            at = slice(piece * size, (piece + 1) * size)
            pltpu.make_async_copy(src.at[at], dst.at[at], loads.at[index]).start()

    for index in range(5):
        start_load(index)
    for step in range(1, slabs):
        greet("slab", slab_peer(step))
    for step in range(1, members):
        greet("img", img_peer(step))

    with jax.named_scope("own_slots"):
        for index in range(3):
            load[index].wait()
        before = jnp.zeros((slabs, cap), F32)
        for slab in range(slabs):
            before += jnp.where(keys[slab] >= 0, 1.0, 0.0) * jnp.where(own > slab, 1.0, 0.0)
        out_start = jnp.sum(before, axis=1, keepdims=True)
        total_slots = slabs * cap
        own_key = keys[own]
        own_code = voxel_of[own] * 32 + jnp.where(own_key >= 0, weight_of[own], 31)

        def ordered(first, count, tables):
            position = iota((1, count), 1) + first
            block_sel = iota((slabs, count), 0) == ((position >> 3) & (slabs - 1))
            start_row = pick_row(block_sel, out_start).astype(jnp.int32)
            slot_row = members * (position & 7) + (((position >> 7) - start_row) & 7)
            slot_sel = iota((cap, count), 0) == slot_row
            chooser = jnp.where(block_sel, 1.0, 0.0)
            found = []
            for table in tables:
                wide = lax.dot_general(
                    table.astype(F32), chooser, (((0,), (0,)), ((), ())),
                    precision=lax.Precision.HIGHEST, preferred_element_type=F32,
                )
                found.append(pick_row(slot_sel, wide))
            return found

        def decoded(code):
            code_row = code.astype(jnp.int32)
            level = code_row & 31
            alive = level <= WSTEPS
            spot = (code_row >> 5).astype(F32)
            lower = jnp.where(alive, level, 0).astype(F32) * (1.0 / WSTEPS)
            upper = jnp.where(alive, WSTEPS - level, 0).astype(F32) * (1.0 / WSTEPS)
            return spot, lower, upper

        parts = decoded(ordered(member * mine, mine, [own_code])[0])
        own_cols = jnp.concatenate(list(parts) + [jnp.zeros((5, mine), F32)], axis=0).T
        place = iota((mine, voxels), 1)
        spot = own_cols[:, 0:1].astype(jnp.int32)
        take = jnp.where(place == spot, own_cols[:, 1:2], 0.0) + jnp.where(place == spot + 1, own_cols[:, 2:3], 0.0)
        load[3].wait()
        for index in range(5, len(load)):
            start_load(index)
        woven = dot(take.astype(BF16), volume_v[...])
        for block in range(slabs):
            outgoing[block] = woven[block * deep : (block + 1) * deep].astype(BF16)
        pl.semaphore_wait(barrier, slabs - 1 + members - 1)

        def slab_copy(stage, src, dst, peer):
            return remote(src.at[peer], dst.at[own], slab_send.at[stage], slab_recv.at[stage], {"slab": peer})

        def slab_whole(stage, ref, count):
            blocks = ref.at[0:count]
            return remote(blocks, blocks, slab_send.at[stage], slab_recv.at[stage], {"slab": slab_peer(1)})

        def slab_exchange(stage, src, dst):
            for step in range(1, slabs):
                slab_copy(stage, src, dst, slab_peer(step)).start()

        def slab_arrivals(stage, dst):
            slab_whole(stage, dst, slabs - 1).wait_recv()

        def img_copy(slot, src, dst, device):
            return remote(src, dst, img_send.at[slot], img_recv.at[slot], {"img": device})

    with jax.named_scope("tables"):
        slab_exchange(0, outgoing, incoming)
        incoming[own] = outgoing[own]

        code, key_row = ordered(0, total_slots, [own_code, own_key])
        for index, value in enumerate(decoded(code) + (key_row,)):
            slot_table[index : index + 1, :] = value
        slot_table[4:8, :] = jnp.zeros((4, total_slots), F32)

        in_key = jnp.concatenate(
            [jnp.sum(jnp.where(iota((slabs, cap), 0) == own, keys[slab], 0), axis=0, keepdims=True) for slab in range(slabs)],
            axis=0,
        )
        live = jnp.where(in_key >= 0, 1.0, 0.0).astype(BF16)
        count = dot(live, jnp.ones((cap, LANES), BF16))
        earlier = jnp.where(iota((slabs, slabs), 1) < iota((slabs, slabs), 0), 1.0, 0.0).astype(BF16)
        start = dot(earlier, count.astype(BF16))
        lane = iota((1, mine), 1)
        slab_sel = iota((slabs, mine), 0) == (lane >> 3)
        in_start = pick_row(slab_sel, start).astype(jnp.int32)
        in_count = pick_row(slab_sel, count).astype(jnp.int32)
        slot = members * (lane & 7) + ((member - in_start) & 7)
        pack_row = jnp.where(slot < in_count, (in_start + slot) >> 3, -1)
        pack_table[...] = jnp.broadcast_to(pack_row, (8, mine)).astype(F32)

        number = start[:, :cap].astype(jnp.int32) + iota((slabs, cap), 1)
        holder = number & (members - 1)
        ahead = ((holder >> 1) - chip) & (ring_len - 1)
        near = jnp.where(ahead == 0, 3, jnp.where(ahead == 1, 1, jnp.where(ahead == 2, 0, 2)))
        row = jnp.where((holder & 1) == core, near, members - 1 - near) * share + (number >> 3)
        key_cols, row_cols = in_key.astype(F32).T, row.astype(F32).T
        pose_ids = iota((cap, NPOSE), 1).astype(F32)
        found_rows = jnp.zeros((cap, NPOSE), F32)
        for slab in range(slabs):
            found_rows += jnp.where(key_cols[:, slab : slab + 1] == pose_ids, row_cols[:, slab : slab + 1], 0.0)
        pose_row[...] = jnp.broadcast_to(jnp.sum(found_rows, axis=0, keepdims=True), (8, NPOSE)).astype(jnp.int32)

        load[4].wait()
        for part in range(poses.shape[1] // LANES):
            for k in range(0, cands, 8):
                at = (slice(k, k + 8), slice(part * LANES, (part + 1) * LANES))
                pose = poses[at]
                low, high = pose & (LANES - 1), pose >> 7
                renamed = jnp.zeros_like(pose)
                for piece in range(NPOSE // LANES):
                    table = pose_row[:, piece * LANES : (piece + 1) * LANES]
                    found = jnp.take_along_axis(table, low, axis=1, mode="promise_in_bounds")
                    renamed = jnp.where(high == piece, found, renamed)
                poses[at] = renamed

        ahead_of = slabs // 2
        turn = own // ahead_of

        def rank_chunk(block):
            at = rows_at(block * LANES, LANES)
            number = poses[:, at].astype(jnp.int16)
            for first in range(0, NPOSE, LANES):
                row = (iota((LANES, LANES), 0) + first).astype(jnp.int16)
                value = jnp.full((LANES, LANES), cands, jnp.int16)
                for k in range(cands):
                    value = jnp.where(number[k : k + 1] == row, jnp.int16(k), value)
                ranks[first : first + LANES, at] = value.astype(jnp.int32)

        each(slabs, rank_chunk, ahead_of)

    with jax.named_scope("pack_rows"):
        slab_arrivals(0, incoming)
        arrived = jnp.concatenate([incoming[block].astype(F32) for block in range(slabs)], axis=0).astype(BF16)
        pack = jnp.where(iota((share, mine), 0).astype(F32) == pack_table[0:1, :], 1.0, 0.0).astype(BF16)

        def block_of(index, first=0, size=share):
            return slices.at[index * share + first : index * share + first + size]

        FAR, RIGHT, LEFT, HOME = 0, 1, 2, 3
        slices[HOME * share : (HOME + 1) * share, :] = dot(pack, arrived).astype(BF16)

        def other(index):
            return members - 1 - index

        def top(index):
            return block_of(index, 0, half)

        def bottom(index):
            return block_of(index, half, half)

        gathers = [
            img_copy(0, top(HOME), top(LEFT), right),
            img_copy(1, bottom(HOME), bottom(RIGHT), left),
            img_copy(2, block_of(HOME), block_of(other(HOME)), partner),
            img_copy(3, bottom(HOME), bottom(LEFT), right),
            img_copy(4, top(HOME), top(RIGHT), left),
            img_copy(5, top(LEFT), top(FAR), right),
            img_copy(6, bottom(RIGHT), bottom(FAR), left),
            img_copy(7, block_of(LEFT), block_of(other(LEFT)), partner),
            img_copy(8, block_of(RIGHT), block_of(other(RIGHT)), partner),
            img_copy(9, top(FAR), top(other(FAR)), partner),
            img_copy(10, bottom(FAR), bottom(other(FAR)), partner),
        ]
        for index in range(5):
            gathers[index].start()

    with jax.named_scope("gather_near"):
        def weave_step(index):
            at = iota((LANES, total_slots), 0) + index * LANES
            spots = slot_table[0:1, :].astype(jnp.int32)
            value = jnp.where(spots == at, slot_table[1:2, :], 0.0) + jnp.where(spots + 1 == at, slot_table[2:3, :], 0.0)
            weave[rows_at(index * LANES, LANES), :] = value.astype(BF16)

        each(voxels // LANES, weave_step)
        gathers[0].wait_recv()
        gathers[5].start()
        gathers[1].wait_recv()
        gathers[6].start()
        gathers[3].wait_recv()
        gathers[7].start()
        gathers[4].wait_recv()
        gathers[8].start()
        load[5].wait()

        def power_step(index):
            at = rows_at(index * share, share)
            values = slices[at, :].astype(F32)
            total = 0.5 * jnp.sum(values * values, axis=1, keepdims=True)
            half_power[at, :] = jnp.broadcast_to(total, (share, LANES))

        chunk = 2 * LANES
        chunks = images_v.shape[0] // chunk

        def picks_of(score, pieces, numbers, value):
            for first, offset, size in pieces:
                block = score[offset : offset + size] - half_power[first : first + size, :]
                for group in range(size // 8):
                    picked = jnp.take_along_axis(
                        block[group * 8 : (group + 1) * 8], numbers[0], axis=0, mode="promise_in_bounds"
                    )
                    value[0] = jnp.where(numbers[2] == first // 8 + group, picked, value[0])
                    picked = jnp.take_along_axis(
                        block[group * 8 : (group + 1) * 8], numbers[1], axis=0, mode="promise_in_bounds"
                    )
                    value[1] = jnp.where(numbers[3] == first // 8 + group, picked, value[1])
            return value

        def score_chunk(index, table, pieces, resume):
            score = lax.dot_general(
                table, images_v[rows_at(index * chunk, chunk), :],
                (((1,), (1,)), ((), ())), preferred_element_type=F32,
            )
            for part in range(chunk // LANES):
                number = poses[:, rows_at(index * chunk + part * LANES, LANES)]
                numbers = [number[0:8] & 7, number[8:16] & 7, number[0:8] >> 3, number[8:16] >> 3]
                block = index * (chunk // LANES) + part
                if resume:
                    value = [picks[block, 0:8], picks[block, 8:16]]
                else:
                    value = [jnp.zeros((8, LANES), F32), jnp.zeros((8, LANES), F32)]
                value = picks_of(score[:, part * LANES : (part + 1) * LANES], pieces, numbers, value)
                picks[block] = jnp.concatenate(value, axis=0)

        def near_step(index):
            score_chunk(index, slices[share : NPOSE - share, :], [(share, 0, NPOSE - 2 * share)], False)

        def far_chunk(index):
            table = jnp.concatenate([slices[0:share, :], slices[NPOSE - share : NPOSE, :]], axis=0)
            score_chunk(index, table, [(0, 0, share), (NPOSE - share, share, share)], True)

        def full_chunk(index):
            score_chunk(index, slices[...], [(0, 0, NPOSE)], False)

    with jax.named_scope("scores"):
        gathers[2].wait_recv()
        gathers[7].wait_recv()
        gathers[8].wait_recv()
        each(members - 1, power_step, 1)
        each(chunks // 4, near_step)
        gathers[5].wait_recv()
        gathers[9].start()
        gathers[6].wait_recv()
        gathers[10].start()
        each(chunks // 2, near_step, chunks // 4)
        gathers[9].wait_recv()
        gathers[10].wait_recv()
        power_step(0)
        power_step(members - 1)

        def pick_send(peer):
            @pl.when(peer != own)
            def _():
                slab_copy(1, picks, picks_in, peer).start()

        def far_step(index):
            far_chunk(index)
            pick_send(2 * index)
            pick_send(2 * index + 1)

        def full_step(index):
            full_chunk(index)
            pick_send(2 * index)
            pick_send(2 * index + 1)

        each(chunks // 2, far_step)
        each(chunks, full_step, chunks // 2)
        picks_in[own] = picks[own]
        load[6].wait()
        row_weight[...] = jnp.zeros_like(row_weight)
        masses[member] = jnp.zeros((8, LANES), F32)

        def share_out():
            slab_arrivals(1, picks_in)
            total = picks_in[0]
            for block in range(1, slabs):
                total = total + picks_in[block]
            total = total * precision[:, rows_at(own * LANES, LANES)]
            exponent = jnp.exp(total - jnp.max(total, axis=0, keepdims=True))
            shares[own] = exponent / jnp.sum(exponent, axis=0, keepdims=True)
            for step in range(1, slabs):
                remote(
                    shares.at[own], shares.at[own], slab_send.at[2], slab_recv.at[5 + turn], {"slab": slab_peer(step)}
                ).start()

    with jax.named_scope("sum_scores"):
        @pl.when(turn == 0)
        def _():
            share_out()

        each(ahead_of, rank_chunk)

        @pl.when(turn != 0)
        def _():
            share_out()

        def shares_arrive(which):
            @pl.when(turn == which)
            def _():
                slab_whole(5 + which, shares, ahead_of - 1).wait_recv()

            @pl.when(turn != which)
            def _():
                slab_whole(5 + which, shares, ahead_of).wait_recv()

        def spread_chunk(block):
            at = rows_at(block * LANES, LANES)
            amount = shares[block] * precision[:, at]
            rounded = amount.astype(BF16).astype(F32)
            low, high = rounded[0:8], rounded[8:16]
            for first in range(0, NPOSE, 16):
                values = []
                for group in (first, first + 8):
                    rank = ranks[group : group + 8, at]
                    place = rank & 7
                    from_low = jnp.take_along_axis(low, place, axis=0, mode="promise_in_bounds")
                    from_high = jnp.take_along_axis(high, place, axis=0, mode="promise_in_bounds")
                    value = jnp.where(rank < 8, from_low, jnp.where(rank < cands, from_high, 0.0))
                    row_weight[group : group + 8, :] += value
                    values.append(value)
                spread[first : first + 16, at] = jnp.concatenate(values, axis=0).astype(BF16)

        stripe = 2 * LANES
        halves = 1
        wide = width // halves
        per_half = wide // stripe

        def away_copy(index):
            at = slice(index * stripe, (index + 1) * stripe)
            return img_copy(40 + index, away.at[:, at], away_in.at[:, at], partner)

        def back_stripe(index):
            at = slice(index * stripe, (index + 1) * stripe)
            part = partial[:, at] + dot(spread[:, early:], images_v[early:, at])
            away[:, at] = part[side:].astype(BF16)
            away_copy(index).start()
            kept[:, at] = part[:side]

        def columns_of(part):
            return slice(part * wide, (part + 1) * wide)

        def kept_part(index, part, first=0, size=share):
            here = index * share + first
            there = (ring_len - 1 - index) * share + first
            at = columns_of(part)
            return kept[here : here + size, at] + away_in[there : there + size, at].astype(F32)

        def ring_copy(part, index):
            at = columns_of(part)
            low, high = slice(0, half), slice(half, share)
            refs = [
                (opposite.at[low, at], opposite_in.at[low, at], right),
                (opposite.at[high, at], opposite_in.at[high, at], left),
                (ring.at[0, high, at], ring_in.at[0, high, at], right),
                (ring.at[1, low, at], ring_in.at[1, low, at], left),
                (ring.at[0, low, at], ring_in.at[0, low, at], right),
                (ring.at[1, high, at], ring_in.at[1, high, at], left),
            ]
            return img_copy(48 + 6 * part + index, *refs[index])

        def ring_start(part):
            at = columns_of(part)
            for index in range(part * per_half, (part + 1) * per_half):
                away_copy(index).wait_recv()
            opposite[:, at] = kept_part(FAR, part).astype(BF16)
            ring_copy(part, 0).start()
            ring_copy(part, 1).start()
            ring[0, half:share, at] = kept_part(RIGHT, part, half, half).astype(BF16)
            ring_copy(part, 2).start()
            ring[1, 0:half, at] = kept_part(LEFT, part, 0, half).astype(BF16)
            ring_copy(part, 3).start()

        def ring_relay(part):
            at = columns_of(part)
            ring_copy(part, 0).wait_recv()
            ring[0, 0:half, at] = (kept_part(RIGHT, part, 0, half) + opposite_in[0:half, at].astype(F32)).astype(BF16)
            ring_copy(part, 4).start()
            ring_copy(part, 1).wait_recv()
            ring[1, half:share, at] = (
                kept_part(LEFT, part, half, half) + opposite_in[half:share, at].astype(F32)
            ).astype(BF16)
            ring_copy(part, 5).start()

        unpack = jnp.where(pack_table[...].T[:, 0:1] == iota((mine, share), 1).astype(F32), 1.0, 0.0).astype(BF16)

        def ring_finish(part):
            at = columns_of(part)
            held = kept_part(HOME, part)
            for index in range(2, 6):
                ring_copy(part, index).wait_recv()
            summed = (held + ring_in[0, :, at].astype(F32) + ring_in[1, :, at].astype(F32)).astype(BF16)
            unpacked = dot(unpack, summed)
            for block in range(slabs):
                returning[part, block] = unpacked[block * deep : (block + 1) * deep].astype(BF16)
            slab_exchange(3 + part, returning.at[part], returned.at[part])
            returned[part, own] = returning[part, own]

        early = images_v.shape[0] // 2

        def early_stripe(index):
            at = rows_at(index * stripe, stripe)
            partial[:, at] = dot(spread[:, :early], images_v[:early, at])

    with jax.named_scope("spread_first"):
        shares_arrive(0)
        each(ahead_of, spread_chunk)
        each(width // stripe, early_stripe)

    with jax.named_scope("spread_second"):
        shares_arrive(1)
        each(slabs, spread_chunk, ahead_of)

    with jax.named_scope("stripes"):
        weight = jnp.sum(row_weight[...], axis=1, keepdims=True)
        mass_row = pick_row(iota((NPOSE, NPOSE), 0) == pose_row[0:1, :], weight)
        for piece in range(NPOSE // LANES):
            masses[member, piece : piece + 1, :] = mass_row[:, piece * LANES : (piece + 1) * LANES]

        def mass_copy(step):
            return img_copy(16, masses.at[member], masses.at[member], img_peer(step))

        def img_whole(slot, ref):
            blocks = ref.at[0 : members - 1]
            return img_copy(slot, blocks, blocks, img_peer(1))

        for step in range(1, members):
            mass_copy(step).start()
        for index in range(width // stripe):
            back_stripe(index)

    with jax.named_scope("ring"):
        ring_start(0)
        ring_relay(0)

    with jax.named_scope("unpack"):
        ring_finish(0)
        for block in range(slabs):
            posterior[:, block * LANES : (block + 1) * LANES] = shares[block]

    with jax.named_scope("voxel_masses"):
        img_whole(16, masses).wait_recv()
        mass_sum = masses[0]
        for index in range(1, members):
            mass_sum = mass_sum + masses[index]
        mass_total = jnp.concatenate([mass_sum[piece : piece + 1] for piece in range(NPOSE // LANES)], axis=1)
        lanes = iota((LANES, LANES), 1)
        mass_cols = []
        for block in range(members):
            key_col = slot_table[:, block * LANES : (block + 1) * LANES].T[:, 3:4]
            matched = key_col == iota((LANES, NPOSE), 1).astype(F32)
            amount = jnp.sum(jnp.where(matched, mass_total, 0.0), axis=1, keepdims=True)
            first = amount.astype(BF16).astype(F32)
            second = (amount - first).astype(BF16).astype(F32)
            third = amount - first - second
            mass_cols.append(
                jnp.where(lanes == 0, first, jnp.where(lanes == 1, second, jnp.where(lanes == 2, third, 0.0))).astype(BF16)
            )
        mass_table = jnp.concatenate(mass_cols, axis=0)

        def mass_step(index):
            at = rows_at(index * LANES, LANES)
            mass = jnp.sum(dot(weave[at, :], mass_table), axis=1, keepdims=True)
            inverse[at, :] = jnp.broadcast_to(1.0 / (mass + RIDGE), (LANES, LANES))

        each(voxels // LANES, mass_step)
        load[7].wait()
        load[8].wait()

    with jax.named_scope("transform_x"):
        turned = jnp.zeros((mine, width), F32)
        for part in range(halves):
            slab_arrivals(3 + part, returned.at[part])
            gathered = jnp.concatenate([returned[part, block].astype(F32) for block in range(slabs)], axis=0)
            turned += dot(gathered.astype(BF16), columns_v[columns_of(part), :])
        for block in range(members):
            crossing[block] = turned[:, block * LANES : (block + 1) * LANES].astype(BF16)

        def cross_copy(step):
            peer = img_peer(step)
            return img_copy(17, crossing.at[peer], crossed.at[member], peer)

        for step in range(1, members):
            cross_copy(step).start()
        crossed[member] = crossing[member]

    with jax.named_scope("sends_done"):
        for stage, ref in ((0, outgoing), (1, picks), (2, shares), (3, returning.at[0])):
            slab_whole(stage, ref, slabs - 1).wait_send()
        for copy in gathers:
            copy.wait_send()
        for index in range(halves * per_half):
            away_copy(index).wait_send()
        for part in range(halves):
            for index in range(6):
                ring_copy(part, index).wait_send()
        img_whole(16, masses).wait_send()
        img_whole(17, crossed).wait_recv()

    with jax.named_scope("transform_y"):
        voxel_rows = dot(weave[...], crossed[...].reshape(members * LANES, LANES)) * inverse[...]
        fourier = voxel_rows.astype(BF16)
        edge = density.shape[2]
        columns_out = density.shape[1]
        for plane in range(density.shape[0]):
            field = fourier[plane * edge : (plane + 1) * edge]
            real = dot(rows_v[:, :edge], field)
            imag = dot(rows_v[:, edge:], field)
            density[plane] = (real[:, :columns_out] + imag[:, columns_out:]).T
        img_whole(17, crossing).wait_send()


def per_device(images, volume, precision, candidates, slot_key, slot_voxel, slot_weight):
    members = lax.axis_size("img")
    slabs = lax.axis_size("slab")
    planes, edge, width = volume.shape
    particles, cands = candidates.shape
    cap = slot_key.shape[2]
    deep = cap // members
    share = NPOSE // members
    voxels = planes * edge
    mine = slabs * deep
    side = NPOSE // 2
    big = pl.BlockSpec(memory_space=pl.ANY)
    near = pl.BlockSpec(memory_space=pltpu.VMEM)
    scratch = [
        pltpu.VMEM((particles, width), BF16),
        pltpu.VMEM((voxels, width), BF16),
        pltpu.VMEM((width, width), BF16),
        pltpu.VMEM((edge, 2 * edge), BF16),
        pltpu.VMEM((1, particles), F32),
        pltpu.VMEM((cands, particles), jnp.int32),
        pltpu.VMEM(slot_key.shape, jnp.int32),
        pltpu.VMEM(slot_key.shape, jnp.int32),
        pltpu.VMEM(slot_key.shape, jnp.int32),
        pltpu.VMEM((8, slabs * cap), F32),
        pltpu.VMEM((8, mine), F32),
        pltpu.VMEM((8, NPOSE), jnp.int32),
        pltpu.VMEM((slabs, deep, width), BF16),
        pltpu.VMEM((slabs, deep, width), BF16),
        pltpu.VMEM((NPOSE, width), BF16),
        pltpu.VMEM((NPOSE, LANES), F32),
        pltpu.VMEM((NPOSE, particles), jnp.int32),
        pltpu.VMEM((voxels, slabs * cap), BF16),
        pltpu.VMEM((slabs, cands, LANES), F32),
        pltpu.VMEM((slabs, cands, LANES), F32),
        pltpu.VMEM((slabs, cands, LANES), F32),
        pltpu.VMEM((NPOSE, particles), BF16),
        pltpu.VMEM((NPOSE, LANES), F32),
        pltpu.VMEM((NPOSE, width), F32),
        pltpu.VMEM((side, width), BF16),
        pltpu.VMEM((side, width), BF16),
        pltpu.VMEM((side, width), F32),
        pltpu.VMEM((share, width), BF16),
        pltpu.VMEM((share, width), BF16),
        pltpu.VMEM((2, share, width), BF16),
        pltpu.VMEM((2, share, width), BF16),
        pltpu.VMEM((members, 8, LANES), F32),
        pltpu.VMEM((voxels, LANES), F32),
        pltpu.VMEM((1, slabs, deep, width), BF16),
        pltpu.VMEM((1, slabs, deep, width), BF16),
        pltpu.VMEM((members, mine, LANES), BF16),
        pltpu.VMEM((members, mine, LANES), BF16),
        pltpu.SemaphoreType.DMA((9,)),
        pltpu.SemaphoreType.DMA((7,)),
        pltpu.SemaphoreType.DMA((7,)),
        pltpu.SemaphoreType.DMA((60,)),
        pltpu.SemaphoreType.DMA((60,)),
    ]
    density, posterior = pl.pallas_call(
        functools.partial(kernel, slabs, members),
        out_shape=(
            jax.ShapeDtypeStruct((planes, edge // members, edge), F32),
            jax.ShapeDtypeStruct((cands, particles), F32),
        ),
        in_specs=[big] * 9,
        out_specs=(near, near),
        scratch_shapes=scratch,
        compiler_params=pltpu.CompilerParams(
            collective_id=0, has_side_effects=True, vmem_limit_bytes=56 * 1024 * 1024
        ),
    )(
        images, volume.reshape(voxels, width), column_table(edge, members), row_table(edge),
        precision[None, :], candidates.T, slot_key, slot_voxel, slot_weight,
    )
    return density.transpose(0, 2, 1), posterior.T


def solution(mesh):
    placed = (P("img", "slab"), P("slab", None, None), P("img"), P("img", None), P(), P(), P())
    return jax.shard_map(
        per_device,
        mesh=mesh,
        in_specs=placed,
        out_specs=(P("slab", None, "img"), P("img", None)),
        check_vma=False,
    )
```

time: 240 us -> 70 us (0.29)
  waiting for transfers between devices: 101 us -> 0 us
  Pallas kernels: 0 us -> 65.9 us
  other arithmetic: 38.9 us -> 0 us
  blocking collectives: 34.4 us -> 0 us
  matrix products: 27.4 us -> 0 us
  starting transfers between devices: 17.6 us -> 0 us
  between operations: 14.3 us -> 0.64 us
  local copies, waits for them, and re-layouts: 6.05 us -> 3.24 us
    psum x1 -> x0, waiting for transfers between devices: 80.5 us -> none  [per_device(): picked = lax.psum(picked, 'slab') * precision[None, :]]
    pallas_call x0 -> x1, Pallas kernels: none -> 65.9 us  [per_device(): pl.pallas_call(functools.partial(kernel, slabs, members), out_shape=(jax....]
    reduce_sum x11 -> x0, other arithmetic: 34.6 us -> none  [the longest x1 14.8 us: per_device(): row_weight = jnp.sum(spread.astype(jnp.float32), axis=1)]
    dot_general x8 -> x0, matrix products: 27.4 us -> none  [the longest x1 14.3 us: per_device(): lax.dot_general(slices, images, (((1,), (1,)), ((), ())), preferred_eleme...]
    all_to_all x1 -> x0, blocking collectives: 21.3 us -> none  [per_device(): lax.all_to_all(back.reshape(members, share, width), 'img', 0, 0, tiled=True)]
    all_to_all x3 -> x0, starting transfers between devices: 17.5 us -> none  [the longest x1 8.6 us: per_device(): lax.all_to_all(outgoing.reshape(slabs, deep, width), 'slab', 0, 0, tiled=...]
    psum x1 -> x0, blocking collectives: 13.1 us -> none  [per_device(): pose_weight = lax.psum(pose_weight, 'img')]
    all_to_all x3 -> x0, waiting for transfers between devices: 10.6 us -> none  [the longest x1 5.47 us: per_device(): lax.all_to_all(turned, 'img', 0, 0, tiled=True)]
  transfers between devices with their start and end apart: 5 -> 0, of which waited for: 4 -> 0; matrix products, arithmetic and copies ran while one was open for 7% -> 0% of each run, Pallas kernels for 0% -> 0%
where the time goes in v7:
time: 70 us; the launch traced here: 69.8 us
  Pallas kernels  65.9 us (94%)
  local copies, waits for them, and re-layouts  3.24 us (5%)
    pallas_call x1, Pallas kernels, per_device(): pl.pallas_call(functools.partial(kernel, slabs, members), out_shape=(jax....  65.9 us
    unnamed x2, local copies, waits for them, and re-layouts  3.24 us

profile of v7, /device:TPU:1, one launch (start us, length us, event | category | flops | bytes accessed | tf_op | source)
XLA Modules:
  0.0 69.8 jit_solution(6386747979270227628)
XLA Ops:
  0.6 65.9 %shard_map.104 = (f32[2,64,512]{2,1,0:T(8,128)}, f32[16,2048]{1,0:T(8,128)}) custom-call(bf16[2048,1024]{1,0:T(8,128)(2,1)} %images.1, bf16[1024,1024]{1,0:T(8,128)(2,1)} %bitcast.5, bf16[1024,1024]{1,0:T(8,128)(2,1)} %constant.4.clone.columns, bf16[512,1024]{1,0:T(8,128)(2,1)} %constant.5.clone.rows, f32[1,2048]{1,0:T(1,128)} %bitcast.9, ...), custom_call_target="tpu_custom_call" | custom-call | tf_op jit(solution)/shard_map/pallas_call | solution.py:709
  66.6 1.7 %copy.13 = f32[2,512,64]{1,2,0:T(8,128)} copy(f32[2,512,64]{1,2,0:T(8,128)} %bitcast.6) | data formatting | bytes 524288
  68.2 1.6 %copy.14 = f32[2048,16]{0,1:T(8,128)} copy(f32[2048,16]{0,1:T(8,128)} %bitcast.8) | data formatting | bytes 262144

commit v8 on v6

--- a/solution.py
+++ b/solution.py
@@ -81,9 +81,9 @@
 
 def kernel(
     slabs, members,
-    images, volume, columns, rows, precision_in, poses_in, keys_in, voxels_in, weights_in,
-    density, posterior,
-    images_v, volume_v, columns_v, rows_v, precision, poses, keys, voxel_of, weight_of,
+    images, volume, columns, precision_in, poses_in, keys_in, voxels_in, weights_in,
+    fourier, shares_out,
+    images_v, volume_v, columns_v, precision, poses, keys, voxel_of, weight_of,
     slot_table, pack_table, pose_row,
     outgoing, incoming, slices, half_power, ranks, weave,
     picks, picks_in, shares, spread, row_weight, partial,
@@ -119,11 +119,20 @@
     def greet(axis, peer):
         pl.semaphore_signal(barrier, inc=1, device_id={axis: peer}, device_id_type=pl.DeviceIdType.MESH)
 
-    sources = [keys_in, voxels_in, weights_in, volume, poses_in, images, precision_in, columns, rows]
-    targets = [keys, voxel_of, weight_of, volume_v, poses, images_v, precision, columns_v, rows_v]
+    sources = [keys_in, voxels_in, weights_in, volume, poses_in, images, precision_in, columns]
+    targets = [keys, voxel_of, weight_of, volume_v, poses, images_v, precision, columns_v]
     load = [pltpu.make_async_copy(src, dst, loads.at[i]) for i, (src, dst) in enumerate(zip(sources, targets))]
+
+    def start_load(index):
+        src, dst = sources[index], targets[index]
+        pieces = 8 if src.shape[0] >= 512 else 1
+        size = src.shape[0] // pieces
+        for piece in range(pieces):
+            at = slice(piece * size, (piece + 1) * size)
+            pltpu.make_async_copy(src.at[at], dst.at[at], loads.at[index]).start()
+
     for index in range(5):
-        load[index].start()
+        start_load(index)
     for step in range(1, slabs):
         greet("slab", slab_peer(step))
     for step in range(1, members):
@@ -171,7 +180,7 @@
     take = jnp.where(place == spot, own_cols[:, 1:2], 0.0) + jnp.where(place == spot + 1, own_cols[:, 2:3], 0.0)
     load[3].wait()
     for index in range(5, len(load)):
-        load[index].start()
+        start_load(index)
     woven = dot(take.astype(BF16), volume_v[...])
     for block in range(slabs):
         outgoing[block] = woven[block * deep : (block + 1) * deep].astype(BF16)
@@ -352,25 +361,28 @@
     def near_step(index):
         score_chunk(index, slices[share : NPOSE - share, :], [(share, 0, NPOSE - 2 * share)], False)
 
+    def far_chunk(index):
+        table = jnp.concatenate([slices[0:share, :], slices[NPOSE - share : NPOSE, :]], axis=0)
+        score_chunk(index, table, [(0, 0, share), (NPOSE - share, share, share)], True)
+
+    def full_chunk(index):
+        score_chunk(index, slices[...], [(0, 0, NPOSE)], False)
+
     gathers[2].wait_recv()
     gathers[7].wait_recv()
     gathers[8].wait_recv()
     each(members - 1, power_step, 1)
-    each(chunks // 2, near_step)
+    each(chunks // 4, near_step)
     gathers[5].wait_recv()
     gathers[9].start()
     gathers[6].wait_recv()
     gathers[10].start()
-    each(chunks, near_step, chunks // 2)
+    each(chunks // 2, near_step, chunks // 4)
     gathers[9].wait_recv()
     gathers[10].wait_recv()
     power_step(0)
     power_step(members - 1)
 
-    def far_chunk(index):
-        table = jnp.concatenate([slices[0:share, :], slices[NPOSE - share : NPOSE, :]], axis=0)
-        score_chunk(index, table, [(0, 0, share), (NPOSE - share, share, share)], True)
-
     def pick_send(peer):
         @pl.when(peer != own)
         def _():
@@ -381,7 +393,13 @@
         pick_send(2 * index)
         pick_send(2 * index + 1)
 
-    each(chunks, far_step)
+    def full_step(index):
+        full_chunk(index)
+        pick_send(2 * index)
+        pick_send(2 * index + 1)
+
+    each(chunks // 2, far_step)
+    each(chunks, full_step, chunks // 2)
     picks_in[own] = picks[own]
     load[6].wait()
     row_weight[...] = jnp.zeros_like(row_weight)
@@ -542,8 +560,8 @@
     ring_start(0)
     ring_relay(0)
     ring_finish(0)
-    for block in range(slabs):
-        posterior[:, block * LANES : (block + 1) * LANES] = shares[block]
+    shares_copy = pltpu.make_async_copy(shares, shares_out, loads.at[8])
+    shares_copy.start()
 
     img_whole(16, masses).wait_recv()
     mass_sum = masses[0]
@@ -571,7 +589,6 @@
 
     each(voxels // LANES, mass_step)
     load[7].wait()
-    load[8].wait()
 
     turned = jnp.zeros((mine, width), F32)
     for part in range(halves):
@@ -602,15 +619,21 @@
     img_whole(17, crossed).wait_recv()
 
     voxel_rows = dot(weave[...], crossed[...].reshape(members * LANES, LANES)) * inverse[...]
-    fourier = voxel_rows.astype(BF16)
+    fourier[...] = voxel_rows.astype(BF16)
+    shares_copy.wait()
+    img_whole(17, crossing).wait_send()
+
+
+def finish(rows, fourier, shares, density, posterior):
     edge = density.shape[2]
     columns_out = density.shape[1]
     for plane in range(density.shape[0]):
-        field = fourier[plane * edge : (plane + 1) * edge]
-        real = dot(rows_v[:, :edge], field)
-        imag = dot(rows_v[:, edge:], field)
+        field = fourier[plane * edge : (plane + 1) * edge, :]
+        real = dot(rows[:, :edge], field)
+        imag = dot(rows[:, edge:], field)
         density[plane] = (real[:, :columns_out] + imag[:, columns_out:]).T
-    img_whole(17, crossing).wait_send()
+    for block in range(shares.shape[0]):
+        posterior[:, block * LANES : (block + 1) * LANES] = shares[block]
 
 
 def per_device(images, volume, precision, candidates, slot_key, slot_voxel, slot_weight):
@@ -630,7 +653,6 @@
         pltpu.VMEM((particles, width), BF16),
         pltpu.VMEM((voxels, width), BF16),
         pltpu.VMEM((width, width), BF16),
-        pltpu.VMEM((edge, 2 * edge), BF16),
         pltpu.VMEM((1, particles), F32),
         pltpu.VMEM((cands, particles), jnp.int32),
         pltpu.VMEM(slot_key.shape, jnp.int32),
@@ -670,22 +692,32 @@
         pltpu.SemaphoreType.DMA((60,)),
         pltpu.SemaphoreType.DMA((60,)),
     ]
-    density, posterior = pl.pallas_call(
+    fourier, shares = pl.pallas_call(
         functools.partial(kernel, slabs, members),
         out_shape=(
-            jax.ShapeDtypeStruct((planes, edge // members, edge), F32),
-            jax.ShapeDtypeStruct((cands, particles), F32),
+            jax.ShapeDtypeStruct((voxels, LANES), BF16),
+            jax.ShapeDtypeStruct((slabs, cands, LANES), F32),
         ),
-        in_specs=[big] * 9,
-        out_specs=(near, near),
+        in_specs=[big] * 8,
+        out_specs=(near, big),
         scratch_shapes=scratch,
         compiler_params=pltpu.CompilerParams(
             collective_id=0, has_side_effects=True, vmem_limit_bytes=56 * 1024 * 1024
         ),
     )(
-        images, volume.reshape(voxels, width), column_table(edge, members), row_table(edge),
+        images, volume.reshape(voxels, width), column_table(edge, members),
         precision[None, :], candidates.T, slot_key, slot_voxel, slot_weight,
     )
+    density, posterior = pl.pallas_call(
+        finish,
+        out_shape=(
+            jax.ShapeDtypeStruct((planes, edge // members, edge), F32),
+            jax.ShapeDtypeStruct((cands, particles), F32),
+        ),
+        in_specs=[near] * 3,
+        out_specs=(near, near),
+        compiler_params=pltpu.CompilerParams(vmem_limit_bytes=56 * 1024 * 1024),
+    )(row_table(edge), fourier, shares)
     return density.transpose(0, 2, 1), posterior.T
 
 

time: 71.7 us -> 68 us (0.948)
  local copies, waits for them, and re-layouts: 3.24 us -> 0 us
    pallas_call x1, Pallas kernels: 67.6 us -> 64.2 us  [per_device(): pl.pallas_call(functools.partial(kernel, slabs, members), out_shape=(jax....]
    unnamed x2 -> x0, local copies, waits for them, and re-layouts: 3.24 us -> none
    pallas_call x0 -> x1, Pallas kernels: none -> 2.92 us  [per_device(): pl.pallas_call(finish, out_shape=(jax.ShapeDtypeStruct((planes, edge // m...]
where the time goes in v8:
time: 68 us; the launch traced here: 67.8 us
  Pallas kernels  67.1 us (99%)
    pallas_call x1, Pallas kernels, per_device(): pl.pallas_call(functools.partial(kernel, slabs, members), out_shape=(jax....  64.2 us
    pallas_call x1, Pallas kernels, per_device(): pl.pallas_call(finish, out_shape=(jax.ShapeDtypeStruct((planes, edge // m...  2.92 us

profile of v8, /device:TPU:1, one launch (start us, length us, event | category | flops | bytes accessed | tf_op | source)
XLA Modules:
  0.0 67.8 jit_solution(14399518024073407670)
XLA Ops:
  0.6 64.2 %shard_map.104 = (bf16[1024,128]{1,0:T(8,128)(2,1)}, f32[16,16,128]{2,1,0:T(8,128)}) custom-call(bf16[2048,1024]{1,0:T(8,128)(2,1)} %images.1, bf16[1024,1024]{1,0:T(8,128)(2,1)} %bitcast.5, bf16[1024,1024]{1,0:T(8,128)(2,1)} %constant.4.clone.columns, f32[1,2048]{1,0:T(1,128)} %bitcast.7, s32[16,2048]{1,0:T(8,128)} %bitcast.6, s32[16,16,64]{2,1,0:T(8,128)} %keys_in.1, ...), custom_call_target="tpu_custom_call" | custom-call | tf_op jit(solution)/shard_map/pallas_call | solution.py:695
  64.9 2.9 %shard_map.105 = (f32[2,64,512]{2,1,0:T(8,128)}, f32[16,2048]{1,0:T(8,128)}) custom-call(bf16[512,1024]{1,0:T(8,128)(2,1)} %constant.5.clone.rows, bf16[1024,128]{1,0:T(8,128)(2,1)} %get-tuple-element.6.fourier, f32[16,16,128]{2,1,0:T(8,128)} %get-tuple-element.7.shares), custom_call_target="tpu_custom_call" | custom-call | tf_op jit(solution)/shard_map/pallas_call | solution.py:711

commit v9 on v8

--- a/solution.py
+++ b/solution.py
@@ -40,8 +40,8 @@
 
 def row_table(length):
     turn = angles(length)
-    scale = gridding(length)[:, None] / length
-    return jnp.asarray(np.concatenate([np.cos(turn), -np.sin(turn)], axis=1) * scale, BF16)
+    scale = gridding(length)[None, :] / length
+    return jnp.asarray(np.concatenate([np.cos(turn), -np.sin(turn)], axis=0) * scale, BF16)
 
 
 def remote(src, dst, sends, recvs, device):
@@ -86,7 +86,7 @@
     images_v, volume_v, columns_v, precision, poses, keys, voxel_of, weight_of,
     slot_table, pack_table, pose_row,
     outgoing, incoming, slices, half_power, ranks, weave,
-    picks, picks_in, shares, spread, row_weight, partial,
+    picks, picks_in, shares, spread_first, spread_middle, spread_last, row_weight, partial,
     away, away_in, kept, opposite, opposite_in, ring, ring_in,
     masses, inverse, returning, returned, crossing, crossed,
     loads, slab_send, slab_recv, img_send, img_recv,
@@ -252,8 +252,10 @@
                 renamed = jnp.where(high == piece, found, renamed)
             poses[at] = renamed
 
-    ahead_of = slabs // 2
-    turn = own // ahead_of
+    first_chunks = 3
+    ahead_of = 2 * first_chunks
+    middle = (slabs + ahead_of) // 2
+    turn = jnp.where(own >= ahead_of, 1, 0)
 
     def rank_chunk(block):
         at = rows_at(block * LANES, LANES)
@@ -303,12 +305,14 @@
         gathers[index].start()
 
     def weave_step(index):
-        at = iota((LANES, total_slots), 0) + index * LANES
-        spots = slot_table[0:1, :].astype(jnp.int32)
-        value = jnp.where(spots == at, slot_table[1:2, :], 0.0) + jnp.where(spots + 1 == at, slot_table[2:3, :], 0.0)
-        weave[rows_at(index * LANES, LANES), :] = value.astype(BF16)
-
-    each(voxels // LANES, weave_step)
+        at = rows_at(index * LANES, LANES)
+        cols = slot_table[:, at].T
+        spots = cols[:, 0:1].astype(jnp.int32)
+        voxel = iota((LANES, voxels), 1)
+        value = jnp.where(voxel == spots, cols[:, 1:2], 0.0) + jnp.where(voxel == spots + 1, cols[:, 2:3], 0.0)
+        weave[at, :] = value.astype(BF16)
+
+    each(total_slots // LANES, weave_step)
     gathers[0].wait_recv()
     gathers[5].start()
     gathers[1].wait_recv()
@@ -372,12 +376,12 @@
     gathers[7].wait_recv()
     gathers[8].wait_recv()
     each(members - 1, power_step, 1)
-    each(chunks // 4, near_step)
+    each(first_chunks - 1, near_step)
     gathers[5].wait_recv()
     gathers[9].start()
     gathers[6].wait_recv()
     gathers[10].start()
-    each(chunks // 2, near_step, chunks // 4)
+    each(first_chunks, near_step, first_chunks - 1)
     gathers[9].wait_recv()
     gathers[10].wait_recv()
     power_step(0)
@@ -398,8 +402,8 @@
         pick_send(2 * index)
         pick_send(2 * index + 1)
 
-    each(chunks // 2, far_step)
-    each(chunks, full_step, chunks // 2)
+    each(first_chunks, far_step)
+    each(chunks, full_step, first_chunks)
     picks_in[own] = picks[own]
     load[6].wait()
     row_weight[...] = jnp.zeros_like(row_weight)
@@ -429,16 +433,19 @@
         share_out()
 
     def shares_arrive(which):
+        group = ahead_of if which == 0 else slabs - ahead_of
+
         @pl.when(turn == which)
         def _():
-            slab_whole(5 + which, shares, ahead_of - 1).wait_recv()
+            slab_whole(5 + which, shares, group - 1).wait_recv()
 
         @pl.when(turn != which)
         def _():
-            slab_whole(5 + which, shares, ahead_of).wait_recv()
-
-    def spread_chunk(block):
+            slab_whole(5 + which, shares, group).wait_recv()
+
+    def spread_chunk(block, spread, origin):
         at = rows_at(block * LANES, LANES)
+        to = rows_at((block - origin) * LANES, LANES)
         amount = shares[block] * precision[:, at]
         rounded = amount.astype(BF16).astype(F32)
         low, high = rounded[0:8], rounded[8:16]
@@ -452,7 +459,7 @@
                 value = jnp.where(rank < 8, from_low, jnp.where(rank < cands, from_high, 0.0))
                 row_weight[group : group + 8, :] += value
                 values.append(value)
-            spread[first : first + 16, at] = jnp.concatenate(values, axis=0).astype(BF16)
+            spread[first : first + 16, to] = jnp.concatenate(values, axis=0).astype(BF16)
 
     stripe = 2 * LANES
     halves = 1
@@ -465,7 +472,7 @@
 
     def back_stripe(index):
         at = slice(index * stripe, (index + 1) * stripe)
-        part = partial[:, at] + dot(spread[:, early:], images_v[early:, at])
+        part = partial[:, at] + dot(spread_last[...], images_v[middle * LANES :, at])
         away[:, at] = part[side:].astype(BF16)
         away_copy(index).start()
         kept[:, at] = part[:side]
@@ -529,17 +536,21 @@
         slab_exchange(3 + part, returning.at[part], returned.at[part])
         returned[part, own] = returning[part, own]
 
-    early = images_v.shape[0] // 2
-
     def early_stripe(index):
         at = rows_at(index * stripe, stripe)
-        partial[:, at] = dot(spread[:, :early], images_v[:early, at])
+        partial[:, at] = dot(spread_first[...], images_v[: ahead_of * LANES, at])
 
     shares_arrive(0)
-    each(ahead_of, spread_chunk)
+    each(ahead_of, lambda block: spread_chunk(block, spread_first, 0))
     each(width // stripe, early_stripe)
     shares_arrive(1)
-    each(slabs, spread_chunk, ahead_of)
+    each(middle, lambda block: spread_chunk(block, spread_middle, ahead_of), ahead_of)
+    waiting = list(range(middle, slabs))
+    for index in range(width // stripe):
+        at = slice(index * stripe, (index + 1) * stripe)
+        partial[:, at] += dot(spread_middle[...], images_v[ahead_of * LANES : middle * LANES, at])
+        for block in waiting[index :: width // stripe]:
+            spread_chunk(block, spread_last, middle)
 
     weight = jnp.sum(row_weight[...], axis=1, keepdims=True)
     mass_row = pick_row(iota((NPOSE, NPOSE), 0) == pose_row[0:1, :], weight)
@@ -567,27 +578,16 @@
     mass_sum = masses[0]
     for index in range(1, members):
         mass_sum = mass_sum + masses[index]
-    mass_total = jnp.concatenate([mass_sum[piece : piece + 1] for piece in range(NPOSE // LANES)], axis=1)
-    lanes = iota((LANES, LANES), 1)
-    mass_cols = []
-    for block in range(members):
-        key_col = slot_table[:, block * LANES : (block + 1) * LANES].T[:, 3:4]
-        matched = key_col == iota((LANES, NPOSE), 1).astype(F32)
-        amount = jnp.sum(jnp.where(matched, mass_total, 0.0), axis=1, keepdims=True)
-        first = amount.astype(BF16).astype(F32)
-        second = (amount - first).astype(BF16).astype(F32)
-        third = amount - first - second
-        mass_cols.append(
-            jnp.where(lanes == 0, first, jnp.where(lanes == 1, second, jnp.where(lanes == 2, third, 0.0))).astype(BF16)
-        )
-    mass_table = jnp.concatenate(mass_cols, axis=0)
-
-    def mass_step(index):
-        at = rows_at(index * LANES, LANES)
-        mass = jnp.sum(dot(weave[at, :], mass_table), axis=1, keepdims=True)
-        inverse[at, :] = jnp.broadcast_to(1.0 / (mass + RIDGE), (LANES, LANES))
-
-    each(voxels // LANES, mass_step)
+    mass_cols = mass_sum.T
+    amount = jnp.zeros((1, total_slots), F32)
+    for piece in range(NPOSE // LANES):
+        pose = (iota((LANES, total_slots), 0) + piece * LANES).astype(F32)
+        amount += pick_row(slot_table[3:4, :] == pose, mass_cols[:, piece : piece + 1])
+    first = amount.astype(BF16).astype(F32)
+    second = (amount - first).astype(BF16).astype(F32)
+    pieces = [first, second, amount - first - second, jnp.zeros((13, total_slots), F32)]
+    mass = dot(jnp.concatenate(pieces, axis=0).astype(BF16), weave[...])
+    inverse[...] = 1.0 / (jnp.sum(mass, axis=0, keepdims=True) + RIDGE)
     load[7].wait()
 
     turned = jnp.zeros((mine, width), F32)
@@ -596,7 +596,7 @@
         gathered = jnp.concatenate([returned[part, block].astype(F32) for block in range(slabs)], axis=0)
         turned += dot(gathered.astype(BF16), columns_v[columns_of(part), :])
     for block in range(members):
-        crossing[block] = turned[:, block * LANES : (block + 1) * LANES].astype(BF16)
+        crossing[block] = turned[:, block * LANES : (block + 1) * LANES].T.astype(BF16)
 
     def cross_copy(step):
         peer = img_peer(step)
@@ -618,20 +618,19 @@
     img_whole(16, masses).wait_send()
     img_whole(17, crossed).wait_recv()
 
-    voxel_rows = dot(weave[...], crossed[...].reshape(members * LANES, LANES)) * inverse[...]
-    fourier[...] = voxel_rows.astype(BF16)
+    slots = jnp.concatenate([crossed[block] for block in range(members)], axis=1)
+    fourier[...] = (dot(slots, weave[...]) * inverse[...]).astype(BF16)
     shares_copy.wait()
     img_whole(17, crossing).wait_send()
 
 
 def finish(rows, fourier, shares, density, posterior):
-    edge = density.shape[2]
-    columns_out = density.shape[1]
-    for plane in range(density.shape[0]):
-        field = fourier[plane * edge : (plane + 1) * edge, :]
-        real = dot(rows[:, :edge], field)
-        imag = dot(rows[:, edge:], field)
-        density[plane] = (real[:, :columns_out] + imag[:, columns_out:]).T
+    planes, columns_out, edge = density.shape
+    real = jnp.concatenate([fourier[:columns_out, z * edge : (z + 1) * edge] for z in range(planes)], axis=0)
+    imag = jnp.concatenate([fourier[columns_out:, z * edge : (z + 1) * edge] for z in range(planes)], axis=0)
+    value = dot(real, rows[:edge, :]) + dot(imag, rows[edge:, :])
+    for z in range(planes):
+        density[z] = value[z * columns_out : (z + 1) * columns_out]
     for block in range(shares.shape[0]):
         posterior[:, block * LANES : (block + 1) * LANES] = shares[block]
 
@@ -666,11 +665,13 @@
         pltpu.VMEM((NPOSE, width), BF16),
         pltpu.VMEM((NPOSE, LANES), F32),
         pltpu.VMEM((NPOSE, particles), jnp.int32),
-        pltpu.VMEM((voxels, slabs * cap), BF16),
+        pltpu.VMEM((slabs * cap, voxels), BF16),
         pltpu.VMEM((slabs, cands, LANES), F32),
         pltpu.VMEM((slabs, cands, LANES), F32),
         pltpu.VMEM((slabs, cands, LANES), F32),
-        pltpu.VMEM((NPOSE, particles), BF16),
+        pltpu.VMEM((NPOSE, 6 * LANES), BF16),
+        pltpu.VMEM((NPOSE, 5 * LANES), BF16),
+        pltpu.VMEM((NPOSE, 5 * LANES), BF16),
         pltpu.VMEM((NPOSE, LANES), F32),
         pltpu.VMEM((NPOSE, width), F32),
         pltpu.VMEM((side, width), BF16),
@@ -681,7 +682,7 @@
         pltpu.VMEM((2, share, width), BF16),
         pltpu.VMEM((2, share, width), BF16),
         pltpu.VMEM((members, 8, LANES), F32),
-        pltpu.VMEM((voxels, LANES), F32),
+        pltpu.VMEM((1, voxels), F32),
         pltpu.VMEM((1, slabs, deep, width), BF16),
         pltpu.VMEM((1, slabs, deep, width), BF16),
         pltpu.VMEM((members, mine, LANES), BF16),
@@ -695,7 +696,7 @@
     fourier, shares = pl.pallas_call(
         functools.partial(kernel, slabs, members),
         out_shape=(
-            jax.ShapeDtypeStruct((voxels, LANES), BF16),
+            jax.ShapeDtypeStruct((LANES, voxels), BF16),
             jax.ShapeDtypeStruct((slabs, cands, LANES), F32),
         ),
         in_specs=[big] * 8,

time: 68 us -> 66.9 us (0.984)
  Pallas kernels: 67.1 us -> 66.1 us
where the time goes in v9:
time: 66.9 us; the launch traced here: 66.8 us
  Pallas kernels  66.1 us (99%)
    pallas_call x1, Pallas kernels, per_device(): pl.pallas_call(functools.partial(kernel, slabs, members), out_shape=(jax....  63.8 us
    pallas_call x1, Pallas kernels, per_device(): pl.pallas_call(finish, out_shape=(jax.ShapeDtypeStruct((planes, edge // m...  2.34 us

profile of v9, /device:TPU:1, one launch (start us, length us, event | category | flops | bytes accessed | tf_op | source)
XLA Modules:
  0.0 66.8 jit_solution(9947335504644738952)
XLA Ops:
  0.6 63.8 %shard_map.104 = (bf16[128,1024]{1,0:T(8,128)(2,1)}, f32[16,16,128]{2,1,0:T(8,128)}) custom-call(bf16[2048,1024]{1,0:T(8,128)(2,1)} %images.1, bf16[1024,1024]{1,0:T(8,128)(2,1)} %bitcast.5, bf16[1024,1024]{1,0:T(8,128)(2,1)} %constant.4.clone.columns, f32[1,2048]{1,0:T(1,128)} %bitcast.7, s32[16,2048]{1,0:T(8,128)} %bitcast.6, s32[16,16,64]{2,1,0:T(8,128)} %keys_in.1, ...), custom_call_target="tpu_custom_call" | custom-call | tf_op jit(solution)/shard_map/pallas_call | solution.py:696
  64.4 2.3 %shard_map.105 = (f32[2,64,512]{2,1,0:T(8,128)}, f32[16,2048]{1,0:T(8,128)}) custom-call(bf16[1024,512]{1,0:T(8,128)(2,1)} %constant.5.clone.rows, bf16[128,1024]{1,0:T(8,128)(2,1)} %get-tuple-element.6.fourier, f32[16,16,128]{2,1,0:T(8,128)} %get-tuple-element.7.shares), custom_call_target="tpu_custom_call" | custom-call | tf_op jit(solution)/shard_map/pallas_call | solution.py:712

commit v10 on v9

--- a/solution.py
+++ b/solution.py
@@ -84,11 +84,11 @@
     images, volume, columns, precision_in, poses_in, keys_in, voxels_in, weights_in,
     fourier, shares_out,
     images_v, volume_v, columns_v, precision, poses, keys, voxel_of, weight_of,
-    slot_table, pack_table, pose_row,
+    pack_table, pose_row, named, unpack,
     outgoing, incoming, slices, half_power, ranks, weave,
-    picks, picks_in, shares, spread_first, spread_middle, spread_last, row_weight, partial,
+    picks, picks_in, shares, spread_first, spread_middle, spread_last, row_weight, partial, back,
     away, away_in, kept, opposite, opposite_in, ring, ring_in,
-    masses, inverse, returning, returned, crossing, crossed,
+    masses, inverse, returning, returned,
     loads, slab_send, slab_recv, img_send, img_recv,
 ):
     own = lax.axis_index("slab")
@@ -206,11 +206,6 @@
     slab_exchange(0, outgoing, incoming)
     incoming[own] = outgoing[own]
 
-    code, key_row = ordered(0, total_slots, [own_code, own_key])
-    for index, value in enumerate(decoded(code) + (key_row,)):
-        slot_table[index : index + 1, :] = value
-    slot_table[4:8, :] = jnp.zeros((4, total_slots), F32)
-
     in_key = jnp.concatenate(
         [jnp.sum(jnp.where(iota((slabs, cap), 0) == own, keys[slab], 0), axis=0, keepdims=True) for slab in range(slabs)],
         axis=0,
@@ -236,7 +231,9 @@
     pose_ids = iota((cap, NPOSE), 1).astype(F32)
     found_rows = jnp.zeros((cap, NPOSE), F32)
     for slab in range(slabs):
-        found_rows += jnp.where(key_cols[:, slab : slab + 1] == pose_ids, row_cols[:, slab : slab + 1], 0.0)
+        matched = key_cols[:, slab : slab + 1] == pose_ids
+        found_rows += jnp.where(matched, row_cols[:, slab : slab + 1], 0.0)
+        unpack[slab * cap : (slab + 1) * cap, :] = jnp.where(matched, 1.0, 0.0).astype(BF16)
     pose_row[...] = jnp.broadcast_to(jnp.sum(found_rows, axis=0, keepdims=True), (8, NPOSE)).astype(jnp.int32)
 
     load[4].wait()
@@ -250,7 +247,7 @@
                 table = pose_row[:, piece * LANES : (piece + 1) * LANES]
                 found = jnp.take_along_axis(table, low, axis=1, mode="promise_in_bounds")
                 renamed = jnp.where(high == piece, found, renamed)
-            poses[at] = renamed
+            named[at] = renamed
 
     first_chunks = 3
     ahead_of = 2 * first_chunks
@@ -267,7 +264,7 @@
                 value = jnp.where(number[k : k + 1] == row, jnp.int16(k), value)
             ranks[first : first + LANES, at] = value.astype(jnp.int32)
 
-    each(slabs, rank_chunk, ahead_of)
+    each(middle, rank_chunk, ahead_of)
 
     slab_arrivals(0, incoming)
     arrived = jnp.concatenate([incoming[block].astype(F32) for block in range(slabs)], axis=0).astype(BF16)
@@ -304,15 +301,7 @@
     for index in range(5):
         gathers[index].start()
 
-    def weave_step(index):
-        at = rows_at(index * LANES, LANES)
-        cols = slot_table[:, at].T
-        spots = cols[:, 0:1].astype(jnp.int32)
-        voxel = iota((LANES, voxels), 1)
-        value = jnp.where(voxel == spots, cols[:, 1:2], 0.0) + jnp.where(voxel == spots + 1, cols[:, 2:3], 0.0)
-        weave[at, :] = value.astype(BF16)
-
-    each(total_slots // LANES, weave_step)
+    each(slabs, rank_chunk, middle)
     gathers[0].wait_recv()
     gathers[5].start()
     gathers[1].wait_recv()
@@ -352,7 +341,7 @@
             (((1,), (1,)), ((), ())), preferred_element_type=F32,
         )
         for part in range(chunk // LANES):
-            number = poses[:, rows_at(index * chunk + part * LANES, LANES)]
+            number = named[:, rows_at(index * chunk + part * LANES, LANES)]
             numbers = [number[0:8] & 7, number[8:16] & 7, number[0:8] >> 3, number[8:16] >> 3]
             block = index * (chunk // LANES) + part
             if resume:
@@ -462,79 +451,6 @@
             spread[first : first + 16, to] = jnp.concatenate(values, axis=0).astype(BF16)
 
     stripe = 2 * LANES
-    halves = 1
-    wide = width // halves
-    per_half = wide // stripe
-
-    def away_copy(index):
-        at = slice(index * stripe, (index + 1) * stripe)
-        return img_copy(40 + index, away.at[:, at], away_in.at[:, at], partner)
-
-    def back_stripe(index):
-        at = slice(index * stripe, (index + 1) * stripe)
-        part = partial[:, at] + dot(spread_last[...], images_v[middle * LANES :, at])
-        away[:, at] = part[side:].astype(BF16)
-        away_copy(index).start()
-        kept[:, at] = part[:side]
-
-    def columns_of(part):
-        return slice(part * wide, (part + 1) * wide)
-
-    def kept_part(index, part, first=0, size=share):
-        here = index * share + first
-        there = (ring_len - 1 - index) * share + first
-        at = columns_of(part)
-        return kept[here : here + size, at] + away_in[there : there + size, at].astype(F32)
-
-    def ring_copy(part, index):
-        at = columns_of(part)
-        low, high = slice(0, half), slice(half, share)
-        refs = [
-            (opposite.at[low, at], opposite_in.at[low, at], right),
-            (opposite.at[high, at], opposite_in.at[high, at], left),
-            (ring.at[0, high, at], ring_in.at[0, high, at], right),
-            (ring.at[1, low, at], ring_in.at[1, low, at], left),
-            (ring.at[0, low, at], ring_in.at[0, low, at], right),
-            (ring.at[1, high, at], ring_in.at[1, high, at], left),
-        ]
-        return img_copy(48 + 6 * part + index, *refs[index])
-
-    def ring_start(part):
-        at = columns_of(part)
-        for index in range(part * per_half, (part + 1) * per_half):
-            away_copy(index).wait_recv()
-        opposite[:, at] = kept_part(FAR, part).astype(BF16)
-        ring_copy(part, 0).start()
-        ring_copy(part, 1).start()
-        ring[0, half:share, at] = kept_part(RIGHT, part, half, half).astype(BF16)
-        ring_copy(part, 2).start()
-        ring[1, 0:half, at] = kept_part(LEFT, part, 0, half).astype(BF16)
-        ring_copy(part, 3).start()
-
-    def ring_relay(part):
-        at = columns_of(part)
-        ring_copy(part, 0).wait_recv()
-        ring[0, 0:half, at] = (kept_part(RIGHT, part, 0, half) + opposite_in[0:half, at].astype(F32)).astype(BF16)
-        ring_copy(part, 4).start()
-        ring_copy(part, 1).wait_recv()
-        ring[1, half:share, at] = (
-            kept_part(LEFT, part, half, half) + opposite_in[half:share, at].astype(F32)
-        ).astype(BF16)
-        ring_copy(part, 5).start()
-
-    unpack = jnp.where(pack_table[...].T[:, 0:1] == iota((mine, share), 1).astype(F32), 1.0, 0.0).astype(BF16)
-
-    def ring_finish(part):
-        at = columns_of(part)
-        held = kept_part(HOME, part)
-        for index in range(2, 6):
-            ring_copy(part, index).wait_recv()
-        summed = (held + ring_in[0, :, at].astype(F32) + ring_in[1, :, at].astype(F32)).astype(BF16)
-        unpacked = dot(unpack, summed)
-        for block in range(slabs):
-            returning[part, block] = unpacked[block * deep : (block + 1) * deep].astype(BF16)
-        slab_exchange(3 + part, returning.at[part], returned.at[part])
-        returned[part, own] = returning[part, own]
 
     def early_stripe(index):
         at = rows_at(index * stripe, stripe)
@@ -552,10 +468,9 @@
         for block in waiting[index :: width // stripe]:
             spread_chunk(block, spread_last, middle)
 
-    weight = jnp.sum(row_weight[...], axis=1, keepdims=True)
-    mass_row = pick_row(iota((NPOSE, NPOSE), 0) == pose_row[0:1, :], weight)
     for piece in range(NPOSE // LANES):
-        masses[member, piece : piece + 1, :] = mass_row[:, piece * LANES : (piece + 1) * LANES]
+        weight = row_weight[piece * LANES : (piece + 1) * LANES, :].T
+        masses[member, piece : piece + 1, :] = jnp.sum(weight, axis=0, keepdims=True)
 
     def mass_copy(step):
         return img_copy(16, masses.at[member], masses.at[member], img_peer(step))
@@ -566,62 +481,115 @@
 
     for step in range(1, members):
         mass_copy(step).start()
-    for index in range(width // stripe):
-        back_stripe(index)
-    ring_start(0)
-    ring_relay(0)
-    ring_finish(0)
+
+    def back_stripe(index):
+        at = rows_at(index * stripe, stripe)
+        part = partial[:, at] + dot(spread_last[...], images_v[middle * LANES :, at])
+        back[:, at] = part.astype(BF16)
+
+    each(width // stripe, back_stripe)
+    load[7].wait()
+    half_rows = NPOSE // 2
+
+    def away_copy(index):
+        return img_copy(40 + index, away.at[index], away_in.at[index], partner)
+
+    def turn_stripe(index, chip_index):
+        part = dot(back[...], columns_v[:, rows_at(chip_index * stripe, stripe)])
+        first, second = part[:, :LANES], part[:, LANES:]
+        kept[index] = jnp.where(core == 0, first, second)
+        away[index] = jnp.where(core == 0, second, first).astype(BF16)
+        away_copy(index).start()
+
+    def kept_part(index, first=0, size=NPOSE):
+        rows = slice(first, first + size)
+        return kept[index, rows, :] + away_in[index, rows, :].astype(F32)
+
+    low, high = slice(0, half_rows), slice(half_rows, NPOSE)
+    ring_copies = [
+        img_copy(48, opposite.at[low], opposite_in.at[low], right),
+        img_copy(49, opposite.at[high], opposite_in.at[high], left),
+        img_copy(50, ring.at[0, high], ring_in.at[0, high], right),
+        img_copy(51, ring.at[1, low], ring_in.at[1, low], left),
+        img_copy(52, ring.at[0, low], ring_in.at[0, low], right),
+        img_copy(53, ring.at[1, high], ring_in.at[1, high], left),
+    ]
+    turn_stripe(FAR, lax.rem(chip + 2, ring_len))
+    turn_stripe(RIGHT, lax.rem(chip + 1, ring_len))
+    away_copy(FAR).wait_recv()
+    opposite[...] = kept_part(FAR).astype(BF16)
+    ring_copies[0].start()
+    ring_copies[1].start()
+    turn_stripe(LEFT, lax.rem(chip + ring_len - 1, ring_len))
+    away_copy(RIGHT).wait_recv()
+    ring[0, high] = kept_part(RIGHT, half_rows, half_rows).astype(BF16)
+    ring_copies[2].start()
+    turn_stripe(HOME, chip)
+    away_copy(LEFT).wait_recv()
+    ring[1, low] = kept_part(LEFT, 0, half_rows).astype(BF16)
+    ring_copies[3].start()
+    ring_copies[0].wait_recv()
+    ring[0, low] = (kept_part(RIGHT, 0, half_rows) + opposite_in[low, :].astype(F32)).astype(BF16)
+    ring_copies[4].start()
+    ring_copies[1].wait_recv()
+    ring[1, high] = (kept_part(LEFT, half_rows, half_rows) + opposite_in[high, :].astype(F32)).astype(BF16)
+    ring_copies[5].start()
     shares_copy = pltpu.make_async_copy(shares, shares_out, loads.at[8])
     shares_copy.start()
+    away_copy(HOME).wait_recv()
+    held = kept_part(HOME)
+    for index in range(2, 6):
+        ring_copies[index].wait_recv()
+    summed = (held + ring_in[0].astype(F32) + ring_in[1].astype(F32)).astype(BF16)
+
+    unpacked = dot(unpack[...], summed)
+    for slab in range(slabs):
+        returning[slab] = unpacked[slab * cap : (slab + 1) * cap].astype(BF16)
+    slab_exchange(3, returning, returned)
+    returned[own] = returning[own]
 
     img_whole(16, masses).wait_recv()
     mass_sum = masses[0]
     for index in range(1, members):
         mass_sum = mass_sum + masses[index]
-    mass_cols = mass_sum.T
-    amount = jnp.zeros((1, total_slots), F32)
-    for piece in range(NPOSE // LANES):
-        pose = (iota((LANES, total_slots), 0) + piece * LANES).astype(F32)
-        amount += pick_row(slot_table[3:4, :] == pose, mass_cols[:, piece : piece + 1])
-    first = amount.astype(BF16).astype(F32)
-    second = (amount - first).astype(BF16).astype(F32)
-    pieces = [first, second, amount - first - second, jnp.zeros((13, total_slots), F32)]
-    mass = dot(jnp.concatenate(pieces, axis=0).astype(BF16), weave[...])
-    inverse[...] = 1.0 / (jnp.sum(mass, axis=0, keepdims=True) + RIDGE)
-    load[7].wait()
-
-    turned = jnp.zeros((mine, width), F32)
-    for part in range(halves):
-        slab_arrivals(3 + part, returned.at[part])
-        gathered = jnp.concatenate([returned[part, block].astype(F32) for block in range(slabs)], axis=0)
-        turned += dot(gathered.astype(BF16), columns_v[columns_of(part), :])
-    for block in range(members):
-        crossing[block] = turned[:, block * LANES : (block + 1) * LANES].T.astype(BF16)
-
-    def cross_copy(step):
-        peer = img_peer(step)
-        return img_copy(17, crossing.at[peer], crossed.at[member], peer)
-
-    for step in range(1, members):
-        cross_copy(step).start()
-    crossed[member] = crossing[member]
-
-    for stage, ref in ((0, outgoing), (1, picks), (2, shares), (3, returning.at[0])):
+    mass_row = jnp.concatenate([mass_sum[piece : piece + 1] for piece in range(NPOSE // LANES)], axis=1)
+    own_keys = keys[own]
+    levels = weight_of[own].astype(F32) * (1.0 / WSTEPS)
+    alive = jnp.where(own_keys >= 0, 1.0, 0.0)
+    spot_cols = voxel_of[own].astype(F32).T.astype(jnp.int32)
+    lower_cols, upper_cols = (levels * alive).T, ((1.0 - levels) * alive).T
+    own_key_cols = own_keys.astype(F32).T
+    voxel = iota((cap, voxels), 1)
+    mass = jnp.zeros((1, voxels), F32)
+    for block in range(slabs):
+        spots, lows, highs, key = (
+            table[:, block : block + 1] for table in (spot_cols, lower_cols, upper_cols, own_key_cols)
+        )
+        value = jnp.where(voxel == spots, lows, 0.0) + jnp.where(voxel == spots + 1, highs, 0.0)
+        weave[block * cap : (block + 1) * cap, :] = value.astype(BF16)
+        amount = jnp.sum(jnp.where(key == pose_ids, mass_row, 0.0), axis=1, keepdims=True)
+        mass += pick_row(value > 0.0, value * amount)
+    inverse[...] = 1.0 / (mass + RIDGE)
+    slab_arrivals(3, returned)
+
+    for stage, ref in ((0, outgoing), (1, picks), (2, shares), (3, returning)):
         slab_whole(stage, ref, slabs - 1).wait_send()
-    for copy in gathers:
+    for copy in gathers + ring_copies:
         copy.wait_send()
-    for index in range(halves * per_half):
+    for index in range(ring_len):
         away_copy(index).wait_send()
-    for part in range(halves):
-        for index in range(6):
-            ring_copy(part, index).wait_send()
     img_whole(16, masses).wait_send()
-    img_whole(17, crossed).wait_recv()
-
-    slots = jnp.concatenate([crossed[block] for block in range(members)], axis=1)
+
+    pair = LANES // cap
+    slots = jnp.concatenate(
+        [
+            returned[block : block + pair].reshape(LANES, LANES).astype(F32).T.astype(BF16)
+            for block in range(0, slabs, pair)
+        ],
+        axis=1,
+    )
     fourier[...] = (dot(slots, weave[...]) * inverse[...]).astype(BF16)
     shares_copy.wait()
-    img_whole(17, crossing).wait_send()
 
 
 def finish(rows, fourier, shares, density, posterior):
@@ -657,9 +625,10 @@
         pltpu.VMEM(slot_key.shape, jnp.int32),
         pltpu.VMEM(slot_key.shape, jnp.int32),
         pltpu.VMEM(slot_key.shape, jnp.int32),
-        pltpu.VMEM((8, slabs * cap), F32),
         pltpu.VMEM((8, mine), F32),
         pltpu.VMEM((8, NPOSE), jnp.int32),
+        pltpu.VMEM((cands, particles), jnp.int32),
+        pltpu.VMEM((slabs * cap, NPOSE), BF16),
         pltpu.VMEM((slabs, deep, width), BF16),
         pltpu.VMEM((slabs, deep, width), BF16),
         pltpu.VMEM((NPOSE, width), BF16),
@@ -674,19 +643,18 @@
         pltpu.VMEM((NPOSE, 5 * LANES), BF16),
         pltpu.VMEM((NPOSE, LANES), F32),
         pltpu.VMEM((NPOSE, width), F32),
-        pltpu.VMEM((side, width), BF16),
-        pltpu.VMEM((side, width), BF16),
-        pltpu.VMEM((side, width), F32),
-        pltpu.VMEM((share, width), BF16),
-        pltpu.VMEM((share, width), BF16),
-        pltpu.VMEM((2, share, width), BF16),
-        pltpu.VMEM((2, share, width), BF16),
+        pltpu.VMEM((NPOSE, width), BF16),
+        pltpu.VMEM((members // 2, NPOSE, LANES), BF16),
+        pltpu.VMEM((members // 2, NPOSE, LANES), BF16),
+        pltpu.VMEM((members // 2, NPOSE, LANES), F32),
+        pltpu.VMEM((NPOSE, LANES), BF16),
+        pltpu.VMEM((NPOSE, LANES), BF16),
+        pltpu.VMEM((2, NPOSE, LANES), BF16),
+        pltpu.VMEM((2, NPOSE, LANES), BF16),
         pltpu.VMEM((members, 8, LANES), F32),
         pltpu.VMEM((1, voxels), F32),
-        pltpu.VMEM((1, slabs, deep, width), BF16),
-        pltpu.VMEM((1, slabs, deep, width), BF16),
-        pltpu.VMEM((members, mine, LANES), BF16),
-        pltpu.VMEM((members, mine, LANES), BF16),
+        pltpu.VMEM((slabs, cap, LANES), BF16),
+        pltpu.VMEM((slabs, cap, LANES), BF16),
         pltpu.SemaphoreType.DMA((9,)),
         pltpu.SemaphoreType.DMA((7,)),
         pltpu.SemaphoreType.DMA((7,)),

time: 66.9 us -> 60.8 us (0.909)
  Pallas kernels: 66.1 us -> 59.5 us
    pallas_call x1, Pallas kernels: 63.8 us -> 57.1 us  [per_device(): pl.pallas_call(functools.partial(kernel, slabs, members), out_shape=(jax....]
where the time goes in v10:
time: 60.8 us; the launch traced here: 60.1 us
  Pallas kernels  59.5 us (98%)
  between operations  0.64 us (1%)
    pallas_call x1, Pallas kernels, per_device(): pl.pallas_call(functools.partial(kernel, slabs, members), out_shape=(jax....  57.1 us
    pallas_call x1, Pallas kernels, per_device(): pl.pallas_call(finish, out_shape=(jax.ShapeDtypeStruct((planes, edge // m...  2.34 us

profile of v10, /device:TPU:1, one launch (start us, length us, event | category | flops | bytes accessed | tf_op | source)
XLA Modules:
  0.0 60.1 jit_solution(3417024453076618170)
XLA Ops:
  0.6 57.1 %shard_map.104 = (bf16[128,1024]{1,0:T(8,128)(2,1)}, f32[16,16,128]{2,1,0:T(8,128)}) custom-call(bf16[2048,1024]{1,0:T(8,128)(2,1)} %images.1, bf16[1024,1024]{1,0:T(8,128)(2,1)} %bitcast.5, bf16[1024,1024]{1,0:T(8,128)(2,1)} %constant.4.clone.columns, f32[1,2048]{1,0:T(1,128)} %bitcast.7, s32[16,2048]{1,0:T(8,128)} %bitcast.6, s32[16,16,64]{2,1,0:T(8,128)} %keys_in.1, ...), custom_call_target="tpu_custom_call" | custom-call | tf_op jit(solution)/shard_map/pallas_call | solution.py:664
  57.8 2.3 %shard_map.105 = (f32[2,64,512]{2,1,0:T(8,128)}, f32[16,2048]{1,0:T(8,128)}) custom-call(bf16[1024,512]{1,0:T(8,128)(2,1)} %constant.5.clone.rows, bf16[128,1024]{1,0:T(8,128)(2,1)} %get-tuple-element.6.fourier, f32[16,16,128]{2,1,0:T(8,128)} %get-tuple-element.7.shares), custom_call_target="tpu_custom_call" | custom-call | tf_op jit(solution)/shard_map/pallas_call | solution.py:680

commit v11 on v10

--- a/solution.py
+++ b/solution.py
@@ -119,7 +119,7 @@
     def greet(axis, peer):
         pl.semaphore_signal(barrier, inc=1, device_id={axis: peer}, device_id_type=pl.DeviceIdType.MESH)
 
-    sources = [keys_in, voxels_in, weights_in, volume, poses_in, images, precision_in, columns]
+    sources = [keys_in, voxels_in.at[own], weights_in.at[own], volume, poses_in, images, precision_in, columns]
     targets = [keys, voxel_of, weight_of, volume_v, poses, images_v, precision, columns_v]
     load = [pltpu.make_async_copy(src, dst, loads.at[i]) for i, (src, dst) in enumerate(zip(sources, targets))]
 
@@ -146,7 +146,7 @@
     out_start = jnp.sum(before, axis=1, keepdims=True)
     total_slots = slabs * cap
     own_key = keys[own]
-    own_code = voxel_of[own] * 32 + jnp.where(own_key >= 0, weight_of[own], 31)
+    own_code = voxel_of[...] * 32 + jnp.where(own_key >= 0, weight_of[...], 31)
 
     def ordered(first, count, tables):
         position = iota((1, count), 1) + first
@@ -251,7 +251,7 @@
 
     first_chunks = 3
     ahead_of = 2 * first_chunks
-    middle = (slabs + ahead_of) // 2
+    middle = 2 * ahead_of
     turn = jnp.where(own >= ahead_of, 1, 0)
 
     def rank_chunk(block):
@@ -302,6 +302,14 @@
         gathers[index].start()
 
     each(slabs, rank_chunk, middle)
+
+    def power_step(index):
+        at = rows_at(index * share, share)
+        values = slices[at, :].astype(F32)
+        total = 0.5 * jnp.sum(values * values, axis=1, keepdims=True)
+        half_power[at, :] = jnp.broadcast_to(total, (share, LANES))
+
+    power_step(HOME)
     gathers[0].wait_recv()
     gathers[5].start()
     gathers[1].wait_recv()
@@ -311,12 +319,6 @@
     gathers[4].wait_recv()
     gathers[8].start()
     load[5].wait()
-
-    def power_step(index):
-        at = rows_at(index * share, share)
-        values = slices[at, :].astype(F32)
-        total = 0.5 * jnp.sum(values * values, axis=1, keepdims=True)
-        half_power[at, :] = jnp.broadcast_to(total, (share, LANES))
 
     chunk = 2 * LANES
     chunks = images_v.shape[0] // chunk
@@ -361,10 +363,14 @@
     def full_chunk(index):
         score_chunk(index, slices[...], [(0, 0, NPOSE)], False)
 
+    power_step(LEFT)
+    power_step(RIGHT)
     gathers[2].wait_recv()
+    power_step(other(HOME))
     gathers[7].wait_recv()
     gathers[8].wait_recv()
-    each(members - 1, power_step, 1)
+    power_step(other(LEFT))
+    power_step(other(RIGHT))
     each(first_chunks - 1, near_step)
     gathers[5].wait_recv()
     gathers[9].start()
@@ -405,7 +411,7 @@
             total = total + picks_in[block]
         total = total * precision[:, rows_at(own * LANES, LANES)]
         exponent = jnp.exp(total - jnp.max(total, axis=0, keepdims=True))
-        shares[own] = exponent / jnp.sum(exponent, axis=0, keepdims=True)
+        shares[own] = (exponent / jnp.sum(exponent, axis=0, keepdims=True)).astype(BF16)
         for step in range(1, slabs):
             remote(
                 shares.at[own], shares.at[own], slab_send.at[2], slab_recv.at[5 + turn], {"slab": slab_peer(step)}
@@ -435,7 +441,7 @@
     def spread_chunk(block, spread, origin):
         at = rows_at(block * LANES, LANES)
         to = rows_at((block - origin) * LANES, LANES)
-        amount = shares[block] * precision[:, at]
+        amount = shares[block].astype(F32) * precision[:, at]
         rounded = amount.astype(BF16).astype(F32)
         low, high = rounded[0:8], rounded[8:16]
         for first in range(0, NPOSE, 16):
@@ -554,9 +560,9 @@
         mass_sum = mass_sum + masses[index]
     mass_row = jnp.concatenate([mass_sum[piece : piece + 1] for piece in range(NPOSE // LANES)], axis=1)
     own_keys = keys[own]
-    levels = weight_of[own].astype(F32) * (1.0 / WSTEPS)
+    levels = weight_of[...].astype(F32) * (1.0 / WSTEPS)
     alive = jnp.where(own_keys >= 0, 1.0, 0.0)
-    spot_cols = voxel_of[own].astype(F32).T.astype(jnp.int32)
+    spot_cols = voxel_of[...].astype(F32).T.astype(jnp.int32)
     lower_cols, upper_cols = (levels * alive).T, ((1.0 - levels) * alive).T
     own_key_cols = own_keys.astype(F32).T
     voxel = iota((cap, voxels), 1)
@@ -600,7 +606,7 @@
     for z in range(planes):
         density[z] = value[z * columns_out : (z + 1) * columns_out]
     for block in range(shares.shape[0]):
-        posterior[:, block * LANES : (block + 1) * LANES] = shares[block]
+        posterior[:, block * LANES : (block + 1) * LANES] = shares[block].astype(F32)
 
 
 def per_device(images, volume, precision, candidates, slot_key, slot_voxel, slot_weight):
@@ -623,8 +629,8 @@
         pltpu.VMEM((1, particles), F32),
         pltpu.VMEM((cands, particles), jnp.int32),
         pltpu.VMEM(slot_key.shape, jnp.int32),
-        pltpu.VMEM(slot_key.shape, jnp.int32),
-        pltpu.VMEM(slot_key.shape, jnp.int32),
+        pltpu.VMEM(slot_key.shape[1:], jnp.int32),
+        pltpu.VMEM(slot_key.shape[1:], jnp.int32),
         pltpu.VMEM((8, mine), F32),
         pltpu.VMEM((8, NPOSE), jnp.int32),
         pltpu.VMEM((cands, particles), jnp.int32),
@@ -637,10 +643,10 @@
         pltpu.VMEM((slabs * cap, voxels), BF16),
         pltpu.VMEM((slabs, cands, LANES), F32),
         pltpu.VMEM((slabs, cands, LANES), F32),
-        pltpu.VMEM((slabs, cands, LANES), F32),
+        pltpu.VMEM((slabs, cands, LANES), BF16),
         pltpu.VMEM((NPOSE, 6 * LANES), BF16),
-        pltpu.VMEM((NPOSE, 5 * LANES), BF16),
-        pltpu.VMEM((NPOSE, 5 * LANES), BF16),
+        pltpu.VMEM((NPOSE, 6 * LANES), BF16),
+        pltpu.VMEM((NPOSE, 4 * LANES), BF16),
         pltpu.VMEM((NPOSE, LANES), F32),
         pltpu.VMEM((NPOSE, width), F32),
         pltpu.VMEM((NPOSE, width), BF16),
@@ -665,7 +671,7 @@
         functools.partial(kernel, slabs, members),
         out_shape=(
             jax.ShapeDtypeStruct((LANES, voxels), BF16),
-            jax.ShapeDtypeStruct((slabs, cands, LANES), F32),
+            jax.ShapeDtypeStruct((slabs, cands, LANES), BF16),
         ),
         in_specs=[big] * 8,
         out_specs=(near, big),

time: 60.8 us -> 59.9 us (0.985)
  Pallas kernels: 59.5 us -> 58.6 us
    pallas_call x1, Pallas kernels: 57.1 us -> 56.3 us  [per_device(): pl.pallas_call(functools.partial(kernel, slabs, members), out_shape=(jax....]
where the time goes in v11:
time: 59.9 us; the launch traced here: 59.3 us
  Pallas kernels  58.6 us (98%)
  between operations  0.64 us (1%)
    pallas_call x1, Pallas kernels, per_device(): pl.pallas_call(functools.partial(kernel, slabs, members), out_shape=(jax....  56.3 us
    pallas_call x1, Pallas kernels, per_device(): pl.pallas_call(finish, out_shape=(jax.ShapeDtypeStruct((planes, edge // m...  2.34 us

profile of v11, /device:TPU:1, one launch (start us, length us, event | category | flops | bytes accessed | tf_op | source)
XLA Modules:
  0.0 59.3 jit_solution(7601768782247306888)
XLA Ops:
  0.6 56.3 %shard_map.104 = (bf16[128,1024]{1,0:T(8,128)(2,1)}, bf16[16,16,128]{2,1,0:T(8,128)(2,1)}) custom-call(bf16[2048,1024]{1,0:T(8,128)(2,1)} %images.1, bf16[1024,1024]{1,0:T(8,128)(2,1)} %bitcast.5, bf16[1024,1024]{1,0:T(8,128)(2,1)} %constant.4.clone.columns, f32[1,2048]{1,0:T(1,128)} %bitcast.7, s32[16,2048]{1,0:T(8,128)} %bitcast.6, s32[16,16,64]{2,1,0:T(8,128)} %keys_in.1, ...), custom_call_target="tpu_custom_call" | custom-call | tf_op jit(solution)/shard_map/pallas_call | solution.py:670
  56.9 2.3 %shard_map.105 = (f32[2,64,512]{2,1,0:T(8,128)}, f32[16,2048]{1,0:T(8,128)}) custom-call(bf16[1024,512]{1,0:T(8,128)(2,1)} %constant.5.clone.rows, bf16[128,1024]{1,0:T(8,128)(2,1)} %get-tuple-element.6.fourier, bf16[16,16,128]{2,1,0:T(8,128)(2,1)} %get-tuple-element.7.shares), custom_call_target="tpu_custom_call" | custom-call | tf_op jit(solution)/shard_map/pallas_call | solution.py:686

commit v12 on v11

--- a/solution.py
+++ b/solution.py
@@ -86,7 +86,7 @@
     images_v, volume_v, columns_v, precision, poses, keys, voxel_of, weight_of,
     pack_table, pose_row, named, unpack,
     outgoing, incoming, slices, half_power, ranks, weave,
-    picks, picks_in, shares, spread_first, spread_middle, spread_last, row_weight, partial, back,
+    picks, picks_in, shares, spread_first, spread_middle, spread_last, row_weight, partial, turned,
     away, away_in, kept, opposite, opposite_in, ring, ring_in,
     masses, inverse, returning, returned,
     loads, slab_send, slab_recv, img_send, img_recv,
@@ -119,8 +119,8 @@
     def greet(axis, peer):
         pl.semaphore_signal(barrier, inc=1, device_id={axis: peer}, device_id_type=pl.DeviceIdType.MESH)
 
-    sources = [keys_in, voxels_in.at[own], weights_in.at[own], volume, poses_in, images, precision_in, columns]
-    targets = [keys, voxel_of, weight_of, volume_v, poses, images_v, precision, columns_v]
+    sources = [keys_in, voxels_in.at[own], weights_in.at[own], volume, poses_in, images, columns, precision_in]
+    targets = [keys, voxel_of, weight_of, volume_v, poses, images_v, columns_v, precision]
     load = [pltpu.make_async_copy(src, dst, loads.at[i]) for i, (src, dst) in enumerate(zip(sources, targets))]
 
     def start_load(index):
@@ -264,7 +264,19 @@
                 value = jnp.where(number[k : k + 1] == row, jnp.int16(k), value)
             ranks[first : first + LANES, at] = value.astype(jnp.int32)
 
-    each(middle, rank_chunk, ahead_of)
+    stripe = 2 * LANES
+    stripes = width // stripe
+    slabful = images_v.shape[0] // stripes
+
+    def prepare(step):
+        block = rows_at(lax.div(step, stripes) * slabful, slabful)
+        at = rows_at(lax.rem(step, stripes) * stripe, stripe)
+        turned[block, at] = dot(images_v[block, :], columns_v[:, at]).astype(BF16)
+        rank_chunk(lax.rem(step + ahead_of, slabs))
+
+    load[5].wait()
+    load[6].wait()
+    each(6, prepare)
 
     slab_arrivals(0, incoming)
     arrived = jnp.concatenate([incoming[block].astype(F32) for block in range(slabs)], axis=0).astype(BF16)
@@ -301,7 +313,7 @@
     for index in range(5):
         gathers[index].start()
 
-    each(slabs, rank_chunk, middle)
+    each(10, prepare, 6)
 
     def power_step(index):
         at = rows_at(index * share, share)
@@ -318,7 +330,6 @@
     gathers[7].start()
     gathers[4].wait_recv()
     gathers[8].start()
-    load[5].wait()
 
     chunk = 2 * LANES
     chunks = images_v.shape[0] // chunk
@@ -363,6 +374,7 @@
     def full_chunk(index):
         score_chunk(index, slices[...], [(0, 0, NPOSE)], False)
 
+    each(12, prepare, 10)
     power_step(LEFT)
     power_step(RIGHT)
     gathers[2].wait_recv()
@@ -400,7 +412,7 @@
     each(first_chunks, far_step)
     each(chunks, full_step, first_chunks)
     picks_in[own] = picks[own]
-    load[6].wait()
+    load[7].wait()
     row_weight[...] = jnp.zeros_like(row_weight)
     masses[member] = jnp.zeros((8, LANES), F32)
 
@@ -421,7 +433,7 @@
     def _():
         share_out()
 
-    each(ahead_of, rank_chunk)
+    each(slabs, prepare, 12)
 
     @pl.when(turn != 0)
     def _():
@@ -456,11 +468,9 @@
                 values.append(value)
             spread[first : first + 16, to] = jnp.concatenate(values, axis=0).astype(BF16)
 
-    stripe = 2 * LANES
-
     def early_stripe(index):
         at = rows_at(index * stripe, stripe)
-        partial[:, at] = dot(spread_first[...], images_v[: ahead_of * LANES, at])
+        partial[:, at] = dot(spread_first[...], turned[: ahead_of * LANES, at])
 
     shares_arrive(0)
     each(ahead_of, lambda block: spread_chunk(block, spread_first, 0))
@@ -470,7 +480,7 @@
     waiting = list(range(middle, slabs))
     for index in range(width // stripe):
         at = slice(index * stripe, (index + 1) * stripe)
-        partial[:, at] += dot(spread_middle[...], images_v[ahead_of * LANES : middle * LANES, at])
+        partial[:, at] += dot(spread_middle[...], turned[ahead_of * LANES : middle * LANES, at])
         for block in waiting[index :: width // stripe]:
             spread_chunk(block, spread_last, middle)
 
@@ -488,20 +498,14 @@
     for step in range(1, members):
         mass_copy(step).start()
 
-    def back_stripe(index):
-        at = rows_at(index * stripe, stripe)
-        part = partial[:, at] + dot(spread_last[...], images_v[middle * LANES :, at])
-        back[:, at] = part.astype(BF16)
-
-    each(width // stripe, back_stripe)
-    load[7].wait()
     half_rows = NPOSE // 2
 
     def away_copy(index):
         return img_copy(40 + index, away.at[index], away_in.at[index], partner)
 
     def turn_stripe(index, chip_index):
-        part = dot(back[...], columns_v[:, rows_at(chip_index * stripe, stripe)])
+        at = rows_at(chip_index * stripe, stripe)
+        part = partial[:, at] + dot(spread_last[...], turned[middle * LANES :, at])
         first, second = part[:, :LANES], part[:, LANES:]
         kept[index] = jnp.where(core == 0, first, second)
         away[index] = jnp.where(core == 0, second, first).astype(BF16)
@@ -649,7 +653,7 @@
         pltpu.VMEM((NPOSE, 4 * LANES), BF16),
         pltpu.VMEM((NPOSE, LANES), F32),
         pltpu.VMEM((NPOSE, width), F32),
-        pltpu.VMEM((NPOSE, width), BF16),
+        pltpu.VMEM((particles, width), BF16),
         pltpu.VMEM((members // 2, NPOSE, LANES), BF16),
         pltpu.VMEM((members // 2, NPOSE, LANES), BF16),
         pltpu.VMEM((members // 2, NPOSE, LANES), F32),

time: 59.9 us -> 58.8 us (0.982)
  Pallas kernels: 58.6 us -> 57.8 us
    pallas_call x1, Pallas kernels: 56.3 us -> 55.4 us  [per_device(): pl.pallas_call(functools.partial(kernel, slabs, members), out_shape=(jax....]
where the time goes in v12:
time: 58.8 us; the launch traced here: 58.4 us
  Pallas kernels  57.8 us (98%)
  between operations  0.64 us (1%)
    pallas_call x1, Pallas kernels, per_device(): pl.pallas_call(functools.partial(kernel, slabs, members), out_shape=(jax....  55.4 us
    pallas_call x1, Pallas kernels, per_device(): pl.pallas_call(finish, out_shape=(jax.ShapeDtypeStruct((planes, edge // m...  2.34 us

profile of v12, /device:TPU:1, one launch (start us, length us, event | category | flops | bytes accessed | tf_op | source)
XLA Modules:
  0.0 58.4 jit_solution(17660830520525274807)
XLA Ops:
  0.6 55.4 %shard_map.104 = (bf16[128,1024]{1,0:T(8,128)(2,1)}, bf16[16,16,128]{2,1,0:T(8,128)(2,1)}) custom-call(bf16[2048,1024]{1,0:T(8,128)(2,1)} %images.1, bf16[1024,1024]{1,0:T(8,128)(2,1)} %bitcast.5, bf16[1024,1024]{1,0:T(8,128)(2,1)} %constant.4.clone.columns, f32[1,2048]{1,0:T(1,128)} %bitcast.7, s32[16,2048]{1,0:T(8,128)} %bitcast.6, s32[16,16,64]{2,1,0:T(8,128)} %keys_in.1, ...), custom_call_target="tpu_custom_call" | custom-call | tf_op jit(solution)/shard_map/pallas_call | solution.py:674
  56.1 2.3 %shard_map.105 = (f32[2,64,512]{2,1,0:T(8,128)}, f32[16,2048]{1,0:T(8,128)}) custom-call(bf16[1024,512]{1,0:T(8,128)(2,1)} %constant.5.clone.rows, bf16[128,1024]{1,0:T(8,128)(2,1)} %get-tuple-element.6.fourier, bf16[16,16,128]{2,1,0:T(8,128)(2,1)} %get-tuple-element.7.shares), custom_call_target="tpu_custom_call" | custom-call | tf_op jit(solution)/shard_map/pallas_call | solution.py:690

commit v13 on v12

--- a/solution.py
+++ b/solution.py
@@ -119,6 +119,10 @@
     def greet(axis, peer):
         pl.semaphore_signal(barrier, inc=1, device_id={axis: peer}, device_id_type=pl.DeviceIdType.MESH)
 
+    for step in range(1, slabs):
+        greet("slab", slab_peer(step))
+    for step in range(1, members):
+        greet("img", img_peer(step))
     sources = [keys_in, voxels_in.at[own], weights_in.at[own], volume, poses_in, images, columns, precision_in]
     targets = [keys, voxel_of, weight_of, volume_v, poses, images_v, columns_v, precision]
     load = [pltpu.make_async_copy(src, dst, loads.at[i]) for i, (src, dst) in enumerate(zip(sources, targets))]
@@ -133,10 +137,6 @@
 
     for index in range(5):
         start_load(index)
-    for step in range(1, slabs):
-        greet("slab", slab_peer(step))
-    for step in range(1, members):
-        greet("img", img_peer(step))
 
     for index in range(3):
         load[index].wait()
@@ -252,7 +252,7 @@
     first_chunks = 3
     ahead_of = 2 * first_chunks
     middle = 2 * ahead_of
-    turn = jnp.where(own >= ahead_of, 1, 0)
+    turn = jnp.where(own >= middle, 2, jnp.where(own >= ahead_of, 1, 0))
 
     def rank_chunk(block):
         at = rows_at(block * LANES, LANES)
@@ -440,7 +440,7 @@
         share_out()
 
     def shares_arrive(which):
-        group = ahead_of if which == 0 else slabs - ahead_of
+        group = (ahead_of, middle - ahead_of, slabs - middle)[which]
 
         @pl.when(turn == which)
         def _():
@@ -477,6 +477,7 @@
     each(width // stripe, early_stripe)
     shares_arrive(1)
     each(middle, lambda block: spread_chunk(block, spread_middle, ahead_of), ahead_of)
+    shares_arrive(2)
     waiting = list(range(middle, slabs))
     for index in range(width // stripe):
         at = slice(index * stripe, (index + 1) * stripe)
@@ -580,15 +581,14 @@
         amount = jnp.sum(jnp.where(key == pose_ids, mass_row, 0.0), axis=1, keepdims=True)
         mass += pick_row(value > 0.0, value * amount)
     inverse[...] = 1.0 / (mass + RIDGE)
-    slab_arrivals(3, returned)
-
-    for stage, ref in ((0, outgoing), (1, picks), (2, shares), (3, returning)):
+    for stage, ref in ((0, outgoing), (1, picks), (2, shares)):
         slab_whole(stage, ref, slabs - 1).wait_send()
     for copy in gathers + ring_copies:
         copy.wait_send()
     for index in range(ring_len):
         away_copy(index).wait_send()
     img_whole(16, masses).wait_send()
+    slab_arrivals(3, returned)
 
     pair = LANES // cap
     slots = jnp.concatenate(
@@ -600,6 +600,7 @@
     )
     fourier[...] = (dot(slots, weave[...]) * inverse[...]).astype(BF16)
     shares_copy.wait()
+    slab_whole(3, returning, slabs - 1).wait_send()
 
 
 def finish(rows, fourier, shares, density, posterior):
@@ -666,8 +667,8 @@
         pltpu.VMEM((slabs, cap, LANES), BF16),
         pltpu.VMEM((slabs, cap, LANES), BF16),
         pltpu.SemaphoreType.DMA((9,)),
-        pltpu.SemaphoreType.DMA((7,)),
-        pltpu.SemaphoreType.DMA((7,)),
+        pltpu.SemaphoreType.DMA((8,)),
+        pltpu.SemaphoreType.DMA((8,)),
         pltpu.SemaphoreType.DMA((60,)),
         pltpu.SemaphoreType.DMA((60,)),
     ]

time: 58.8 us -> 58.7 us (level)
  no operation moved by 1% of the time
where the time goes in v13:
time: 58.7 us; the launch traced here: 58.2 us
  Pallas kernels  57.6 us (98%)
  between operations  0.64 us (1%)
    pallas_call x1, Pallas kernels, per_device(): pl.pallas_call(functools.partial(kernel, slabs, members), out_shape=(jax....  55.3 us
    pallas_call x1, Pallas kernels, per_device(): pl.pallas_call(finish, out_shape=(jax.ShapeDtypeStruct((planes, edge // m...  2.34 us

profile of v13, /device:TPU:1, one launch (start us, length us, event | category | flops | bytes accessed | tf_op | source)
XLA Modules:
  0.0 58.2 jit_solution(6770147625395652192)
XLA Ops:
  0.6 55.3 %shard_map.104 = (bf16[128,1024]{1,0:T(8,128)(2,1)}, bf16[16,16,128]{2,1,0:T(8,128)(2,1)}) custom-call(bf16[2048,1024]{1,0:T(8,128)(2,1)} %images.1, bf16[1024,1024]{1,0:T(8,128)(2,1)} %bitcast.5, bf16[1024,1024]{1,0:T(8,128)(2,1)} %constant.4.clone.columns, f32[1,2048]{1,0:T(1,128)} %bitcast.7, s32[16,2048]{1,0:T(8,128)} %bitcast.6, s32[16,16,64]{2,1,0:T(8,128)} %keys_in.1, ...), custom_call_target="tpu_custom_call" | custom-call | tf_op jit(solution)/shard_map/pallas_call | solution.py:675
  55.9 2.3 %shard_map.105 = (f32[2,64,512]{2,1,0:T(8,128)}, f32[16,2048]{1,0:T(8,128)}) custom-call(bf16[1024,512]{1,0:T(8,128)(2,1)} %constant.5.clone.rows, bf16[128,1024]{1,0:T(8,128)(2,1)} %get-tuple-element.6.fourier, bf16[16,16,128]{2,1,0:T(8,128)(2,1)} %get-tuple-element.7.shares), custom_call_target="tpu_custom_call" | custom-call | tf_op jit(solution)/shard_map/pallas_call | solution.py:691

commit v14 on v13

--- a/solution.py
+++ b/solution.py
@@ -682,7 +682,7 @@
         out_specs=(near, big),
         scratch_shapes=scratch,
         compiler_params=pltpu.CompilerParams(
-            collective_id=0, has_side_effects=True, vmem_limit_bytes=56 * 1024 * 1024
+            collective_id=0, has_side_effects=True, vmem_limit_bytes=52 * 1024 * 1024
         ),
     )(
         images, volume.reshape(voxels, width), column_table(edge, members),
@@ -696,7 +696,7 @@
         ),
         in_specs=[near] * 3,
         out_specs=(near, near),
-        compiler_params=pltpu.CompilerParams(vmem_limit_bytes=56 * 1024 * 1024),
+        compiler_params=pltpu.CompilerParams(vmem_limit_bytes=52 * 1024 * 1024),
     )(row_table(edge), fourier, shares)
     return density.transpose(0, 2, 1), posterior.T
 

time: 58.7 us -> 61.1 us (1.041)
  local copies, waits for them, and re-layouts: 0 us -> 4.31 us
  Pallas kernels: 57.6 us -> 55.5 us
    unnamed x0 -> x12, local copies, waits for them, and re-layouts: none -> 4.31 us
    pallas_call x1, Pallas kernels: 2.34 us -> 1.01 us  [per_device(): pl.pallas_call(finish, out_shape=(jax.ShapeDtypeStruct((planes, edge // m...]
    pallas_call x1, Pallas kernels: 55.3 us -> 54.5 us  [per_device(): pl.pallas_call(functools.partial(kernel, slabs, members), out_shape=(jax....]
where the time goes in v14:
time: 61.1 us; the launch traced here: 60.5 us
  Pallas kernels  55.5 us (91%)
  local copies, waits for them, and re-layouts  4.31 us (7%)
  between operations  0.66 us (1%)
    pallas_call x1, Pallas kernels, per_device(): pl.pallas_call(functools.partial(kernel, slabs, members), out_shape=(jax....  54.5 us
    unnamed x12, local copies, waits for them, and re-layouts  4.31 us

profile of v14, /device:TPU:1, one launch (start us, length us, event | category | flops | bytes accessed | tf_op | source)
XLA Modules:
  0.0 60.5 jit_solution(982396178894481997)
XLA Ops:
  0.6 0.0 copy-start.1
  0.6 0.9 %copy-done.1 = s32[2048,16]{0,1:T(8,128)S(1)} copy-done((s32[2048,16]{0,1:T(8,128)S(1)}, s32[2048,16]{0,1:T(8,128)}, u32[]{:S(2)}) %copy-start.1) | copy-done | bytes 131096
  1.5 0.0 copy-start.2
  1.5 0.9 %copy-done.2 = s32[16,16,64]{2,1,0:T(8,128)S(1)} copy-done((s32[16,16,64]{2,1,0:T(8,128)S(1)}, s32[16,16,64]{2,1,0:T(8,128)}, u32[]{:S(2)}) %copy-start.2) | copy-done | bytes 65560
  2.4 0.0 copy-start.3
  2.4 0.9 %copy-done.3 = s32[16,16,64]{2,1,0:T(8,128)S(1)} copy-done((s32[16,16,64]{2,1,0:T(8,128)S(1)}, s32[16,16,64]{2,1,0:T(8,128)}, u32[]{:S(2)}) %copy-start.3) | copy-done | bytes 65560
  3.3 0.0 copy-start.4
  3.3 0.9 %copy-done.4 = s32[16,16,64]{2,1,0:T(8,128)S(1)} copy-done((s32[16,16,64]{2,1,0:T(8,128)S(1)}, s32[16,16,64]{2,1,0:T(8,128)}, u32[]{:S(2)}) %copy-start.4) | copy-done | bytes 65560
  4.3 0.0 copy-start.5
  4.3 0.7 %copy-done.5 = f32[2048]{0:T(1024)S(1)} copy-done((f32[2048]{0:T(1024)S(1)}, f32[2048]{0:T(1024)}, u32[]{:S(2)}) %copy-start.5) | copy-done | bytes 8216
  4.9 0.0 copy-start
  5.0 54.5 %shard_map.104 = (bf16[128,1024]{1,0:T(8,128)(2,1)S(1)}, bf16[16,16,128]{2,1,0:T(8,128)(2,1)S(1)}) custom-call(bf16[2048,1024]{1,0:T(8,128)(2,1)} %images.1, bf16[1024,1024]{1,0:T(8,128)(2,1)} %bitcast.7, bf16[1024,1024]{1,0:T(8,128)(2,1)} %constant.4.clone.columns, f32[1,2048]{1,0:T(1,128)S(1)} %bitcast.6, s32[16,2048]{1,0:T(8,128)S(1)} %bitcast.5, ...), custom_call_target="tpu_custom_call" | custom-call | tf_op jit(solution)/shard_map/pallas_call | solution.py:675
  59.4 0.0 copy-done
  59.5 1.0 %shard_map.105 = (f32[2,64,512]{2,1,0:T(8,128)}, f32[16,2048]{1,0:T(8,128)}) custom-call(bf16[1024,512]{1,0:T(8,128)(2,1)S(1)} %copy-done, bf16[128,1024]{1,0:T(8,128)(2,1)S(1)} %get-tuple-element.6.fourier, bf16[16,16,128]{2,1,0:T(8,128)(2,1)S(1)} %get-tuple-element.7.shares), custom_call_target="tpu_custom_call" | custom-call | tf_op jit(solution)/shard_map/pallas_call | solution.py:691
Async XLA Ops:
  0.6 0.9 %copy-start.1 = (s32[2048,16]{0,1:T(8,128)S(1)}, s32[2048,16]{0,1:T(8,128)}, u32[]{:S(2)}) copy-start(s32[2048,16]{0,1:T(8,128)} %param.12) | copy-start | bytes 393220
  1.5 0.9 %copy-start.2 = (s32[16,16,64]{2,1,0:T(8,128)S(1)}, s32[16,16,64]{2,1,0:T(8,128)}, u32[]{:S(2)}) copy-start(s32[16,16,64]{2,1,0:T(8,128)} %keys_in.1) | copy-start | bytes 196612
  2.4 0.9 %copy-start.3 = (s32[16,16,64]{2,1,0:T(8,128)S(1)}, s32[16,16,64]{2,1,0:T(8,128)}, u32[]{:S(2)}) copy-start(s32[16,16,64]{2,1,0:T(8,128)} %voxels_in.1) | copy-start | bytes 196612
  3.3 0.9 %copy-start.4 = (s32[16,16,64]{2,1,0:T(8,128)S(1)}, s32[16,16,64]{2,1,0:T(8,128)}, u32[]{:S(2)}) copy-start(s32[16,16,64]{2,1,0:T(8,128)} %weights_in.1) | copy-start | bytes 196612
  4.3 0.7 %copy-start.5 = (f32[2048]{0:T(1024)S(1)}, f32[2048]{0:T(1024)}, u32[]{:S(2)}) copy-start(f32[2048]{0:T(1024)} %param.11) | copy-start | bytes 24580
  4.9 54.5 %copy-start = (bf16[1024,512]{1,0:T(8,128)(2,1)S(1)}, bf16[1024,512]{1,0:T(8,128)(2,1)}, u32[]{:S(2)}) copy-start(bf16[1024,512]{1,0:T(8,128)(2,1)} %constant.5.clone.rows) | copy-start | bytes 3145732

commit v15 on v14

--- a/solution.py
+++ b/solution.py
@@ -675,8 +675,8 @@
     fourier, shares = pl.pallas_call(
         functools.partial(kernel, slabs, members),
         out_shape=(
-            jax.ShapeDtypeStruct((LANES, voxels), BF16),
-            jax.ShapeDtypeStruct((slabs, cands, LANES), BF16),
+            pltpu.VMEM((LANES, voxels), BF16),
+            pltpu.VMEM((slabs, cands, LANES), BF16),
         ),
         in_specs=[big] * 8,
         out_specs=(near, big),
@@ -684,10 +684,13 @@
         compiler_params=pltpu.CompilerParams(
             collective_id=0, has_side_effects=True, vmem_limit_bytes=52 * 1024 * 1024
         ),
-    )(
-        images, volume.reshape(voxels, width), column_table(edge, members),
-        precision[None, :], candidates.T, slot_key, slot_voxel, slot_weight,
-    )
+    )(*(
+        pltpu.with_memory_space_constraint(operand, pltpu.HBM)
+        for operand in (
+            images, volume.reshape(voxels, width), column_table(edge, members),
+            precision[None, :], candidates.T, slot_key, slot_voxel, slot_weight,
+        )
+    ))
     density, posterior = pl.pallas_call(
         finish,
         out_shape=(
@@ -696,7 +699,7 @@
         ),
         in_specs=[near] * 3,
         out_specs=(near, near),
-        compiler_params=pltpu.CompilerParams(vmem_limit_bytes=52 * 1024 * 1024),
+        compiler_params=pltpu.CompilerParams(vmem_limit_bytes=16 * 1024 * 1024),
     )(row_table(edge), fourier, shares)
     return density.transpose(0, 2, 1), posterior.T
 

time: 61.1 us -> 56.7 us (0.928)
  local copies, waits for them, and re-layouts: 4.31 us -> 0.01 us
    unnamed x12 -> x2, local copies, waits for them, and re-layouts: 4.31 us -> 0.01 us
where the time goes in v15:
time: 56.7 us; the launch traced here: 56.2 us
  Pallas kernels  55.6 us (98%)
  between operations  0.66 us (1%)
    pallas_call x1, Pallas kernels, per_device(): pl.pallas_call(functools.partial(kernel, slabs, members), out_shape=(pltp...  54.6 us

profile of v15, /device:TPU:1, one launch (start us, length us, event | category | flops | bytes accessed | tf_op | source)
XLA Modules:
  0.0 56.2 jit_solution(10361298853042807925)
XLA Ops:
  0.6 0.0 copy-start
  0.6 54.6 %shard_map.104 = (bf16[128,1024]{1,0:T(8,128)(2,1)S(1)}, bf16[16,16,128]{2,1,0:T(8,128)(2,1)S(1)}) custom-call(bf16[2048,1024]{1,0:T(8,128)(2,1)} %images.1, bf16[1024,1024]{1,0:T(8,128)(2,1)} %bitcast.5, bf16[1024,1024]{1,0:T(8,128)(2,1)} %constant.4.clone.columns, f32[1,2048]{1,0:T(1,128)} %bitcast.7, s32[16,2048]{1,0:T(8,128)} %bitcast.6, ...), custom_call_target="tpu_custom_call" | custom-call | tf_op jit(solution)/shard_map/pallas_call | solution.py:675
  55.2 0.0 copy-done
  55.2 1.0 %shard_map.105 = (f32[2,64,512]{2,1,0:T(8,128)}, f32[16,2048]{1,0:T(8,128)}) custom-call(bf16[1024,512]{1,0:T(8,128)(2,1)S(1)} %copy-done, bf16[128,1024]{1,0:T(8,128)(2,1)S(1)} %get-tuple-element.6.fourier, bf16[16,16,128]{2,1,0:T(8,128)(2,1)S(1)} %get-tuple-element.7.shares), custom_call_target="tpu_custom_call" | custom-call | tf_op jit(solution)/shard_map/pallas_call | solution.py:694
Async XLA Ops:
  0.6 54.6 %copy-start = (bf16[1024,512]{1,0:T(8,128)(2,1)S(1)}, bf16[1024,512]{1,0:T(8,128)(2,1)}, u32[]{:S(2)}) copy-start(bf16[1024,512]{1,0:T(8,128)(2,1)} %constant.5.clone.rows) | copy-start | bytes 3145732

commit v16 on v15

--- a/solution.py
+++ b/solution.py
@@ -272,11 +272,11 @@
         block = rows_at(lax.div(step, stripes) * slabful, slabful)
         at = rows_at(lax.rem(step, stripes) * stripe, stripe)
         turned[block, at] = dot(images_v[block, :], columns_v[:, at]).astype(BF16)
-        rank_chunk(lax.rem(step + ahead_of, slabs))
+        rank_chunk(step)
 
     load[5].wait()
     load[6].wait()
-    each(6, prepare)
+    each(5, prepare)
 
     slab_arrivals(0, incoming)
     arrived = jnp.concatenate([incoming[block].astype(F32) for block in range(slabs)], axis=0).astype(BF16)
@@ -313,7 +313,7 @@
     for index in range(5):
         gathers[index].start()
 
-    each(10, prepare, 6)
+    each(9, prepare, 5)
 
     def power_step(index):
         at = rows_at(index * share, share)
@@ -374,7 +374,7 @@
     def full_chunk(index):
         score_chunk(index, slices[...], [(0, 0, NPOSE)], False)
 
-    each(12, prepare, 10)
+    each(11, prepare, 9)
     power_step(LEFT)
     power_step(RIGHT)
     gathers[2].wait_recv()
@@ -433,7 +433,7 @@
     def _():
         share_out()
 
-    each(slabs, prepare, 12)
+    each(slabs, prepare, 11)
 
     @pl.when(turn != 0)
     def _():

time: 56.7 us -> 56.7 us (level)
  no operation moved by 1% of the time
where the time goes in v16:
time: 56.7 us; the launch traced here: 56.4 us
  Pallas kernels  55.7 us (98%)
  between operations  0.66 us (1%)
    pallas_call x1, Pallas kernels, per_device(): pl.pallas_call(functools.partial(kernel, slabs, members), out_shape=(pltp...  54.7 us

profile of v16, /device:TPU:1, one launch (start us, length us, event | category | flops | bytes accessed | tf_op | source)
XLA Modules:
  0.0 56.4 jit_solution(13755929530239533210)
XLA Ops:
  0.6 0.0 copy-start
  0.6 54.7 %shard_map.104 = (bf16[128,1024]{1,0:T(8,128)(2,1)S(1)}, bf16[16,16,128]{2,1,0:T(8,128)(2,1)S(1)}) custom-call(bf16[2048,1024]{1,0:T(8,128)(2,1)} %images.1, bf16[1024,1024]{1,0:T(8,128)(2,1)} %bitcast.5, bf16[1024,1024]{1,0:T(8,128)(2,1)} %constant.4.clone.columns, f32[1,2048]{1,0:T(1,128)} %bitcast.7, s32[16,2048]{1,0:T(8,128)} %bitcast.6, ...), custom_call_target="tpu_custom_call" | custom-call | tf_op jit(solution)/shard_map/pallas_call | solution.py:675
  55.3 0.0 copy-done
  55.4 1.0 %shard_map.105 = (f32[2,64,512]{2,1,0:T(8,128)}, f32[16,2048]{1,0:T(8,128)}) custom-call(bf16[1024,512]{1,0:T(8,128)(2,1)S(1)} %copy-done, bf16[128,1024]{1,0:T(8,128)(2,1)S(1)} %get-tuple-element.6.fourier, bf16[16,16,128]{2,1,0:T(8,128)(2,1)S(1)} %get-tuple-element.7.shares), custom_call_target="tpu_custom_call" | custom-call | tf_op jit(solution)/shard_map/pallas_call | solution.py:694
Async XLA Ops:
  0.6 54.7 %copy-start = (bf16[1024,512]{1,0:T(8,128)(2,1)S(1)}, bf16[1024,512]{1,0:T(8,128)(2,1)}, u32[]{:S(2)}) copy-start(bf16[1024,512]{1,0:T(8,128)(2,1)} %constant.5.clone.rows) | copy-start | bytes 3145732

commit v17 on v16

--- a/solution.py
+++ b/solution.py
@@ -107,6 +107,7 @@
     right = 2 * lax.rem(chip + 1, ring_len) + core
     left = 2 * lax.rem(chip + ring_len - 1, ring_len) + core
     partner = 2 * chip + 1 - core
+    across = 2 * lax.rem(chip + 2, ring_len) + core
 
     def slab_peer(step):
         return lax.rem(own + step, slabs)
@@ -303,14 +304,14 @@
         img_copy(2, block_of(HOME), block_of(other(HOME)), partner),
         img_copy(3, bottom(HOME), bottom(LEFT), right),
         img_copy(4, top(HOME), top(RIGHT), left),
-        img_copy(5, top(LEFT), top(FAR), right),
-        img_copy(6, bottom(RIGHT), bottom(FAR), left),
+        img_copy(5, top(HOME), top(FAR), across),
+        img_copy(6, bottom(HOME), bottom(FAR), across),
         img_copy(7, block_of(LEFT), block_of(other(LEFT)), partner),
         img_copy(8, block_of(RIGHT), block_of(other(RIGHT)), partner),
         img_copy(9, top(FAR), top(other(FAR)), partner),
         img_copy(10, bottom(FAR), bottom(other(FAR)), partner),
     ]
-    for index in range(5):
+    for index in range(7):
         gathers[index].start()
 
     each(9, prepare, 5)
@@ -323,9 +324,7 @@
 
     power_step(HOME)
     gathers[0].wait_recv()
-    gathers[5].start()
     gathers[1].wait_recv()
-    gathers[6].start()
     gathers[3].wait_recv()
     gathers[7].start()
     gathers[4].wait_recv()
@@ -499,7 +498,6 @@
     for step in range(1, members):
         mass_copy(step).start()
 
-    half_rows = NPOSE // 2
 
     def away_copy(index):
         return img_copy(40 + index, away.at[index], away_in.at[index], partner)
@@ -516,42 +514,31 @@
         rows = slice(first, first + size)
         return kept[index, rows, :] + away_in[index, rows, :].astype(F32)
 
-    low, high = slice(0, half_rows), slice(half_rows, NPOSE)
     ring_copies = [
-        img_copy(48, opposite.at[low], opposite_in.at[low], right),
-        img_copy(49, opposite.at[high], opposite_in.at[high], left),
-        img_copy(50, ring.at[0, high], ring_in.at[0, high], right),
-        img_copy(51, ring.at[1, low], ring_in.at[1, low], left),
-        img_copy(52, ring.at[0, low], ring_in.at[0, low], right),
-        img_copy(53, ring.at[1, high], ring_in.at[1, high], left),
+        img_copy(48, opposite, opposite_in, across),
+        img_copy(50, ring.at[0], ring_in.at[0], right),
+        img_copy(51, ring.at[1], ring_in.at[1], left),
     ]
     turn_stripe(FAR, lax.rem(chip + 2, ring_len))
     turn_stripe(RIGHT, lax.rem(chip + 1, ring_len))
     away_copy(FAR).wait_recv()
     opposite[...] = kept_part(FAR).astype(BF16)
     ring_copies[0].start()
-    ring_copies[1].start()
     turn_stripe(LEFT, lax.rem(chip + ring_len - 1, ring_len))
     away_copy(RIGHT).wait_recv()
-    ring[0, high] = kept_part(RIGHT, half_rows, half_rows).astype(BF16)
-    ring_copies[2].start()
+    ring[0] = kept_part(RIGHT).astype(BF16)
+    ring_copies[1].start()
     turn_stripe(HOME, chip)
     away_copy(LEFT).wait_recv()
-    ring[1, low] = kept_part(LEFT, 0, half_rows).astype(BF16)
-    ring_copies[3].start()
-    ring_copies[0].wait_recv()
-    ring[0, low] = (kept_part(RIGHT, 0, half_rows) + opposite_in[low, :].astype(F32)).astype(BF16)
-    ring_copies[4].start()
-    ring_copies[1].wait_recv()
-    ring[1, high] = (kept_part(LEFT, half_rows, half_rows) + opposite_in[high, :].astype(F32)).astype(BF16)
-    ring_copies[5].start()
+    ring[1] = kept_part(LEFT).astype(BF16)
+    ring_copies[2].start()
     shares_copy = pltpu.make_async_copy(shares, shares_out, loads.at[8])
     shares_copy.start()
     away_copy(HOME).wait_recv()
     held = kept_part(HOME)
-    for index in range(2, 6):
-        ring_copies[index].wait_recv()
-    summed = (held + ring_in[0].astype(F32) + ring_in[1].astype(F32)).astype(BF16)
+    for copy in ring_copies:
+        copy.wait_recv()
+    summed = (held + ring_in[0].astype(F32) + ring_in[1].astype(F32) + opposite_in[...].astype(F32)).astype(BF16)
 
     unpacked = dot(unpack[...], summed)
     for slab in range(slabs):

time: 56.7 us -> 58.3 us (1.028)
  Pallas kernels: 55.7 us -> 57.4 us
    pallas_call x1, Pallas kernels: 54.7 us -> 56.3 us  [per_device(): pl.pallas_call(functools.partial(kernel, slabs, members), out_shape=(pltp...]
where the time goes in v17:
time: 58.3 us; the launch traced here: 58 us
  Pallas kernels  57.4 us (98%)
  between operations  0.66 us (1%)
    pallas_call x1, Pallas kernels, per_device(): pl.pallas_call(functools.partial(kernel, slabs, members), out_shape=(pltp...  56.3 us

profile of v17, /device:TPU:1, one launch (start us, length us, event | category | flops | bytes accessed | tf_op | source)
XLA Modules:
  0.0 58.0 jit_solution(2952218825649387980)
XLA Ops:
  0.6 0.0 copy-start
  0.6 56.3 %shard_map.104 = (bf16[128,1024]{1,0:T(8,128)(2,1)S(1)}, bf16[16,16,128]{2,1,0:T(8,128)(2,1)S(1)}) custom-call(bf16[2048,1024]{1,0:T(8,128)(2,1)} %images.1, bf16[1024,1024]{1,0:T(8,128)(2,1)} %bitcast.5, bf16[1024,1024]{1,0:T(8,128)(2,1)} %constant.4.clone.columns, f32[1,2048]{1,0:T(1,128)} %bitcast.7, s32[16,2048]{1,0:T(8,128)} %bitcast.6, ...), custom_call_target="tpu_custom_call" | custom-call | tf_op jit(solution)/shard_map/pallas_call | solution.py:662
  57.0 0.0 copy-done
  57.0 1.0 %shard_map.105 = (f32[2,64,512]{2,1,0:T(8,128)}, f32[16,2048]{1,0:T(8,128)}) custom-call(bf16[1024,512]{1,0:T(8,128)(2,1)S(1)} %copy-done, bf16[128,1024]{1,0:T(8,128)(2,1)S(1)} %get-tuple-element.6.fourier, bf16[16,16,128]{2,1,0:T(8,128)(2,1)S(1)} %get-tuple-element.7.shares), custom_call_target="tpu_custom_call" | custom-call | tf_op jit(solution)/shard_map/pallas_call | solution.py:681
Async XLA Ops:
  0.6 56.4 %copy-start = (bf16[1024,512]{1,0:T(8,128)(2,1)S(1)}, bf16[1024,512]{1,0:T(8,128)(2,1)}, u32[]{:S(2)}) copy-start(bf16[1024,512]{1,0:T(8,128)(2,1)} %constant.5.clone.rows) | copy-start | bytes 3145732
